TPU v7x, 128 devices: a whole 4x4x4 slice. The times are simulated.
128 devices in a mesh: dp: 16 (over y_lo, z, core), cp: 8 (over x, y_hi).
Axes of the slice: x: 4, y: 4 (y_hi: 2, y_lo: 2; y = y_hi * 2 + y_lo), z: 4, core: 2. Of those that a mesh axis runs over, the one named last changes fastest.
Arguments:
- queries: bfloat16 [16384, 3072], P(('dp', 'cp')), may hold values from -48 to 48
- key_heads: bfloat16 [16384, 512], P(('dp', 'cp')), may hold values from -6 to 6
- value_heads: bfloat16 [16384, 512], P(('dp', 'cp')), may hold values from -6 to 6
- segment_ids: int32 [16, 1024], P('dp', 'cp'), may hold values from 0 to 1, never falling along the last dimension, each value on 1 to 768 neighbouring positions
- out_weight: bfloat16 [3072, 3072], P('dp', 'cp'), may hold values from -0.109375 to 0.109375
- grad_out: bfloat16 [16384, 3072], P('dp', 'cp'), may hold values from -6 to 6
Outputs:
- output: bfloat16 [16384, 3072], P('dp', 'cp')
- grad_queries: bfloat16 [16384, 3072], P(('dp', 'cp'))
- grad_keys: bfloat16 [16384, 512], P(('dp', 'cp'))
- grad_values: bfloat16 [16384, 512], P(('dp', 'cp'))
- grad_weight: float32 [3072, 3072], P('dp', 'cp')
Inputs may be any that keep to these rules, and one draw needn't show every extreme that they name: `segment_ids`: document numbers of a group never fall; a document holds at most 768 positions.
All inputs are finite; a program needn't handle non-finite values.
Results may differ from a plain program's by a relative error of at most 0.023.
Values may be sent and summed in bfloat16 or wider, within the bound.
No kernel may reach another device: no remote copies, remote signals or barrier semaphores. Data moves between devices by JAX's collectives and lax.ppermute only.
A program may use at most 128 MiB of HBM per device.

v0:
```python
import math

import jax
import jax.numpy as jnp
from jax import lax
from jax.sharding import PartitionSpec as P

HQ = 24
HK = 4
HD = 128


def masked_logits(query_tiles, query_pos, own_segment, key_block, segment_block):
    count_rows = key_block.shape[0]
    key_tiles = key_block.reshape(count_rows, HK, HD)
    logits = jnp.einsum(
        "qhrd,khd->hrqk", query_tiles, key_tiles, preferred_element_type=jnp.float32
    ) * (1.0 / math.sqrt(HD))
    key_pos = jnp.arange(count_rows, dtype=jnp.int32)
    allowed = (own_segment[:, None] == segment_block[None, :]) & (
        key_pos[None, :] <= query_pos[:, None]
    )
    return (jnp.where(allowed, logits, -1e30), allowed)


def per_device(queries, key_heads, value_heads, segment_ids, out_weight, grad_out):
    rows_own = queries.shape[0]
    head_share = HQ // HK
    kv_width = key_heads.shape[1]
    score_scale = 1.0 / math.sqrt(HD)
    weight_cols = lax.all_gather(out_weight, "dp", axis=0, tiled=True)
    grad_rows = grad_out
    grad_attended = lax.psum_scatter(
        lax.dot_general(
            grad_rows, weight_cols, (((1,), (1,)), ((), ())), preferred_element_type=jnp.float32
        ),
        "cp",
        scatter_dimension=0,
        tiled=True,
    ).astype(jnp.bfloat16)
    query_tiles = queries.reshape(rows_own, HK, head_share, HD)
    grad_tiles = grad_attended.reshape(rows_own, HK, head_share, HD)
    query_pos = lax.axis_index("cp") * rows_own + jnp.arange(rows_own, dtype=jnp.int32)
    own_segment = segment_ids[0].astype(jnp.bfloat16)

    def logits_of(blocks):
        return masked_logits(query_tiles, query_pos, own_segment, blocks[0], blocks[-1])

    def probability_of(softmax_stats, blocks):
        logits, allowed = logits_of(blocks)
        weights = jnp.where(allowed, jnp.exp(logits - softmax_stats[0][..., None]), 0.0)
        return weights / softmax_stats[1][..., None]

    row_peak = jnp.full((HK, head_share, rows_own), -1e30, jnp.float32)
    logits, allowed = logits_of(
        (
            lax.all_gather(key_heads, "cp", axis=0, tiled=True),
            lax.all_gather(own_segment, "cp", axis=0, tiled=True),
        )
    )
    new_peak = jnp.maximum(row_peak, jnp.max(logits, axis=-1))
    kept_terms = jnp.where(allowed, jnp.exp(logits - new_peak[..., None]), 0.0)
    softmax_stats = (new_peak, jnp.sum(kept_terms, axis=-1))
    blocks = (
        lax.all_gather(key_heads, "cp", axis=0, tiled=True),
        lax.all_gather(value_heads, "cp", axis=0, tiled=True),
        lax.all_gather(own_segment, "cp", axis=0, tiled=True),
    )
    count_rows = blocks[1].shape[0]
    value_tiles = blocks[1].reshape(count_rows, HK, HD)
    probability = probability_of(softmax_stats, blocks)
    rounded_prob = probability.astype(jnp.bfloat16)
    value_acc = jnp.einsum(
        "hrqk,khd->qhrd", rounded_prob, value_tiles, preferred_element_type=jnp.float32
    )
    grad_prob = jnp.einsum(
        "qhrd,khd->hrqk", grad_tiles, value_tiles, preferred_element_type=jnp.float32
    )
    value_acc, delta_sum = (value_acc, jnp.sum(probability * grad_prob, axis=-1))
    blocks = (
        lax.all_gather(key_heads, "cp", axis=0, tiled=True),
        lax.all_gather(value_heads, "cp", axis=0, tiled=True),
        lax.all_gather(own_segment, "cp", axis=0, tiled=True),
    )
    count_rows = blocks[0].shape[0]
    key_tiles = blocks[0].reshape(count_rows, HK, HD)
    value_tiles = blocks[1].reshape(count_rows, HK, HD)
    probability = probability_of(softmax_stats, blocks)
    rounded_prob = probability.astype(jnp.bfloat16)
    grad_prob = jnp.einsum(
        "qhrd,khd->hrqk", grad_tiles, value_tiles, preferred_element_type=jnp.float32
    )
    grad_logit = (probability * (grad_prob - delta_sum[..., None])).astype(jnp.bfloat16)
    grad_query_acc = jnp.einsum(
        "hrqk,khd->qhrd", grad_logit, key_tiles, preferred_element_type=jnp.float32
    )
    key_part = (
        jnp.einsum("hrqk,qhrd->khd", grad_logit, query_tiles, preferred_element_type=jnp.float32)
        * score_scale
    ).reshape(count_rows, kv_width)
    value_part = jnp.einsum(
        "hrqk,qhrd->khd", rounded_prob, grad_tiles, preferred_element_type=jnp.float32
    ).reshape(count_rows, kv_width)
    key_grad_all = key_part
    value_grad_all = value_part
    grad_query_acc, key_grad_all, value_grad_all = (grad_query_acc, key_grad_all, value_grad_all)
    attended = value_acc.astype(jnp.bfloat16).reshape(rows_own, -1)
    attended_block = lax.all_gather(attended, "cp", axis=0, tiled=True)
    out_all = jnp.dot(attended_block, weight_cols, preferred_element_type=jnp.float32)
    grad_rows = grad_out
    weight_partial = lax.dot_general(
        attended_block, grad_rows, (((0,), (0,)), ((), ())), preferred_element_type=jnp.float32
    )
    out_all, weight_partial = (out_all, weight_partial)
    grad_weight = lax.psum_scatter(
        weight_partial.astype(jnp.bfloat16), "dp", scatter_dimension=0, tiled=True
    ).astype(jnp.float32)
    key_sums, value_sums = (
        lax.psum_scatter(key_grad_all, "cp", scatter_dimension=0, tiled=True),
        lax.psum_scatter(value_grad_all, "cp", scatter_dimension=0, tiled=True),
    )
    grad_queries = (grad_query_acc * score_scale).astype(jnp.bfloat16).reshape(rows_own, -1)
    return (
        out_all.astype(jnp.bfloat16),
        grad_queries,
        key_sums.astype(jnp.bfloat16),
        value_sums.astype(jnp.bfloat16),
        grad_weight,
    )


def solution(mesh):
    in_specs = (
        P(("dp", "cp"), None),
        P(("dp", "cp"), None),
        P(("dp", "cp"), None),
        P("dp", "cp"),
        P("dp", "cp"),
        P("dp", "cp"),
    )
    out_specs = (
        P("dp", "cp"),
        P(("dp", "cp"), None),
        P(("dp", "cp"), None),
        P(("dp", "cp"), None),
        P("dp", "cp"),
    )
    return jax.shard_map(
        per_device, mesh=mesh, in_specs=in_specs, out_specs=out_specs, check_vma=False
    )
```

profile of v0, /device:TPU:22, one launch (start us, length us, event | category | flops | bytes accessed | tf_op | source)
XLA Modules:
  0.0 626.5 jit_solution(6003438745203183686)
XLA Ops:
  8.0 1.7 copy.26
  11.1 1.5 copy.27
  12.6 17.8 %all-gather = bf16[1,1024]{1,0:T(2,128)(2,1)S(1)} all-gather(bf16[1,128]{1,0:T(2,128)(2,1)S(1)} %get-tuple-element.15), channel_id=2, replica_groups=mesh['dp'=16,'cp'=8] {'cp'}, dimensions={1}, use_global_device_ids=true | all-gather | bytes 2304 | tf_op jit(solution)/shard_map/all_gather | solution.py:67
  30.6 26.5 %all-gather.8.cloned.1.call-done = bf16[1024,512]{1,0:T(8,128)(2,1)} async-done(((bf16[128,512]{1,0:T(8,128)(2,1)}), bf16[1024,512]{1,0:T(8,128)(2,1)}) %all-gather.8.cloned.1.call-update) | async-done | bytes 1048592 | tf_op jit(solution)/shard_map/all_gather | solution.py:66
  57.1 1.5 copy.30
  58.6 48.3 %all-gather.6.cloned.1.call-done = bf16[1024,512]{0,1:T(8,128)(2,1)} async-done(((bf16[128,512]{0,1:T(8,128)(2,1)}), bf16[1024,512]{0,1:T(8,128)(2,1)}) %all-gather.6.cloned.1.call-update) | async-done | bytes 1048592 | tf_op jit(solution)/shard_map/all_gather | solution.py:65
  106.9 3.3 fusion.3
  110.1 3.1 fusion.5
  113.2 4.9 fusion.10
  118.2 26.3 %all-gather.12.cloned.1.call-done = bf16[3072,384]{1,0:T(8,128)(2,1)} async-done(((bf16[192,384]{1,0:T(8,128)(2,1)}), bf16[3072,384]{1,0:T(8,128)(2,1)}) %all-gather.12.cloned.1.call-update) | async-done | bytes 2359312 | tf_op jit(solution)/shard_map/all_gather | solution.py:31
  144.5 8.0 %fusion.17 = f32[1024,3072]{1,0:T(8,128)} fusion(bf16[1024,384]{1,0:T(8,128)(2,1)S(1)} %copy-done, bf16[3072,384]{1,0:T(8,128)(2,1)} %all-gather.12.cloned.1.call-done), kind=kOutput, calls=%fused_computation.25 | convolution fusion | flops 2415919104 | bytes 15728640 | tf_op jit(solution)/shard_map/dot_general | solution.py:34
  152.5 91.4 %all-gather.10.cloned.1.call-done = bf16[1024,3072]{0,1:T(8,128)(2,1)} async-done(((bf16[128,3072]{0,1:T(8,128)(2,1)}), bf16[1024,3072]{0,1:T(8,128)(2,1)}) %all-gather.10.cloned.1.call-update) | async-done | bytes 6291472 | tf_op jit(solution)/shard_map/all_gather | solution.py:108
  243.9 7.6 %convolution_convert_fusion = bf16[3072,384]{1,0:T(8,128)(2,1)} fusion(bf16[1024,3072]{0,1:T(8,128)(2,1)} %all-gather.10.cloned.1.call-done, bf16[1024,384]{1,0:T(8,128)(2,1)S(1)} %copy-done), kind=kOutput, calls=%fused_computation.10 | convolution fusion | flops 2417098752 | bytes 9437184 | tf_op jit(solution)/shard_map/dot_general | solution.py:111
  251.8 144.7 %reduce-scatter.5.cloned.1.call-done = f32[128,3072]{1,0:T(8,128)} async-done(((f32[1024,3072]{1,0:T(8,128)}), f32[128,3072]{1,0:T(8,128)}) %reduce-scatter.5.cloned.1.call-update) | async-done | bytes 1572880 | tf_op jit(solution)/shard_map/reduce_scatter | solution.py:33
  396.5 1.5 convert_element_type.53
  398.0 1.2 copy.32
  399.1 7.1 %fusion.6 = f32[4,128,1024,1]{2,1,3,0:T(8,128)S(1)} fusion(bf16[128,4,6,128]{0,3,2,1:T(8,128)(2,1)} %bitcast.93, f32[4,1024,128,6]{2,1,3,0:T(8,128)} %copy-done.2, f32[4,6,128]{2,1,0:T(8,128)S(1)} %fusion.5, f32[4,6,128]{2,1,0:T(8,128)S(1)} %broadcast_maximum_fusion, pred[128,1024]{0,1:T(8,128)(4,1)S(1)} %fusion.13), kind=kOutput, calls=%fused_computation.11 | convolution fusion | flops 824180736 | bytes 15622144 | tf_op jit(solution)/shard_map/hrqk,qhrd->khd/dot_general | solution.py:101
  406.2 1.8 copy.40
  408.1 8.1 %fusion = (f32[4,6,128]{2,1,0:T(8,128)S(1)}, f32[4,128,6,1024]{1,3,2,0:T(8,128)S(1)}) fusion(f32[4,6,128]{2,1,0:T(8,128)S(1)} %fusion.5, f32[4,6,128]{2,1,0:T(8,128)S(1)} %broadcast_maximum_fusion, f32[4,1024,128,6]{2,1,3,0:T(8,128)} %copy-done.2, pred[128,1024]{0,1:T(8,128)(4,1)S(1)} %fusion.13, bf16[128,4,6,128]{0,3,2,1:T(8,128)(2,1)S(1)} %bitcast.94, ...), kind=kOutput, calls=%fused_computation.2 | convolution fusion | flops 827323392 | bytes 27168768 | tf_op jit(solution)/shard_map/qhrd,khd->hrqk/dot_general | solution.py:90
  416.2 7.3 %fusion.2 = bf16[4,6,128,1024]{2,3,1,0:T(8,128)(2,1)S(1)} fusion(f32[4,128,6,1024]{1,3,2,0:T(8,128)S(1)} %get-tuple-element.20, f32[4,6,128]{2,1,0:T(8,128)S(1)} %get-tuple-element.19, f32[4,6,128]{2,1,0:T(8,128)S(1)} %fusion.5, f32[4,6,128]{2,1,0:T(8,128)S(1)} %broadcast_maximum_fusion, f32[4,1024,128,6]{2,1,3,0:T(8,128)} %copy-done.2, ...), kind=kLoop, calls=%fused_computation.4 | loop fusion | flops 25165824 | bytes 31625216 | tf_op jit(solution)/shard_map/convert_element_type | solution.py:93
  423.5 2.6 copy-done.3
  426.2 2.2 bitcast_multiply_fusion.1
  428.4 1.9 copy.38
  430.2 7.9 %convolution_convert_fusion.1 = bf16[1024,384]{1,0:T(8,128)(2,1)} fusion(bf16[1024,3072]{0,1:T(8,128)(2,1)} %all-gather.10.cloned.1.call-done, bf16[3072,384]{1,0:T(8,128)(2,1)} %all-gather.12.cloned.1.call-done), kind=kOutput, calls=%fused_computation.18 | convolution fusion | flops 2416312320 | bytes 9437184 | tf_op jit(solution)/shard_map/dot_general | solution.py:109
  438.2 26.5 %reduce-scatter.11.cloned.1.call-done = bf16[192,384]{1,0:T(8,128)(2,1)} async-done(((bf16[3072,384]{1,0:T(8,128)(2,1)}), bf16[192,384]{1,0:T(8,128)(2,1)}) %reduce-scatter.11.cloned.1.call-update) | async-done | bytes 147472 | tf_op jit(solution)/shard_map/reduce_scatter | solution.py:115
  464.7 1.6 convert_element_type.60
  466.3 3.8 multiply_convert_fusion
  470.1 1.2 copy.41
  471.3 68.8 %reduce-scatter.9.cloned.1.call-done = f32[128,512]{1,0:T(8,128)} async-done(((f32[1024,512]{1,0:T(8,128)}), f32[128,512]{1,0:T(8,128)}) %reduce-scatter.9.cloned.1.call-update) | async-done | bytes 262160 | tf_op jit(solution)/shard_map/reduce_scatter | solution.py:120
  540.0 1.6 convert_element_type.58
  541.7 76.3 %reduce-scatter.7.cloned.1.call-done = f32[128,512]{1,0:T(8,128)} async-done(((f32[1024,512]{1,0:T(8,128)}), f32[128,512]{1,0:T(8,128)}) %reduce-scatter.7.cloned.1.call-update) | async-done | bytes 262160 | tf_op jit(solution)/shard_map/reduce_scatter | solution.py:119
  618.0 1.6 convert_element_type.57
  (38 shorter events, 2.9 us)
Async XLA Ops:
  7.2 137.3 %copy-start = (bf16[1024,384]{1,0:T(8,128)(2,1)S(1)}, bf16[1024,384]{1,0:T(8,128)(2,1)}, u32[]{:S(2)}) copy-start(bf16[1024,384]{1,0:T(8,128)(2,1)} %param.11) | copy-start | bytes 2359300
  7.2 49.9 %all-gather.8.cloned.1.call-start = ((), (), s32[]{:S(2)}) async-start(), calls=%async_computation.5 | async-start | bytes 1179648 | tf_op jit(solution)/shard_map/all_gather | solution.py:66
  7.9 98.9 %all-gather.6.cloned.1.call-start = ((), (), s32[]{:S(2)}) async-start(), calls=%async_computation.4 | async-start | bytes 1179648 | tf_op jit(solution)/shard_map/all_gather | solution.py:65
  9.7 134.8 %all-gather.12.cloned.1.call-start = ((), (), s32[]{:S(2)}) async-start(), calls=%async_computation.7 | async-start | bytes 2506752 | tf_op jit(solution)/shard_map/all_gather | solution.py:31
  10.4 233.5 %all-gather.10.cloned.1.call-start = ((), (), s32[]{:S(2)}) async-start(), calls=%async_computation.6 | async-start | bytes 7077888 | tf_op jit(solution)/shard_map/all_gather | solution.py:108
  12.6 100.6 %copy-start.4 = (bf16[128,3072]{0,1:T(8,128)(2,1)}, bf16[128,3072]{0,1:T(8,128)(2,1)S(1)}, u32[]{:S(2)}) copy-start(bf16[128,3072]{0,1:T(8,128)(2,1)S(1)} %copy.27) | copy-start | bytes 2359300
  58.6 54.6 %copy-start.7 = (bf16[1024,512]{0,1:T(8,128)(2,1)}, bf16[1024,512]{0,1:T(8,128)(2,1)S(1)}, u32[]{:S(2)}) copy-start(bf16[1024,512]{0,1:T(8,128)(2,1)S(1)} %copy.30) | copy-start | bytes 3145732
  110.1 8.0 %copy-start.2 = (f32[4,1024,128,6]{2,1,3,0:T(8,128)}, f32[4,1024,128,6]{2,1,3,0:T(8,128)S(1)}, u32[]{:S(2)}) copy-start(f32[4,1024,128,6]{2,1,3,0:T(8,128)S(1)} %get-tuple-element.18) | copy-start | bytes 37748740
  118.2 278.3 %reduce-scatter.5.cloned.1.call-start = ((), (), s32[]{:S(2)}) async-start(), calls=%async_computation.8 | async-start | bytes 14155776 | tf_op jit(solution)/shard_map/reduce_scatter | solution.py:33
  152.5 312.2 %reduce-scatter.11.cloned.1.call-start = ((), (), s32[]{:S(2)}) async-start(), calls=%async_computation.11 | async-start | bytes 2506752 | tf_op jit(solution)/shard_map/reduce_scatter | solution.py:115
  251.6 288.5 %reduce-scatter.9.cloned.1.call-start = ((), (), s32[]{:S(2)}) async-start(), calls=%async_computation.10 | async-start | bytes 2359296 | tf_op jit(solution)/shard_map/reduce_scatter | solution.py:120
  399.1 9.0 %copy-start.8 = (bf16[128,3072]{0,1:T(8,128)(2,1)S(1)}, bf16[128,3072]{0,1:T(8,128)(2,1)}, u32[]{:S(2)}) copy-start(bf16[128,3072]{0,1:T(8,128)(2,1)} %copy.32) | copy-start | bytes 2359300
  408.0 210.0 %reduce-scatter.7.cloned.1.call-start = ((), (), s32[]{:S(2)}) async-start(), calls=%async_computation.9 | async-start | bytes 2359296 | tf_op jit(solution)/shard_map/reduce_scatter | solution.py:119
  416.2 10.0 %copy-start.5 = (bf16[128,3072]{0,1:T(8,128)(2,1)S(1)}, bf16[128,3072]{0,1:T(8,128)(2,1)}, u32[]{:S(2)}) copy-start(bf16[128,3072]{0,1:T(8,128)(2,1)} %copy-done.4) | copy-start | bytes 2359300
  423.5 2.7 copy-start.3
  428.4 191.3 %copy-start.1 = (bf16[1024,384]{1,0:T(8,128)(2,1)S(1)}, bf16[1024,384]{1,0:T(8,128)(2,1)}, u32[]{:S(2)}) copy-start(bf16[1024,384]{1,0:T(8,128)(2,1)} %param.11) | copy-start | bytes 2359300
  430.2 36.1 %copy-start.6 = (bf16[1024,512]{0,1:T(8,128)(2,1)S(1)}, bf16[1024,512]{0,1:T(8,128)(2,1)}, u32[]{:S(2)}) copy-start(bf16[1024,512]{0,1:T(8,128)(2,1)} %all-gather.6.cloned.1.call-done) | copy-start | bytes 3145732
Sparse Core Ops, SparseCore 0:
  10.4 46.6 all-gather.7
  59.9 46.9 all-gather.5
  108.6 35.8 all-gather.11
  147.1 96.7 all-gather.9
  247.7 148.7 reduce-scatter.4
  398.8 65.7 reduce-scatter.10
  468.9 71.1 reduce-scatter.8
  543.8 74.1 reduce-scatter.6
where the time goes:
time: 630 us; the launch traced here: 626 us
  waiting for transfers between devices  510 us (81%)
  matrix products  52.8 us (8%)
  blocking collectives  17.8 us (3%)
  other arithmetic  17.7 us (3%)
  between operations  14.3 us (2%)
  local copies, waits for them, and re-layouts  13.3 us (2%)
    reduce_scatter x1, waiting for transfers between devices, per_device(): lax.psum_scatter(lax.dot_general(grad_rows, weight_cols, (((1,), (1,)), (...  145 us
    all_gather x1, waiting for transfers between devices, per_device(): attended_block = lax.all_gather(attended, 'cp', axis=0, tiled=True)  91.4 us
    reduce_scatter x1, waiting for transfers between devices, per_device(): lax.psum_scatter(key_grad_all, 'cp', scatter_dimension=0, tiled=True)  76.3 us
    reduce_scatter x1, waiting for transfers between devices, per_device(): lax.psum_scatter(value_grad_all, 'cp', scatter_dimension=0, tiled=True)  68.8 us
    all_gather x1, waiting for transfers between devices, per_device(): lax.all_gather(key_heads, 'cp', axis=0, tiled=True)  48.3 us
    reduce_scatter x1, waiting for transfers between devices, per_device(): lax.psum_scatter(weight_partial.astype(jnp.bfloat16), 'dp', scatter_dimen...  26.5 us
    all_gather x1, waiting for transfers between devices, per_device(): lax.all_gather(value_heads, 'cp', axis=0, tiled=True)  26.5 us
    all_gather x1, waiting for transfers between devices, per_device(): weight_cols = lax.all_gather(out_weight, 'dp', axis=0, tiled=True)  26.3 us
  transfers between devices with their start and end apart: 8, of which 8 were waited for; matrix products, arithmetic and copies ran while one was open for 13% of the time, Pallas kernels for 0%

commit v1 on v0

v1 whole, which is shorter than its diff:
```python
import math

import jax
import jax.numpy as jnp
from jax import lax
from jax.experimental import pallas as pl
from jax.experimental.pallas import tpu as pltpu
from jax.sharding import PartitionSpec as P


NX = 4
GROUP = 1024
HD = 128
HEADS = 3
FEAT = 384
ROWS = 128
QB = 256
SEG_ROWS = 16
PACK = 5 * ROWS + SEG_ROWS
SHIFTS = [(dx, dh) for dx in range(NX) for dh in range(2)]
SCALE = 1.0 / math.sqrt(HD)
EXP2_SCALE = SCALE * math.log2(math.e)
F32 = jnp.float32
BF16 = jnp.bfloat16
VMEM_LIMIT = 48 * 1024 * 1024


def cp_pairs(dx, dh):
    return [(x * 2 + h, ((x + dx) % NX) * 2 + (h ^ dh)) for x in range(NX) for h in range(2)]


def z_pairs(dz):
    return [
        (y * 8 + z * 2 + c, y * 8 + ((z + dz) % 4) * 2 + c)
        for y in range(2)
        for z in range(4)
        for c in range(2)
    ]


def core_pairs():
    return [(d, d ^ 1) for d in range(16)]


def y_pairs(moves):
    pairs = []
    for src, dst in moves:
        for r in range(8):
            for x in range(NX):
                pairs.append(
                    (
                        ((src % 2) * 8 + r) * 8 + x * 2 + src // 2,
                        ((dst % 2) * 8 + r) * 8 + x * 2 + dst // 2,
                    )
                )
    return pairs


Y_SWAP = y_pairs([(1, 2), (2, 1)])
Y_CYCLE_IN = y_pairs([(0, 1), (2, 0), (3, 2), (1, 3)])
Y_CYCLE_OUT = y_pairs([(1, 0), (0, 2), (2, 3), (3, 1)])


def dot_nt(a, b):
    return lax.dot_general(a, b, (((1,), (1,)), ((), ())), preferred_element_type=F32)


def dot_nn(a, b):
    return lax.dot_general(a, b, (((1,), (0,)), ((), ())), preferred_element_type=F32)


def dot_tn(a, b):
    return lax.dot_general(a, b, (((0,), (0,)), ((), ())), preferred_element_type=F32)


def call(kernel, name, meta, operands, outs, scratch=(), flops=0, transcendentals=0):
    moved = sum(math.prod(o.shape) * o.dtype.itemsize for o in list(operands) + list(outs))
    return pl.pallas_call(
        kernel,
        name=name,
        out_shape=tuple(outs),
        in_specs=[pl.BlockSpec(memory_space=pltpu.SMEM)]
        + [pl.BlockSpec(memory_space=pltpu.VMEM)] * len(operands),
        out_specs=tuple(pl.BlockSpec(memory_space=pltpu.VMEM) for _ in outs),
        scratch_shapes=list(scratch),
        compiler_params=pltpu.CompilerParams(vmem_limit_bytes=VMEM_LIMIT),
        cost_estimate=pl.CostEstimate(
            flops=flops, bytes_accessed=moved, transcendentals=transcendentals
        ),
    )(meta, *operands)


def shaped(shape, dtype):
    return jax.ShapeDtypeStruct(shape, dtype)


def pack_kernel(meta, q_ref, k_ref, v_ref, seg_ref, *out_refs):
    x, h = meta[0], meta[1]
    seg = jnp.broadcast_to(seg_ref[...].astype(F32), (SEG_ROWS, ROWS)).astype(BF16)
    for (dx, dh), out in zip(SHIFTS, out_refs):
        to_x = lax.rem(x + dx, NX)
        to_h = h if dh == 0 else 1 - h
        q_off = pl.multiple_of(to_h * (NX * FEAT) + to_x * FEAT, 128)
        kv_off = pl.multiple_of((to_h * 2 + to_x // 2) * HD, 128)
        for head in range(HEADS):
            out[pl.ds(head * ROWS, ROWS), :] = q_ref[:, pl.ds(pl.multiple_of(q_off + head * HD, 128), HD)]
        out[pl.ds(3 * ROWS, ROWS), :] = k_ref[:, pl.ds(kv_off, HD)]
        out[pl.ds(4 * ROWS, ROWS), :] = v_ref[:, pl.ds(kv_off, HD)]
        out[pl.ds(5 * ROWS, SEG_ROWS), :] = seg


def transposed_scores(k, q, first, qb):
    scores = dot_nt(k, q)
    key_pos = lax.broadcasted_iota(jnp.int32, scores.shape, 0)
    query_pos = lax.broadcasted_iota(jnp.int32, scores.shape, 1) + qb * QB
    return jnp.where((key_pos <= query_pos) & (key_pos >= first), scores * EXP2_SCALE, -1e30)


def forward_kernel(meta, *refs):
    blocks, (att_ref, q_ref, kv_ref, stat_ref, vt_ref) = refs[:8], refs[8:]
    x, h = meta[0], meta[1]
    seg_sum = jnp.zeros((1, ROWS), F32)
    for (dx, dh), block in zip(SHIFTS, blocks):
        from_x = lax.rem(x - dx + NX, NX)
        from_h = h if dh == 0 else 1 - h
        row = pl.multiple_of((from_x * 2 + from_h) * ROWS, ROWS)
        for head in range(HEADS):
            q_ref[head, pl.ds(row, ROWS), :] = block[pl.ds(head * ROWS, ROWS), :]
        kv_ref[0, pl.ds(row, ROWS), :] = block[pl.ds(3 * ROWS, ROWS), :]
        kv_ref[1, pl.ds(row, ROWS), :] = block[pl.ds(4 * ROWS, ROWS), :]
        seg_sum = seg_sum + block[pl.ds(5 * ROWS, SEG_ROWS), :].astype(F32)[0:1]
    second = jnp.sum(seg_sum, axis=1, keepdims=True)
    boundary = (GROUP - second).astype(jnp.int32)
    position = lax.broadcasted_iota(jnp.int32, (1, GROUP), 1)
    first = jnp.where(position >= boundary, boundary, 0)
    stat_ref[...] = jnp.zeros_like(stat_ref)
    stat_ref[3:4, :] = first.astype(F32)
    vt_ref[...] = kv_ref[1].astype(F32).T.astype(BF16)
    for qb in range(GROUP // QB):
        keys = (qb + 1) * QB
        rows = pl.ds(qb * QB, QB)
        for head in range(HEADS):
            scores = transposed_scores(
                kv_ref[0, pl.ds(0, keys), :], q_ref[head, rows, :], first[:, qb * QB : keys], qb
            )
            peak = jnp.max(scores, axis=0, keepdims=True)
            weights = jnp.exp2(scores - peak)
            total = jnp.sum(weights, axis=0, keepdims=True)
            stat_ref[head : head + 1, rows] = peak + jnp.log2(total)
            mixed = dot_nn(vt_ref[:, pl.ds(0, keys)], weights.astype(BF16)) / total
            att_ref[rows, pl.ds(head * HD, HD)] = mixed.T.astype(BF16)


def backward_kernel(meta, q_ref, kv_ref, stat_ref, own_ref, *refs):
    received, outs, (kt_ref, g_ref, gq_ref, gk_ref, gv_ref) = refs[:3], refs[3:11], refs[11:]
    x, h = meta[0], meta[1]
    total = own_ref[...]
    for part in received:
        total = total + part[...].astype(F32)
    for head in range(HEADS):
        g_ref[head] = total[:, head * HD : (head + 1) * HD].astype(BF16)
    kt_ref[...] = kv_ref[0].astype(F32).T.astype(BF16)
    gk_ref[...] = jnp.zeros_like(gk_ref)
    gv_ref[...] = jnp.zeros_like(gv_ref)
    first = stat_ref[3:4, :].astype(jnp.int32)
    for qb in range(GROUP // QB):
        keys = (qb + 1) * QB
        rows = pl.ds(qb * QB, QB)
        span = pl.ds(0, keys)
        for head in range(HEADS):
            q = q_ref[head, rows, :]
            g = g_ref[head, rows, :]
            scores = transposed_scores(kv_ref[0, span, :], q, first[:, qb * QB : keys], qb)
            prob = jnp.exp2(scores - stat_ref[head : head + 1, rows])
            grad_prob = dot_nt(kv_ref[1, span, :], g)
            delta = jnp.sum(prob * grad_prob, axis=0, keepdims=True)
            grad_logit = (prob * (grad_prob - delta)).astype(BF16)
            gv_ref[span, :] += dot_nn(prob.astype(BF16), g)
            gk_ref[span, :] += dot_nn(grad_logit, q)
            gq = dot_nn(kt_ref[:, span], grad_logit) * SCALE
            gq_ref[head, rows, :] = gq.T.astype(BF16)
    for (dx, dh), out in zip(SHIFTS, outs):
        to_x = lax.rem(x + dx, NX)
        to_h = h if dh == 0 else 1 - h
        row = pl.multiple_of((to_x * 2 + to_h) * ROWS, ROWS)
        for head in range(HEADS):
            out[pl.ds(head * ROWS, ROWS), :] = gq_ref[head, pl.ds(row, ROWS), :]
        out[pl.ds(3 * ROWS, ROWS), :] = (gk_ref[pl.ds(row, ROWS), :] * SCALE).astype(BF16)
        out[pl.ds(4 * ROWS, ROWS), :] = gv_ref[pl.ds(row, ROWS), :].astype(BF16)


def unpack_kernel(meta, *refs):
    blocks, (gq_ref, gk_ref, gv_ref, held) = refs[:8], refs[8:]
    x, h = meta[0], meta[1]
    for (dx, dh), block in zip(SHIFTS, blocks):
        from_x = lax.rem(x - dx + NX, NX)
        from_h = h if dh == 0 else 1 - h
        source = from_h * NX + from_x
        for head in range(HEADS):
            col = pl.multiple_of(source * FEAT + head * HD, 128)
            gq_ref[:, pl.ds(col, HD)] = block[pl.ds(head * ROWS, ROWS), :]
        held[source] = block[pl.ds(3 * ROWS, 2 * ROWS), :].astype(F32)
    for head in range(4):
        both = held[2 * head] + held[2 * head + 1]
        gk_ref[:, pl.ds(head * HD, HD)] = both[:ROWS].astype(BF16)
        gv_ref[:, pl.ds(head * HD, HD)] = both[ROWS:].astype(BF16)


def weight_kernel(meta, *refs):
    mine, others, out = refs[:4], refs[4:8], refs[8]
    z, core = meta[2], meta[3]
    for dz in range(4):
        slot = lax.rem(z - dz + 4, 4)
        out[slot, pl.ds(pl.multiple_of(core * 192, 64), 192), :] = mine[dz][...]
        out[slot, pl.ds(pl.multiple_of((1 - core) * 192, 64), 192), :] = others[dz][...]


def grad_send_kernel(meta, here_ref, there_ref, w_ref, *outs):
    x = meta[0]
    for shift, out in zip((2, 1, 3), outs):
        slot = lax.rem(x + shift, NX)

        @pl.loop(0, GROUP // QB)
        def _(i):
            rows = pl.ds(pl.multiple_of(i * QB, QB), QB)
            out[rows, :] = (
                dot_nt(here_ref[rows, :], w_ref[slot, :, pl.ds(0, FEAT)])
                + dot_nt(there_ref[rows, :], w_ref[slot, :, pl.ds(FEAT, FEAT)])
            ).astype(BF16)


def grad_own_kernel(meta, here_ref, there_ref, w_ref, out):
    x = meta[0]

    @pl.loop(0, GROUP // QB)
    def _(i):
        rows = pl.ds(pl.multiple_of(i * QB, QB), QB)
        out[rows, :] = dot_nt(here_ref[rows, :], w_ref[x, :, pl.ds(0, FEAT)]) + dot_nt(
            there_ref[rows, :], w_ref[x, :, pl.ds(FEAT, FEAT)]
        )


def out_kernel(half, meta, *refs):
    att, w_ref, out = refs[:4], refs[4], refs[5]
    x = meta[0]

    @pl.loop(0, GROUP // QB)
    def _(i):
        rows = pl.ds(pl.multiple_of(i * QB, QB), QB)
        total = jnp.zeros((QB, FEAT), F32)
        for shift in range(NX):
            slot = lax.rem(x - shift + NX, NX)
            total = total + dot_nn(att[shift][rows, :], w_ref[slot, :, pl.ds(half * FEAT, FEAT)])
        out[rows, :] = total.astype(out.dtype)


def grad_weight_kernel(meta, *refs):
    att, here_ref, there_ref, keep_ref, send_ref, held = refs[:4], *refs[4:]
    x, core = meta[0], meta[3]
    for shift in range(NX):
        slot = lax.rem(x - shift + NX, NX)
        turned = att[shift][...].T
        held[:, pl.ds(0, FEAT)] = dot_nn(turned, here_ref[...])
        held[:, pl.ds(FEAT, FEAT)] = dot_nn(turned, there_ref[...])
        keep_ref[slot] = held[pl.ds(pl.multiple_of(core * 192, 64), 192), :]
        send_ref[slot] = held[pl.ds(pl.multiple_of((1 - core) * 192, 64), 192), :].astype(BF16)


def per_device(queries, key_heads, value_heads, segment_ids, out_weight, grad_out):
    dp = lax.axis_index("dp")
    cp = lax.axis_index("cp")
    x, h = cp // 2, cp % 2
    z, core = (dp // 2) % 4, dp % 2
    corner = (dp // 8) == h
    meta = jnp.stack([x, h, z, core]).astype(jnp.int32)
    both = ("dp", "cp")

    packed = call(
        pack_kernel,
        "pack",
        meta,
        (queries, key_heads, value_heads, segment_ids),
        [shaped((PACK, ROWS), BF16)] * 8,
    )
    blocks = [packed[0]] + [
        lax.ppermute(b, "cp", cp_pairs(*s)) for s, b in zip(SHIFTS[1:], packed[1:])
    ]
    grad_there = lax.ppermute(grad_out, "cp", cp_pairs(0, 1))

    swapped = lax.ppermute(out_weight, both, Y_SWAP)
    cycled = lax.ppermute(out_weight, both, Y_CYCLE_IN)
    w_here = jnp.where(corner, out_weight, cycled)
    w_there = jnp.where(corner, cycled, swapped)
    w_mine = jnp.concatenate([w_here, w_there], axis=1)
    mine = [w_mine] + [lax.ppermute(w_mine, "dp", z_pairs(dz)) for dz in (1, 2, 3)]
    others = [lax.ppermute(w, "dp", core_pairs()) for w in mine]
    (weight,) = call(
        weight_kernel, "weight", meta, (*mine, *others), [shaped((NX, FEAT, 2 * FEAT), BF16)]
    )

    attended, q_all, kv_all, stats = call(
        forward_kernel,
        "forward",
        meta,
        blocks,
        [
            shaped((GROUP, FEAT), BF16),
            shaped((HEADS, GROUP, HD), BF16),
            shaped((2, GROUP, HD), BF16),
            shaped((8, GROUP), F32),
        ],
        [pltpu.VMEM((HD, GROUP), BF16)],
        flops=2 * 2 * HEADS * GROUP * GROUP * HD,
        transcendentals=HEADS * GROUP * GROUP,
    )
    att = [attended] + [lax.ppermute(attended, "cp", cp_pairs(dx, 0)) for dx in (1, 2, 3)]

    block_flops = 2 * GROUP * FEAT * 2 * FEAT
    sends = call(
        grad_send_kernel,
        "grad_send",
        meta,
        (grad_out, grad_there, weight),
        [shaped((GROUP, FEAT), BF16)] * 3,
        flops=3 * block_flops,
    )
    parts = [lax.ppermute(p, "cp", cp_pairs(dx, 0)) for dx, p in zip((2, 1, 3), sends)]
    (own,) = call(
        grad_own_kernel,
        "grad_own",
        meta,
        (grad_out, grad_there, weight),
        [shaped((GROUP, FEAT), F32)],
        flops=block_flops,
    )

    (out_there,) = call(
        lambda *refs: out_kernel(1, *refs),
        "out_there",
        meta,
        (*att, weight),
        [shaped((GROUP, FEAT), BF16)],
        flops=2 * block_flops,
    )
    out_part = lax.ppermute(out_there, "cp", cp_pairs(0, 1))
    keep, send = call(
        grad_weight_kernel,
        "grad_weight",
        meta,
        (*att, grad_out, grad_there),
        [shaped((4, 192, 2 * FEAT), F32), shaped((4, 192, 2 * FEAT), BF16)],
        [pltpu.VMEM((FEAT, 2 * FEAT), F32)],
        flops=4 * block_flops,
    )
    core_part = lax.ppermute(send, "dp", core_pairs())
    (out_here,) = call(
        lambda *refs: out_kernel(0, *refs),
        "out_here",
        meta,
        (*att, weight),
        [shaped((GROUP, FEAT), F32)],
        flops=2 * block_flops,
    )

    def z_sum(dz):
        slot = (z + dz) % 4
        return lax.dynamic_index_in_dim(keep, slot, 0, False) + lax.dynamic_index_in_dim(
            core_part, slot, 0, False
        ).astype(F32)

    z_parts = [lax.ppermute(z_sum(dz).astype(BF16), "dp", z_pairs(dz)) for dz in (1, 2, 3)]
    z_total = z_sum(0) + sum(p.astype(F32) for p in z_parts)
    part_here, part_there = z_total[:, :FEAT], z_total[:, FEAT:]
    swap_part = lax.ppermute(part_there.astype(BF16), both, Y_SWAP)
    cycle_part = lax.ppermute(
        jnp.where(corner, part_there, part_here).astype(BF16), both, Y_CYCLE_OUT
    )
    grad_weight = jnp.where(corner, part_here, swap_part.astype(F32)) + cycle_part.astype(F32)

    output = (out_here + out_part.astype(F32)).astype(BF16)

    grads = call(
        backward_kernel,
        "backward",
        meta,
        (q_all, kv_all, stats, own, *parts),
        [shaped((5 * ROWS, ROWS), BF16)] * 8,
        [
            pltpu.VMEM((HD, GROUP), BF16),
            pltpu.VMEM((HEADS, GROUP, HD), BF16),
            pltpu.VMEM((HEADS, GROUP, HD), BF16),
            pltpu.VMEM((GROUP, HD), F32),
            pltpu.VMEM((GROUP, HD), F32),
        ],
        flops=5 * 2 * HEADS * GROUP * GROUP * HD,
        transcendentals=HEADS * GROUP * GROUP,
    )
    returned = [grads[0]] + [
        lax.ppermute(b, "cp", cp_pairs(*s)) for s, b in zip(SHIFTS[1:], grads[1:])
    ]
    grad_queries, grad_keys, grad_values = call(
        unpack_kernel,
        "unpack",
        meta,
        returned,
        [shaped((ROWS, 8 * FEAT), BF16), shaped((ROWS, 4 * HD), BF16), shaped((ROWS, 4 * HD), BF16)],
        [pltpu.VMEM((8, 2 * ROWS, HD), F32)],
    )
    return output, grad_queries, grad_keys, grad_values, grad_weight


def solution(mesh):
    in_specs = (
        P(("dp", "cp"), None),
        P(("dp", "cp"), None),
        P(("dp", "cp"), None),
        P("dp", "cp"),
        P("dp", "cp"),
        P("dp", "cp"),
    )
    out_specs = (
        P("dp", "cp"),
        P(("dp", "cp"), None),
        P(("dp", "cp"), None),
        P(("dp", "cp"), None),
        P("dp", "cp"),
    )
    return jax.shard_map(
        per_device, mesh=mesh, in_specs=in_specs, out_specs=out_specs, check_vma=False
    )
```

time: 630 us -> 188 us (0.30)
  the two profiles are of different devices: /device:TPU:22 before, /device:TPU:9 now
where the time goes in v1:
time: 188 us
  starting transfers between devices  71.3 us (38%)
  waiting for transfers between devices  55.5 us (30%)
  Pallas kernels  44.1 us (23%)
  local copies, waits for them, and re-layouts  8.29 us (4%)
  other arithmetic  7.52 us (4%)
    pallas_call x10, Pallas kernels, call(): pl.pallas_call(kernel, name=name, out_shape=tuple(outs), in_specs=[pl.Blo...  44.1 us
    ppermute x14, starting transfers between devices, per_device(): lax.ppermute(b, 'cp', cp_pairs(*s))  21.6 us
    ppermute x3, waiting for transfers between devices, per_device(): lax.ppermute(attended, 'cp', cp_pairs(dx, 0))  18 us
    ppermute x1, starting transfers between devices, per_device(): core_part = lax.ppermute(send, 'dp', core_pairs())  10.6 us
    ppermute x3, waiting for transfers between devices, per_device(): lax.ppermute(p, 'cp', cp_pairs(dx, 0))  10.4 us
    ppermute x4, starting transfers between devices, per_device(): others = [lax.ppermute(w, 'dp', core_pairs()) for w in mine]  9.99 us
    ppermute x3, starting transfers between devices, per_device(): lax.ppermute(attended, 'cp', cp_pairs(dx, 0))  9.97 us
    ppermute x14, waiting for transfers between devices, per_device(): lax.ppermute(b, 'cp', cp_pairs(*s))  9.65 us
  transfers between devices with their start and end apart: 37, of which 9 were waited for; matrix products, arithmetic and copies ran while one was open for 4% of the time, Pallas kernels for 23%

profile of v1, /device:TPU:9, one launch (start us, length us, event | category | flops | bytes accessed | tf_op | source)
XLA Modules:
  0.0 187.6 jit_solution(6300647834273951787)
XLA Ops:
  0.6 2.1 %collective-permute-start.10 = (bf16[192,384]{1,0:T(8,128)(2,1)}, bf16[192,384]{1,0:T(8,128)(2,1)S(1)}, u32[]{:S(2)}, u32[]{:S(2)}) collective-permute-start(bf16[192,384]{1,0:T(8,128)(2,1)} %param.10), channel_id=1, source_target_pairs={{0,64},{2,66},{4,68},{6,70},{8,72},{10,74},{12,76},{14,78},{16,80}... | collective-permute-start | bytes 442376 | tf_op jit(solution)/shard_map/ppermute | solution.py:291
  2.7 1.9 %collective-permute-start.11 = (bf16[192,384]{1,0:T(8,128)(2,1)}, bf16[192,384]{1,0:T(8,128)(2,1)S(1)}, u32[]{:S(2)}, u32[]{:S(2)}) collective-permute-start(bf16[192,384]{1,0:T(8,128)(2,1)} %param.10), channel_id=1, source_target_pairs={{64,1},{66,3},{68,5},{70,7},{72,9},{74,11},{76,13},{78,15},{80,17}... | collective-permute-start | bytes 442376 | tf_op jit(solution)/shard_map/ppermute | solution.py:290
  10.7 3.8 %collective-permute-start.14 = (bf16[192,768]{1,0:T(8,128)(2,1)S(1)}, bf16[192,768]{1,0:T(8,128)(2,1)S(1)}, u32[]{:S(2)}, u32[]{:S(2)}) collective-permute-start(bf16[192,768]{1,0:T(8,128)(2,1)S(1)} %pad_maximum_fusion.refs_0_), channel_id=1, source_target_pairs={{0,48},{8,56},{16,0},{24,8},{32,16},{40,24},{48,32},{56,40},{64,11... | collective-permute-start | bytes 884744 | tf_op jit(solution)/shard_map/ppermute | solution.py:295
  14.5 4.7 %collective-permute-start.2 = (bf16[656,128]{1,0:T(8,128)(2,1)S(1)}, bf16[656,128]{1,0:T(8,128)(2,1)S(1)}, u32[]{:S(2)}, u32[]{:S(2)}) collective-permute-start(bf16[656,128]{1,0:T(8,128)(2,1)S(1)} %get-tuple-element.36), channel_id=1, source_target_pairs={{0,3},{1,2},{2,5},{3,4},{4,7},{5,6},{6,1},{7,0},{8,11},{9,10},{10,... | collective-permute-start | bytes 503816 | tf_op jit(solution)/shard_map/ppermute | solution.py:286
  22.6 3.7 %collective-permute-start.6 = (bf16[656,128]{1,0:T(8,128)(2,1)S(1)}, bf16[656,128]{1,0:T(8,128)(2,1)S(1)}, u32[]{:S(2)}, u32[]{:S(2)}) collective-permute-start(bf16[656,128]{1,0:T(8,128)(2,1)S(1)} %get-tuple-element.40), channel_id=1, source_target_pairs={{0,7},{1,6},{2,1},{3,0},{4,3},{5,2},{6,5},{7,4},{8,15},{9,14},{10,... | collective-permute-start | bytes 503816 | tf_op jit(solution)/shard_map/ppermute | solution.py:286
  26.5 5.1 %collective-permute-start.15 = (bf16[192,768]{1,0:T(8,128)(2,1)S(1)}, bf16[192,768]{1,0:T(8,128)(2,1)S(1)}, u32[]{:S(2)}, u32[]{:S(2)}) collective-permute-start(bf16[192,768]{1,0:T(8,128)(2,1)S(1)} %pad_maximum_fusion.refs_0_), channel_id=1, source_target_pairs={{0,8},{8,0},{16,24},{24,16},{32,40},{40,32},{48,56},{56,48},{64,72... | collective-permute-start | bytes 884744 | tf_op jit(solution)/shard_map/ppermute | solution.py:296
  33.8 3.5 %collective-permute-start.18 = (bf16[192,768]{1,0:T(8,128)(2,1)S(1)}, bf16[192,768]{1,0:T(8,128)(2,1)S(1)}, u32[]{:S(2)}, u32[]{:S(2)}) collective-permute-start(bf16[192,768]{1,0:T(8,128)(2,1)S(1)} %collective-permute-done.14.refs_3_), channel_id=1, source_target_pairs={{0,8},{8,0},{16,24},{24,16},{32,40},{40,32},{48,56},{56,48},{64,72... | collective-permute-start | bytes 884744 | tf_op jit(solution)/shard_map/ppermute | solution.py:296
  38.1 6.4 %forward.1 = (bf16[1024,384]{1,0:T(8,128)(2,1)S(1)}, bf16[3,1024,128]{2,1,0:T(8,128)(2,1)S(1)}, bf16[2,1024,128]{2,1,0:T(8,128)(2,1)S(1)}, f32[8,1024]{1,0:T(8,128)S(1)}) custom-call(s32[4]{0:T(128)S(1)} %pad_add_fusion.meta.refs_0_, bf16[656,128]{1,0:T(8,128)(2,1)S(1)} %get-tuple-element.33.refs_0_, bf16[656,128]{1,0:T(8,128)(2,1)S(1)} %collective-permute-done.refs_1_, ...), custom_call_target="tpu_custom_call" | custom-call | flops 1610612736 | bytes 3473408 | tf_op jit(solution)/shard_map/forward/pallas_call | solution.py:78
  44.5 3.9 %collective-permute-start.9 = (bf16[1024,384]{1,0:T(8,128)(2,1)S(1)}, bf16[1024,384]{1,0:T(8,128)(2,1)S(1)}, u32[]{:S(2)}, u32[]{:S(2)}) collective-permute-start(bf16[1024,384]{1,0:T(8,128)(2,1)S(1)} %get-tuple-element.41.refs_1_.refs_0_), channel_id=1, source_target_pairs={{0,6},{1,7},{2,0},{3,1},{4,2},{5,3},{6,4},{7,5},{8,14},{9,15},{10,... | collective-permute-start | bytes 2359304 | tf_op jit(solution)/shard_map/ppermute | solution.py:316
  49.6 4.9 %collective-permute-start.7 = (bf16[1024,384]{1,0:T(8,128)(2,1)S(1)}, bf16[1024,384]{1,0:T(8,128)(2,1)S(1)}, u32[]{:S(2)}, u32[]{:S(2)}) collective-permute-start(bf16[1024,384]{1,0:T(8,128)(2,1)S(1)} %get-tuple-element.41.refs_1_.refs_0_), channel_id=1, source_target_pairs={{0,2},{1,3},{2,4},{3,5},{4,6},{5,7},{6,0},{7,1},{8,10},{9,11},{10,... | collective-permute-start | bytes 2359304 | tf_op jit(solution)/shard_map/ppermute | solution.py:316
  60.5 6.7 %grad_send.1 = (bf16[1024,384]{1,0:T(8,128)(2,1)S(1)}, bf16[1024,384]{1,0:T(8,128)(2,1)S(1)}, bf16[1024,384]{1,0:T(8,128)(2,1)S(1)}) custom-call(s32[4]{0:T(128)S(1)} %pad_add_fusion.meta.refs_0_, bf16[1024,384]{1,0:T(8,128)(2,1)S(1)} %copy-done.10, bf16[1024,384]{1,0:T(8,128)(2,1)S(1)} %collective-permute-done.20.there_ref.refs_5_, bf16[4,384,768]{2,1,0:T(8,128)(2,1)} %copy-done), custom_call_target="tpu_custom_call" | custom-call | flops 1811939328 | bytes 6291456 | tf_op jit(solution)/shard_map/grad_send/pallas_call | solution.py:78
  67.1 1.8 collective-permute-start.21
  69.0 2.7 %collective-permute-start.23 = (bf16[1024,384]{1,0:T(8,128)(2,1)S(1)}, bf16[1024,384]{1,0:T(8,128)(2,1)S(1)}, u32[]{:S(2)}, u32[]{:S(2)}) collective-permute-start(bf16[1024,384]{1,0:T(8,128)(2,1)S(1)} %get-tuple-element.47), channel_id=1, source_target_pairs={{0,6},{1,7},{2,0},{3,1},{4,2},{5,3},{6,4},{7,5},{8,14},{9,15},{10,... | collective-permute-start | bytes 2359304 | tf_op jit(solution)/shard_map/ppermute | solution.py:327
  71.6 18.0 %collective-permute-done.7.refs_2_.refs_1_ = bf16[1024,384]{1,0:T(8,128)(2,1)S(1)} collective-permute-done((bf16[1024,384]{1,0:T(8,128)(2,1)S(1)}, bf16[1024,384]{1,0:T(8,128)(2,1)S(1)}, u32[]{:S(2)}, u32[]{:S(2)}) %collective-permute-start.7) | collective-permute-done | bytes 786464 | tf_op jit(solution)/shard_map/ppermute | solution.py:316
  89.6 5.9 %grad_weight.1 = (f32[4,192,768]{2,1,0:T(8,128)}, bf16[4,192,768]{2,1,0:T(8,128)(2,1)}) custom-call(s32[4]{0:T(128)S(1)} %pad_add_fusion.meta.refs_0_, bf16[1024,384]{1,0:T(8,128)(2,1)S(1)} %get-tuple-element.41.refs_1_.refs_0_, bf16[1024,384]{1,0:T(8,128)(2,1)S(1)} %collective-permute-done.7.refs_2_.refs_1_, ...), custom_call_target="tpu_custom_call" | custom-call | flops 2415919104 | bytes 8257536 | tf_op jit(solution)/shard_map/grad_weight/pallas_call | solution.py:78
  95.6 10.6 %collective-permute-start.31 = (bf16[4,192,768]{2,1,0:T(8,128)(2,1)}, bf16[4,192,768]{2,1,0:T(8,128)(2,1)}, u32[]{:S(2)}, u32[]{:S(2)}) collective-permute-start(bf16[4,192,768]{2,1,0:T(8,128)(2,1)} %get-tuple-element.60), channel_id=1, source_target_pairs={{0,8},{8,0},{16,24},{24,16},{32,40},{40,32},{48,56},{56,48},{64,72... | collective-permute-start | bytes 3538952 | tf_op jit(solution)/shard_map/ppermute | solution.py:355
  106.2 2.2 %grad_own.1.own_ref = f32[1024,384]{1,0:T(8,128)S(1)} custom-call(s32[4]{0:T(128)S(1)} %pad_add_fusion.meta.refs_0_, bf16[1024,384]{1,0:T(8,128)(2,1)S(1)} %copy-done.11, bf16[1024,384]{1,0:T(8,128)(2,1)S(1)} %collective-permute-done.20.there_ref.refs_5_, bf16[4,384,768]{2,1,0:T(8,128)(2,1)S(1)} %copy-done.1), custom_call_target="tpu_custom_call" | custom-call | flops 603979776 | bytes 5505024 | tf_op jit(solution)/shard_map/grad_own/pallas_call | solution.py:78
  109.5 10.4 %collective-permute-done.22.refs_1_ = bf16[1024,384]{1,0:T(8,128)(2,1)S(1)} collective-permute-done((bf16[1024,384]{1,0:T(8,128)(2,1)S(1)}, bf16[1024,384]{1,0:T(8,128)(2,1)S(1)}, u32[]{:S(2)}, u32[]{:S(2)}) %collective-permute-start.22) | collective-permute-done | bytes 786464 | tf_op jit(solution)/shard_map/ppermute | solution.py:327
  119.9 9.6 %backward.1 = (bf16[640,128]{1,0:T(8,128)(2,1)S(1)}, bf16[640,128]{1,0:T(8,128)(2,1)}, bf16[640,128]{1,0:T(8,128)(2,1)}, bf16[640,128]{1,0:T(8,128)(2,1)}, bf16[...) custom-call(s32[4]{0:T(128)S(1)} %pad_add_fusion.meta.refs_0_, ...), custom_call_target="tpu_custom_call" | custom-call | flops 4026531840 | bytes 6586368 | tf_op jit(solution)/shard_map/backward/pallas_call | solution.py:78
  130.2 3.6 %collective-permute-start.26 = (bf16[640,128]{1,0:T(8,128)(2,1)}, bf16[640,128]{1,0:T(8,128)(2,1)}, u32[]{:S(2)}, u32[]{:S(2)}) collective-permute-start(bf16[640,128]{1,0:T(8,128)(2,1)} %get-tuple-element.51), channel_id=1, source_target_pairs={{0,3},{1,2},{2,5},{3,4},{4,7},{5,6},{6,1},{7,0},{8,11},{9,10},{10,... | collective-permute-start | bytes 491528 | tf_op jit(solution)/shard_map/ppermute | solution.py:399
  133.8 2.9 %collective-permute-start.27 = (bf16[640,128]{1,0:T(8,128)(2,1)}, bf16[640,128]{1,0:T(8,128)(2,1)}, u32[]{:S(2)}, u32[]{:S(2)}) collective-permute-start(bf16[640,128]{1,0:T(8,128)(2,1)} %get-tuple-element.52), channel_id=1, source_target_pairs={{0,4},{1,5},{2,6},{3,7},{4,0},{5,1},{6,2},{7,3},{8,12},{9,13},{10,... | collective-permute-start | bytes 491528 | tf_op jit(solution)/shard_map/ppermute | solution.py:399
  136.8 2.8 %fusion = (bf16[192,768]{1,0:T(8,128)(2,1)}, bf16[192,768]{1,0:T(8,128)(2,1)}, bf16[192,768]{1,0:T(8,128)(2,1)}) fusion(f32[4,192,768]{2,1,0:T(8,128)} %get-tuple-element.59, s32[]{:T(128)S(6)} %select_n.93, bf16[4,192,768]{2,1,0:T(8,128)(2,1)} %collective-permute-done.31, s32[]{:T(128)S(6)} %select_n.97, s32[]{:T(128)S(6)} %select_n.95), kind=kLoop, calls=%fused_computation.5 | loop fusion | flops 1327104 | bytes 3538956 | tf_op jit(solution)/shard_map/convert_element_type | solution.py:371
  139.6 1.8 collective-permute-start.29
  143.2 6.7 %collective-permute-done.26.refs_3_ = bf16[640,128]{1,0:T(8,128)(2,1)} collective-permute-done((bf16[640,128]{1,0:T(8,128)(2,1)}, bf16[640,128]{1,0:T(8,128)(2,1)}, u32[]{:S(2)}, u32[]{:S(2)}) %collective-permute-start.26) | collective-permute-done | bytes 163872 | tf_op jit(solution)/shard_map/ppermute | solution.py:399
  150.1 5.1 %out_there.1 = bf16[1024,384]{1,0:T(8,128)(2,1)} custom-call(s32[4]{0:T(128)S(1)} %pad_add_fusion.meta.refs_0_, bf16[1024,384]{1,0:T(8,128)(2,1)S(1)} %get-tuple-element.41.refs_1_.refs_0_, bf16[1024,384]{1,0:T(8,128)(2,1)S(1)} %copy-done.7, bf16[1024,384]{1,0:T(8,128)(2,1)S(1)} %copy-done.5, bf16[1024,384]{1,0:T(8,128)(2,1)S(1)} %copy-done.3, ...), custom_call_target="tpu_custom_call" | custom-call | flops 1207959552 | bytes 6291456 | tf_op jit(solution)/shard_map/out_there/pallas_call | solution.py:78
  156.5 4.2 %out_here.1 = f32[1024,384]{1,0:T(8,128)S(1)} custom-call(s32[4]{0:T(128)S(1)} %pad_add_fusion.meta.refs_0_, bf16[1024,384]{1,0:T(8,128)(2,1)S(1)} %get-tuple-element.41.refs_1_.refs_0_, bf16[1024,384]{1,0:T(8,128)(2,1)S(1)} %copy-done.7, bf16[1024,384]{1,0:T(8,128)(2,1)S(1)} %copy-done.5, bf16[1024,384]{1,0:T(8,128)(2,1)S(1)} %copy-done.3, ...), custom_call_target="tpu_custom_call" | custom-call | flops 1207959552 | bytes 7077888 | tf_op jit(solution)/shard_map/out_here/pallas_call | solution.py:78
  160.8 2.7 %collective-permute-done.30.refs_7_ = bf16[640,128]{1,0:T(8,128)(2,1)} collective-permute-done((bf16[640,128]{1,0:T(8,128)(2,1)}, bf16[640,128]{1,0:T(8,128)(2,1)}, u32[]{:S(2)}, u32[]{:S(2)}) %collective-permute-start.30) | collective-permute-done | bytes 163872 | tf_op jit(solution)/shard_map/ppermute | solution.py:399
  163.5 2.4 %unpack.1 = (bf16[128,3072]{1,0:T(8,128)(2,1)}, bf16[128,512]{1,0:T(8,128)(2,1)}, bf16[128,512]{1,0:T(8,128)(2,1)}) custom-call(s32[4]{0:T(128)S(1)} %pad_add_fusion.meta.refs_0_, bf16[640,128]{1,0:T(8,128)(2,1)S(1)} %get-tuple-element.48.refs_0_, bf16[640,128]{1,0:T(8,128)(2,1)S(1)} %collective-permute-done.24.refs_1_, ...), custom_call_target="tpu_custom_call" | custom-call | bytes 2359296 | tf_op jit(solution)/shard_map/unpack/pallas_call | solution.py:78
  167.5 1.9 %collective-permute-start.35 = (bf16[192,384]{1,0:T(8,128)(2,1)S(1)}, bf16[192,384]{1,0:T(8,128)(2,1)S(1)}, u32[]{:S(2)}, u32[]{:S(2)}) collective-permute-start(bf16[192,384]{1,0:T(8,128)(2,1)S(1)} %get-tuple-element.64), channel_id=1, source_target_pairs={{64,1},{66,3},{68,5},{70,7},{72,9},{74,11},{76,13},{78,15},{80,17}... | collective-permute-start | bytes 442376 | tf_op jit(solution)/shard_map/ppermute | solution.py:374
  169.5 9.4 %collective-permute-done.19 = bf16[1024,384]{1,0:T(8,128)(2,1)} collective-permute-done((bf16[1024,384]{1,0:T(8,128)(2,1)}, bf16[1024,384]{1,0:T(8,128)(2,1)}, u32[]{:S(2)}, u32[]{:S(2)}) %collective-permute-start.19) | collective-permute-done | bytes 786464 | tf_op jit(solution)/shard_map/ppermute | solution.py:345
  179.0 2.2 %add_convert_fusion = bf16[1024,384]{1,0:T(8,128)(2,1)} fusion(f32[1024,384]{1,0:T(8,128)S(1)} %out_here.1, bf16[1024,384]{1,0:T(8,128)(2,1)} %collective-permute-done.19), kind=kLoop, calls=%fused_computation | loop fusion | flops 1179648 | bytes 3145728 | tf_op jit(solution)/shard_map/convert_element_type | solution.py:380
  181.2 5.7 %collective-permute-done.35 = bf16[192,384]{1,0:T(8,128)(2,1)S(1)} collective-permute-done((bf16[192,384]{1,0:T(8,128)(2,1)S(1)}, bf16[192,384]{1,0:T(8,128)(2,1)S(1)}, u32[]{:S(2)}, u32[]{:S(2)}) %collective-permute-start.35) | collective-permute-done | bytes 147488 | tf_op jit(solution)/shard_map/ppermute | solution.py:374
  (102 shorter events, 27.3 us)
Async XLA Ops:
  0.6 9.9 %collective-permute-start.10 = (bf16[192,384]{1,0:T(8,128)(2,1)}, bf16[192,384]{1,0:T(8,128)(2,1)S(1)}, u32[]{:S(2)}, u32[]{:S(2)}) collective-permute-start(bf16[192,384]{1,0:T(8,128)(2,1)} %param.10), channel_id=1, source_target_pairs={{0,64},{2,66},{4,68},{6,70},{8,72},{10,74},{12,76},{14,78},{16,80}... | collective-permute-start | bytes 442376 | tf_op jit(solution)/shard_map/ppermute | solution.py:291
  9.2 11.4 %collective-permute-start = (bf16[656,128]{1,0:T(8,128)(2,1)S(1)}, bf16[656,128]{1,0:T(8,128)(2,1)S(1)}, u32[]{:S(2)}, u32[]{:S(2)}) collective-permute-start(bf16[656,128]{1,0:T(8,128)(2,1)S(1)} %get-tuple-element.34), channel_id=1, source_target_pairs={{0,1},{1,0},{2,3},{3,2},{4,5},{5,4},{6,7},{7,6},{8,9},{9,8},{10,11... | collective-permute-start | bytes 503816 | tf_op jit(solution)/shard_map/ppermute | solution.py:286
  9.3 11.8 %collective-permute-start.1 = (bf16[656,128]{1,0:T(8,128)(2,1)S(1)}, bf16[656,128]{1,0:T(8,128)(2,1)S(1)}, u32[]{:S(2)}, u32[]{:S(2)}) collective-permute-start(bf16[656,128]{1,0:T(8,128)(2,1)S(1)} %get-tuple-element.35), channel_id=1, source_target_pairs={{0,2},{1,3},{2,4},{3,5},{4,6},{5,7},{6,0},{7,1},{8,10},{9,11},{10,... | collective-permute-start | bytes 503816 | tf_op jit(solution)/shard_map/ppermute | solution.py:286
  10.7 23.2 %collective-permute-start.14 = (bf16[192,768]{1,0:T(8,128)(2,1)S(1)}, bf16[192,768]{1,0:T(8,128)(2,1)S(1)}, u32[]{:S(2)}, u32[]{:S(2)}) collective-permute-start(bf16[192,768]{1,0:T(8,128)(2,1)S(1)} %pad_maximum_fusion.refs_0_), channel_id=1, source_target_pairs={{0,48},{8,56},{16,0},{24,8},{32,16},{40,24},{48,32},{56,40},{64,11... | collective-permute-start | bytes 884744 | tf_op jit(solution)/shard_map/ppermute | solution.py:295
  14.5 8.1 %collective-permute-start.2 = (bf16[656,128]{1,0:T(8,128)(2,1)S(1)}, bf16[656,128]{1,0:T(8,128)(2,1)S(1)}, u32[]{:S(2)}, u32[]{:S(2)}) collective-permute-start(bf16[656,128]{1,0:T(8,128)(2,1)S(1)} %get-tuple-element.36), channel_id=1, source_target_pairs={{0,3},{1,2},{2,5},{3,4},{4,7},{5,6},{6,1},{7,0},{8,11},{9,10},{10,... | collective-permute-start | bytes 503816 | tf_op jit(solution)/shard_map/ppermute | solution.py:286
  20.6 10.9 %collective-permute-start.4 = (bf16[656,128]{1,0:T(8,128)(2,1)S(1)}, bf16[656,128]{1,0:T(8,128)(2,1)S(1)}, u32[]{:S(2)}, u32[]{:S(2)}) collective-permute-start(bf16[656,128]{1,0:T(8,128)(2,1)S(1)} %get-tuple-element.38), channel_id=1, source_target_pairs={{0,5},{1,4},{2,7},{3,6},{4,1},{5,0},{6,3},{7,2},{8,13},{9,12},{10,... | collective-permute-start | bytes 503816 | tf_op jit(solution)/shard_map/ppermute | solution.py:286
  21.1 12.0 %collective-permute-start.5 = (bf16[656,128]{1,0:T(8,128)(2,1)S(1)}, bf16[656,128]{1,0:T(8,128)(2,1)S(1)}, u32[]{:S(2)}, u32[]{:S(2)}) collective-permute-start(bf16[656,128]{1,0:T(8,128)(2,1)S(1)} %get-tuple-element.39), channel_id=1, source_target_pairs={{0,6},{1,7},{2,0},{3,1},{4,2},{5,3},{6,4},{7,5},{8,14},{9,15},{10,... | collective-permute-start | bytes 503816 | tf_op jit(solution)/shard_map/ppermute | solution.py:286
  22.6 14.8 %collective-permute-start.6 = (bf16[656,128]{1,0:T(8,128)(2,1)S(1)}, bf16[656,128]{1,0:T(8,128)(2,1)S(1)}, u32[]{:S(2)}, u32[]{:S(2)}) collective-permute-start(bf16[656,128]{1,0:T(8,128)(2,1)S(1)} %get-tuple-element.40), channel_id=1, source_target_pairs={{0,7},{1,6},{2,1},{3,0},{4,3},{5,2},{6,5},{7,4},{8,15},{9,14},{10,... | collective-permute-start | bytes 503816 | tf_op jit(solution)/shard_map/ppermute | solution.py:286
  26.5 18.0 %collective-permute-start.15 = (bf16[192,768]{1,0:T(8,128)(2,1)S(1)}, bf16[192,768]{1,0:T(8,128)(2,1)S(1)}, u32[]{:S(2)}, u32[]{:S(2)}) collective-permute-start(bf16[192,768]{1,0:T(8,128)(2,1)S(1)} %pad_maximum_fusion.refs_0_), channel_id=1, source_target_pairs={{0,8},{8,0},{16,24},{24,16},{32,40},{40,32},{48,56},{56,48},{64,72... | collective-permute-start | bytes 884744 | tf_op jit(solution)/shard_map/ppermute | solution.py:296
  31.6 16.8 %collective-permute-start.13 = (bf16[192,768]{1,0:T(8,128)(2,1)S(1)}, bf16[192,768]{1,0:T(8,128)(2,1)S(1)}, u32[]{:S(2)}, u32[]{:S(2)}) collective-permute-start(bf16[192,768]{1,0:T(8,128)(2,1)S(1)} %pad_maximum_fusion.refs_0_), channel_id=1, source_target_pairs={{0,32},{8,40},{16,48},{24,56},{32,0},{40,8},{48,16},{56,24},{64,96... | collective-permute-start | bytes 884744 | tf_op jit(solution)/shard_map/ppermute | solution.py:295
  33.1 16.5 %collective-permute-start.12 = (bf16[192,768]{1,0:T(8,128)(2,1)S(1)}, bf16[192,768]{1,0:T(8,128)(2,1)S(1)}, u32[]{:S(2)}, u32[]{:S(2)}) collective-permute-start(bf16[192,768]{1,0:T(8,128)(2,1)S(1)} %pad_maximum_fusion.refs_0_), channel_id=1, source_target_pairs={{0,16},{8,24},{16,32},{24,40},{32,48},{40,56},{48,0},{56,8},{64,80... | collective-permute-start | bytes 884744 | tf_op jit(solution)/shard_map/ppermute | solution.py:295
  33.8 20.6 %collective-permute-start.18 = (bf16[192,768]{1,0:T(8,128)(2,1)S(1)}, bf16[192,768]{1,0:T(8,128)(2,1)S(1)}, u32[]{:S(2)}, u32[]{:S(2)}) collective-permute-start(bf16[192,768]{1,0:T(8,128)(2,1)S(1)} %collective-permute-done.14.refs_3_), channel_id=1, source_target_pairs={{0,8},{8,0},{16,24},{24,16},{32,40},{40,32},{48,56},{56,48},{64,72... | collective-permute-start | bytes 884744 | tf_op jit(solution)/shard_map/ppermute | solution.py:296
  37.4 23.1 %collective-permute-start.20 = (bf16[1024,384]{1,0:T(8,128)(2,1)S(1)}, bf16[1024,384]{1,0:T(8,128)(2,1)S(1)}, u32[]{:S(2)}, u32[]{:S(2)}) collective-permute-start(bf16[1024,384]{1,0:T(8,128)(2,1)S(1)} %copy-done.10), channel_id=1, source_target_pairs={{0,1},{1,0},{2,3},{3,2},{4,5},{5,4},{6,7},{7,6},{8,9},{9,8},{10,11... | collective-permute-start | bytes 2359304 | tf_op jit(solution)/shard_map/ppermute | solution.py:288
  44.5 24.5 %collective-permute-start.9 = (bf16[1024,384]{1,0:T(8,128)(2,1)S(1)}, bf16[1024,384]{1,0:T(8,128)(2,1)S(1)}, u32[]{:S(2)}, u32[]{:S(2)}) collective-permute-start(bf16[1024,384]{1,0:T(8,128)(2,1)S(1)} %get-tuple-element.41.refs_1_.refs_0_), channel_id=1, source_target_pairs={{0,6},{1,7},{2,0},{3,1},{4,2},{5,3},{6,4},{7,5},{8,14},{9,15},{10,... | collective-permute-start | bytes 2359304 | tf_op jit(solution)/shard_map/ppermute | solution.py:316
  48.4 23.3 %collective-permute-start.8 = (bf16[1024,384]{1,0:T(8,128)(2,1)S(1)}, bf16[1024,384]{1,0:T(8,128)(2,1)S(1)}, u32[]{:S(2)}, u32[]{:S(2)}) collective-permute-start(bf16[1024,384]{1,0:T(8,128)(2,1)S(1)} %get-tuple-element.41.refs_1_.refs_0_), channel_id=1, source_target_pairs={{0,4},{1,5},{2,6},{3,7},{4,0},{5,1},{6,2},{7,3},{8,12},{9,13},{10,... | collective-permute-start | bytes 2359304 | tf_op jit(solution)/shard_map/ppermute | solution.py:316
  49.6 40.0 %collective-permute-start.7 = (bf16[1024,384]{1,0:T(8,128)(2,1)S(1)}, bf16[1024,384]{1,0:T(8,128)(2,1)S(1)}, u32[]{:S(2)}, u32[]{:S(2)}) collective-permute-start(bf16[1024,384]{1,0:T(8,128)(2,1)S(1)} %get-tuple-element.41.refs_1_.refs_0_), channel_id=1, source_target_pairs={{0,2},{1,3},{2,4},{3,5},{4,6},{5,7},{6,0},{7,1},{8,10},{9,11},{10,... | collective-permute-start | bytes 2359304 | tf_op jit(solution)/shard_map/ppermute | solution.py:316
  67.1 42.4 %collective-permute-start.21 = (bf16[1024,384]{1,0:T(8,128)(2,1)S(1)}, bf16[1024,384]{1,0:T(8,128)(2,1)S(1)}, u32[]{:S(2)}, u32[]{:S(2)}) collective-permute-start(bf16[1024,384]{1,0:T(8,128)(2,1)S(1)} %get-tuple-element.45), channel_id=1, source_target_pairs={{0,4},{1,5},{2,6},{3,7},{4,0},{5,1},{6,2},{7,3},{8,12},{9,13},{10,... | collective-permute-start | bytes 2359304 | tf_op jit(solution)/shard_map/ppermute | solution.py:327
  69.0 50.9 %collective-permute-start.22 = (bf16[1024,384]{1,0:T(8,128)(2,1)S(1)}, bf16[1024,384]{1,0:T(8,128)(2,1)S(1)}, u32[]{:S(2)}, u32[]{:S(2)}) collective-permute-start(bf16[1024,384]{1,0:T(8,128)(2,1)S(1)} %get-tuple-element.46), channel_id=1, source_target_pairs={{0,2},{1,3},{2,4},{3,5},{4,6},{5,7},{6,0},{7,1},{8,10},{9,11},{10,... | collective-permute-start | bytes 2359304 | tf_op jit(solution)/shard_map/ppermute | solution.py:327
  69.0 50.9 %collective-permute-start.23 = (bf16[1024,384]{1,0:T(8,128)(2,1)S(1)}, bf16[1024,384]{1,0:T(8,128)(2,1)S(1)}, u32[]{:S(2)}, u32[]{:S(2)}) collective-permute-start(bf16[1024,384]{1,0:T(8,128)(2,1)S(1)} %get-tuple-element.47), channel_id=1, source_target_pairs={{0,6},{1,7},{2,0},{3,1},{4,2},{5,3},{6,4},{7,5},{8,14},{9,15},{10,... | collective-permute-start | bytes 2359304 | tf_op jit(solution)/shard_map/ppermute | solution.py:327
  95.6 41.2 %collective-permute-start.31 = (bf16[4,192,768]{2,1,0:T(8,128)(2,1)}, bf16[4,192,768]{2,1,0:T(8,128)(2,1)}, u32[]{:S(2)}, u32[]{:S(2)}) collective-permute-start(bf16[4,192,768]{2,1,0:T(8,128)(2,1)} %get-tuple-element.60), channel_id=1, source_target_pairs={{0,8},{8,0},{16,24},{24,16},{32,40},{40,32},{48,56},{56,48},{64,72... | collective-permute-start | bytes 3538952 | tf_op jit(solution)/shard_map/ppermute | solution.py:355
  130.2 9.4 %collective-permute-start.24 = (bf16[640,128]{1,0:T(8,128)(2,1)}, bf16[640,128]{1,0:T(8,128)(2,1)S(1)}, u32[]{:S(2)}, u32[]{:S(2)}) collective-permute-start(bf16[640,128]{1,0:T(8,128)(2,1)} %get-tuple-element.49), channel_id=1, source_target_pairs={{0,1},{1,0},{2,3},{3,2},{4,5},{5,4},{6,7},{7,6},{8,9},{9,8},{10,11... | collective-permute-start | bytes 491528 | tf_op jit(solution)/shard_map/ppermute | solution.py:399
  130.2 11.2 %collective-permute-start.25 = (bf16[640,128]{1,0:T(8,128)(2,1)}, bf16[640,128]{1,0:T(8,128)(2,1)}, u32[]{:S(2)}, u32[]{:S(2)}) collective-permute-start(bf16[640,128]{1,0:T(8,128)(2,1)} %get-tuple-element.50), channel_id=1, source_target_pairs={{0,2},{1,3},{2,4},{3,5},{4,6},{5,7},{6,0},{7,1},{8,10},{9,11},{10,... | collective-permute-start | bytes 491528 | tf_op jit(solution)/shard_map/ppermute | solution.py:399
  130.2 19.7 %collective-permute-start.26 = (bf16[640,128]{1,0:T(8,128)(2,1)}, bf16[640,128]{1,0:T(8,128)(2,1)}, u32[]{:S(2)}, u32[]{:S(2)}) collective-permute-start(bf16[640,128]{1,0:T(8,128)(2,1)} %get-tuple-element.51), channel_id=1, source_target_pairs={{0,3},{1,2},{2,5},{3,4},{4,7},{5,6},{6,1},{7,0},{8,11},{9,10},{10,... | collective-permute-start | bytes 491528 | tf_op jit(solution)/shard_map/ppermute | solution.py:399
  133.8 16.2 %collective-permute-start.27 = (bf16[640,128]{1,0:T(8,128)(2,1)}, bf16[640,128]{1,0:T(8,128)(2,1)}, u32[]{:S(2)}, u32[]{:S(2)}) collective-permute-start(bf16[640,128]{1,0:T(8,128)(2,1)} %get-tuple-element.52), channel_id=1, source_target_pairs={{0,4},{1,5},{2,6},{3,7},{4,0},{5,1},{6,2},{7,3},{8,12},{9,13},{10,... | collective-permute-start | bytes 491528 | tf_op jit(solution)/shard_map/ppermute | solution.py:399
  136.8 18.4 %collective-permute-start.28 = (bf16[640,128]{1,0:T(8,128)(2,1)}, bf16[640,128]{1,0:T(8,128)(2,1)S(1)}, u32[]{:S(2)}, u32[]{:S(2)}) collective-permute-start(bf16[640,128]{1,0:T(8,128)(2,1)} %get-tuple-element.53), channel_id=1, source_target_pairs={{0,5},{1,4},{2,7},{3,6},{4,1},{5,0},{6,3},{7,2},{8,13},{9,12},{10,... | collective-permute-start | bytes 491528 | tf_op jit(solution)/shard_map/ppermute | solution.py:399
  139.6 16.2 %collective-permute-start.29 = (bf16[640,128]{1,0:T(8,128)(2,1)S(1)}, bf16[640,128]{1,0:T(8,128)(2,1)S(1)}, u32[]{:S(2)}, u32[]{:S(2)}) collective-permute-start(bf16[640,128]{1,0:T(8,128)(2,1)S(1)} %copy-done.20), channel_id=1, source_target_pairs={{0,6},{1,7},{2,0},{3,1},{4,2},{5,3},{6,4},{7,5},{8,14},{9,15},{10,... | collective-permute-start | bytes 491528 | tf_op jit(solution)/shard_map/ppermute | solution.py:399
  141.5 24.4 %collective-permute-start.32 = (bf16[192,768]{1,0:T(8,128)(2,1)}, bf16[192,768]{1,0:T(8,128)(2,1)}, u32[]{:S(2)}, u32[]{:S(2)}) collective-permute-start(bf16[192,768]{1,0:T(8,128)(2,1)} %get-tuple-element.61), channel_id=1, source_target_pairs={{0,16},{8,24},{16,32},{24,40},{32,48},{40,56},{48,0},{56,8},{64,80... | collective-permute-start | bytes 884744 | tf_op jit(solution)/shard_map/ppermute | solution.py:371
  149.9 16.0 %collective-permute-start.34 = (bf16[192,768]{1,0:T(8,128)(2,1)}, bf16[192,768]{1,0:T(8,128)(2,1)}, u32[]{:S(2)}, u32[]{:S(2)}) collective-permute-start(bf16[192,768]{1,0:T(8,128)(2,1)} %get-tuple-element.62), channel_id=1, source_target_pairs={{0,48},{8,56},{16,0},{24,8},{32,16},{40,24},{48,32},{56,40},{64,11... | collective-permute-start | bytes 884744 | tf_op jit(solution)/shard_map/ppermute | solution.py:371
  150.0 15.9 %collective-permute-start.33 = (bf16[192,768]{1,0:T(8,128)(2,1)}, bf16[192,768]{1,0:T(8,128)(2,1)}, u32[]{:S(2)}, u32[]{:S(2)}) collective-permute-start(bf16[192,768]{1,0:T(8,128)(2,1)} %get-tuple-element.63), channel_id=1, source_target_pairs={{0,32},{8,40},{16,48},{24,56},{32,0},{40,8},{48,16},{56,24},{64,96... | collective-permute-start | bytes 884744 | tf_op jit(solution)/shard_map/ppermute | solution.py:371
  155.8 23.1 %collective-permute-start.19 = (bf16[1024,384]{1,0:T(8,128)(2,1)}, bf16[1024,384]{1,0:T(8,128)(2,1)}, u32[]{:S(2)}, u32[]{:S(2)}) collective-permute-start(bf16[1024,384]{1,0:T(8,128)(2,1)} %out_there.1), channel_id=1, source_target_pairs={{0,1},{1,0},{2,3},{3,2},{4,5},{5,4},{6,7},{7,6},{8,9},{9,8},{10,11... | collective-permute-start | bytes 2359304 | tf_op jit(solution)/shard_map/ppermute | solution.py:345
  167.5 19.3 %collective-permute-start.35 = (bf16[192,384]{1,0:T(8,128)(2,1)S(1)}, bf16[192,384]{1,0:T(8,128)(2,1)S(1)}, u32[]{:S(2)}, u32[]{:S(2)}) collective-permute-start(bf16[192,384]{1,0:T(8,128)(2,1)S(1)} %get-tuple-element.64), channel_id=1, source_target_pairs={{64,1},{66,3},{68,5},{70,7},{72,9},{74,11},{76,13},{78,15},{80,17}... | collective-permute-start | bytes 442376 | tf_op jit(solution)/shard_map/ppermute | solution.py:374
  169.5 17.4 %collective-permute-start.36 = (bf16[192,384]{1,0:T(8,128)(2,1)S(1)}, bf16[192,384]{1,0:T(8,128)(2,1)S(1)}, u32[]{:S(2)}, u32[]{:S(2)}) collective-permute-start(bf16[192,384]{1,0:T(8,128)(2,1)S(1)} %get-tuple-element.65), channel_id=1, source_target_pairs={{64,0},{66,2},{68,4},{70,6},{72,8},{74,10},{76,12},{78,14},{80,16}... | collective-permute-start | bytes 442376 | tf_op jit(solution)/shard_map/ppermute | solution.py:375
  (26 other events, 221.9 us)

commit v2 on v1

v2 whole, which is shorter than its diff:
```python
import math

import jax
import jax.numpy as jnp
from jax import lax
from jax.experimental import pallas as pl
from jax.experimental.pallas import tpu as pltpu
from jax.sharding import PartitionSpec as P


NX = 4
GROUP = 1024
HD = 128
HEADS = 3
FEAT = 384
ROWS = 128
QB = 256
SEG_ROWS = 16
PACK = 5 * ROWS + SEG_ROWS
SCALE = 1.0 / math.sqrt(HD)
EXP2_SCALE = SCALE * math.log2(math.e)
F32 = jnp.float32
BF16 = jnp.bfloat16


def cp_pairs(dx, dh):
    return [(x * 2 + h, ((x + dx) % NX) * 2 + (h ^ dh)) for x in range(NX) for h in range(2)]


def z_pairs(dz):
    return [
        (y * 8 + z * 2 + c, y * 8 + ((z + dz) % 4) * 2 + c)
        for y in range(2)
        for z in range(4)
        for c in range(2)
    ]


def core_pairs():
    return [(d, d ^ 1) for d in range(16)]


def x_to_z_pairs(dy):
    return [
        (((y * 4 + z) * 2 + c) * 8 + x * 2 + h, (((y ^ dy) * 4 + x) * 2 + c) * 8 + z * 2 + h)
        for y in range(2)
        for z in range(4)
        for c in range(2)
        for x in range(4)
        for h in range(2)
    ]


def dot_nt(a, b):
    return lax.dot_general(a, b, (((1,), (1,)), ((), ())), preferred_element_type=F32)


def dot_nn(a, b):
    return lax.dot_general(a, b, (((1,), (0,)), ((), ())), preferred_element_type=F32)


def dot_tn(a, b):
    return lax.dot_general(a, b, (((0,), (0,)), ((), ())), preferred_element_type=F32)


def call(kernel, name, meta, operands, outs, scratch=(), span=0, after=(), hbm=(), vmem=48):
    count = len(operands)

    def body(meta_ref, *refs):
        kernel(meta_ref, *refs[:count], *refs[count + len(after) :])

    return pl.pallas_call(
        body,
        name=name,
        out_shape=tuple(outs),
        in_specs=[pl.BlockSpec(memory_space=pltpu.SMEM)]
        + [pl.BlockSpec(memory_space=pl.ANY if i in hbm else pltpu.VMEM) for i in range(count)]
        + [pl.BlockSpec(memory_space=pl.ANY)] * len(after),
        out_specs=tuple(pl.BlockSpec(memory_space=pltpu.VMEM) for _ in outs),
        scratch_shapes=list(scratch),
        compiler_params=pltpu.CompilerParams(vmem_limit_bytes=vmem * 1024 * 1024),
        cost_estimate=pl.CostEstimate(flops=span * 10**9, bytes_accessed=0, transcendentals=0),
    )(meta, *operands, *after)


def shaped(shape, dtype):
    return jax.ShapeDtypeStruct(shape, dtype)


def pack_kernel(meta, q_ref, k_ref, v_ref, seg_ref, out, sems):
    copies = []
    for to in range(8):
        to_x, to_h = to // 2, to % 2
        q_off = (to_h * NX + to_x) * FEAT
        kv_off = (to_h * 2 + to_x // 2) * HD
        sources = [q_ref.at[:, pl.ds(q_off + head * HD, HD)] for head in range(HEADS)]
        sources += [k_ref.at[:, pl.ds(kv_off, HD)], v_ref.at[:, pl.ds(kv_off, HD)]]
        for i, source in enumerate(sources):
            copies.append(
                pltpu.make_async_copy(source, out.at[to, pl.ds(i * ROWS, ROWS), :], sems.at[to, i])
            )
            copies[-1].start()
    seg = jnp.broadcast_to(seg_ref[...].astype(F32), (SEG_ROWS, ROWS)).astype(BF16)
    for to in range(8):
        out[to, pl.ds(5 * ROWS, SEG_ROWS), :] = seg
    for copy in copies:
        copy.wait()


def transposed_scores(k, q, first, qb):
    scores = dot_nt(k, q)
    key_pos = lax.broadcasted_iota(jnp.int32, scores.shape, 0)
    query_pos = lax.broadcasted_iota(jnp.int32, scores.shape, 1) + qb * QB
    return jnp.where((key_pos <= query_pos) & (key_pos >= first), scores * EXP2_SCALE, -1e30)


def forward_kernel(meta, *refs):
    blocks, (att_ref, q_ref, kv_ref, stat_ref, vt_ref) = refs[0], refs[1:]
    seg_sum = jnp.zeros((1, ROWS), F32)
    for source in range(8):
        rows = pl.ds(source * ROWS, ROWS)
        for head in range(HEADS):
            q_ref[head, rows, :] = blocks[source, pl.ds(head * ROWS, ROWS), :]
        kv_ref[0, rows, :] = blocks[source, pl.ds(3 * ROWS, ROWS), :]
        kv_ref[1, rows, :] = blocks[source, pl.ds(4 * ROWS, ROWS), :]
        seg_sum = seg_sum + blocks[source, pl.ds(5 * ROWS, SEG_ROWS), :].astype(F32)[0:1]
    second = jnp.sum(seg_sum, axis=1, keepdims=True)
    boundary = (GROUP - second).astype(jnp.int32)
    position = lax.broadcasted_iota(jnp.int32, (1, GROUP), 1)
    first = jnp.where(position >= boundary, boundary, 0)
    stat_ref[...] = jnp.zeros_like(stat_ref)
    stat_ref[3:4, :] = first.astype(F32)
    vt_ref[...] = kv_ref[1].astype(F32).T.astype(BF16)
    for qb in range(GROUP // QB):
        keys = (qb + 1) * QB
        rows = pl.ds(qb * QB, QB)
        for head in range(HEADS):
            scores = transposed_scores(
                kv_ref[0, pl.ds(0, keys), :], q_ref[head, rows, :], first[:, qb * QB : keys], qb
            )
            peak = jnp.max(scores, axis=0, keepdims=True)
            weights = jnp.exp2(scores - peak)
            total = jnp.sum(weights, axis=0, keepdims=True)
            stat_ref[head : head + 1, rows] = peak + jnp.log2(total)
            mixed = dot_nn(vt_ref[:, pl.ds(0, keys)], weights.astype(BF16)) / total
            att_ref[rows, pl.ds(head * HD, HD)] = mixed.T.astype(BF16)


def backward_kernel(meta, q_ref, kv_ref, stat_ref, own_ref, *refs):
    high_ref, low_ref, out, kt_ref, g_ref, gq_ref, gk_ref, gv_ref = refs
    half = GROUP // 2
    for received, first in ((low_ref, 0), (high_ref, half)):
        total = own_ref[pl.ds(first, half), :] + received[...].astype(F32)
        for head in range(HEADS):
            g_ref[head, pl.ds(first, half), :] = total[:, head * HD : (head + 1) * HD].astype(BF16)
    kt_ref[...] = kv_ref[0].astype(F32).T.astype(BF16)
    gk_ref[...] = jnp.zeros_like(gk_ref)
    gv_ref[...] = jnp.zeros_like(gv_ref)
    first = stat_ref[3:4, :].astype(jnp.int32)
    for qb in range(GROUP // QB):
        keys = (qb + 1) * QB
        rows = pl.ds(qb * QB, QB)
        span = pl.ds(0, keys)
        for head in range(HEADS):
            q = q_ref[head, rows, :]
            g = g_ref[head, rows, :]
            scores = transposed_scores(kv_ref[0, span, :], q, first[:, qb * QB : keys], qb)
            prob = jnp.exp2(scores - stat_ref[head : head + 1, rows])
            grad_prob = dot_nt(kv_ref[1, span, :], g)
            delta = jnp.sum(prob * grad_prob, axis=0, keepdims=True)
            grad_logit = (prob * (grad_prob - delta)).astype(BF16)
            gv_ref[span, :] += dot_nn(prob.astype(BF16), g)
            gk_ref[span, :] += dot_nn(grad_logit, q)
            gq = dot_nn(kt_ref[:, span], grad_logit) * SCALE
            gq_ref[head, rows, :] = gq.T.astype(BF16)
    for to in range(8):
        rows = pl.ds(to * ROWS, ROWS)
        for head in range(HEADS):
            out[to, pl.ds(head * ROWS, ROWS), :] = gq_ref[head, rows, :]
        out[to, pl.ds(3 * ROWS, ROWS), :] = (gk_ref[rows, :] * SCALE).astype(BF16)
        out[to, pl.ds(4 * ROWS, ROWS), :] = gv_ref[rows, :].astype(BF16)


def unpack_kernel(meta, blocks, gq_ref, gk_ref, gv_ref):
    def block(head, first):
        return blocks[(head % NX) * 2 + head // NX, pl.ds(first * ROWS, ROWS), :]

    for source in range(8):
        for head in range(HEADS):
            gq_ref[:, pl.ds(source * FEAT + head * HD, HD)] = block(source, head)
    for head in range(4):
        cols = pl.ds(head * HD, HD)
        for first, out in ((3, gk_ref), (4, gv_ref)):
            both = block(2 * head, first).astype(F32) + block(2 * head + 1, first).astype(F32)
            out[:, cols] = both.astype(BF16)


def gather_columns(x, refs, out):
    own, right, left, low, high = refs
    half = GROUP // 2
    out[:, pl.ds(0, FEAT)] = own[...]
    out[:, pl.ds(FEAT, FEAT)] = right[...]
    out[pl.ds(0, half), pl.ds(2 * FEAT, FEAT)] = low[...]
    out[pl.ds(half, half), pl.ds(2 * FEAT, FEAT)] = high[...]
    out[:, pl.ds(3 * FEAT, FEAT)] = left[...]


def place_weight(meta, w_ref, part, column, out, row, col):
    which = jnp.where(part == meta[4], 0, 1)
    for core in range(2):
        out[pl.ds(row + core * 192, 192), pl.ds(col, FEAT)] = w_ref[column, core, which]


def grad_kernel(meta, *refs):
    grads, w_ref, high_ref, low_ref, own_ref, held, wide = refs[:5], *refs[5:]
    x, h = meta[0], meta[1]
    gather_columns(x, grads, held)
    for shift in range(NX):
        slot = lax.rem(x - shift + NX, NX)
        place_weight(meta, w_ref, 1 - h, slot, wide, 0, shift * FEAT)
        place_weight(meta, w_ref, h, slot, wide, FEAT, shift * FEAT)

    for send, first in ((high_ref, GROUP // 2), (low_ref, 0)):

        @pl.loop(0, GROUP // QB // 2)
        def _(i):
            row = pl.multiple_of(i * QB, QB)
            rows = pl.ds(row + first, QB)
            total = dot_nt(held[rows, :], wide[...])
            send[pl.ds(row, QB), :] = total[:, :FEAT].astype(BF16)
            own_ref[rows, :] = total[:, FEAT:]


def out_kernel(meta, here_ref, there_ref, w_ref, out, wide):
    h = meta[1]
    for column in range(NX):
        place_weight(meta, w_ref, h, column, wide, 0, column * FEAT)
        place_weight(meta, w_ref, 1 - h, column, wide, FEAT, column * FEAT)

    @pl.loop(0, GROUP // QB)
    def _(i):
        rows = pl.ds(pl.multiple_of(i * QB, QB), QB)
        total = dot_nn(here_ref[rows, :], wide[pl.ds(0, FEAT), :]) + dot_nn(
            there_ref[rows, :], wide[pl.ds(FEAT, FEAT), :]
        )
        for column in range(NX):
            out[column, rows, :] = total[:, column * FEAT : (column + 1) * FEAT].astype(BF16)


def grad_weight_kernel(meta, *refs):
    att, grads, (keep_ref, *sends, held, total) = refs[:2], refs[2:7], refs[7:]
    x, h, core = meta[0], meta[1], meta[3]
    gather_columns(x, grads, held)
    for which in range(2):
        part = h if which == 0 else 1 - h
        turned = att[which][...].T
        total[...] = dot_nn(turned, held[...])
        for shift in range(NX):
            slot = lax.rem(x - shift + NX, NX)
            cols = pl.ds(shift * FEAT, FEAT)
            keep_ref[part, slot] = total[pl.ds(pl.multiple_of(core * 192, 64), 192), cols]
            for part_rows in range(2):
                row = pl.multiple_of((1 - core) * 192 + part_rows * 96, 32)
                sends[which * 2 + part_rows][slot] = total[pl.ds(row, 96), cols].astype(BF16)


def z_kernel(meta, keep_ref, *refs):
    parts, own_ref, outs = refs[:4], refs[4], refs[5:]
    h, z = meta[1], meta[2]
    for dz in range(4):
        slot = lax.rem(z + dz, 4)
        for which, row in ((0, h), (1, 1 - h)):
            for part_rows in range(2):
                rows = pl.ds(part_rows * 96, 96)
                total = keep_ref[row, slot, rows, :] + parts[which * 2 + part_rows][slot].astype(F32)
                if dz == 0:
                    own_ref[row, rows, :] = total
                else:
                    outs[dz - 1][row, rows, :] = total.astype(BF16)


def y_kernel(meta, own_ref, *refs):
    parts, (keep_ref, send_ref) = refs[:3], refs[3:]
    y_lo = meta[4]
    for which, out in ((y_lo, keep_ref), (1 - y_lo, send_ref)):
        total = own_ref[which]
        for part in parts:
            total = total + part[which].astype(F32)
        out[...] = total.astype(out.dtype)


def sum_kernel(meta, a_ref, b_ref, out):
    out[...] = a_ref[...].astype(F32) + b_ref[...].astype(F32)


def stack_kernel(meta, a_ref, b_ref, grad_ref, out, grad_out, sem):
    copy = pltpu.make_async_copy(grad_ref, grad_out, sem)
    copy.start()
    out[0] = a_ref[...]
    out[1] = b_ref[...]
    copy.wait()


def per_device(queries, key_heads, value_heads, segment_ids, out_weight, grad_out):
    dp = lax.axis_index("dp")
    cp = lax.axis_index("cp")
    x, h = cp // 2, cp % 2
    y_lo, z, core = dp // 8, (dp // 2) % 4, dp % 2
    meta = jnp.stack([x, h, z, core, y_lo]).astype(jnp.int32)
    both = ("dp", "cp")
    half = GROUP // 2

    turned = [lax.ppermute(out_weight, both, x_to_z_pairs(dy)) for dy in (0, 1)]
    (packed,) = call(
        pack_kernel,
        "pack",
        meta,
        (queries, key_heads, value_heads, segment_ids),
        [shaped((8, PACK, ROWS), BF16)],
        [pltpu.SemaphoreType.DMA((8, 5))],
        hbm=(0, 1, 2),
        vmem=60,
    )
    blocks = lax.all_to_all(packed, "cp", 0, 0)
    turned, grad_out = call(
        stack_kernel,
        "turned",
        meta,
        (*turned, grad_out),
        [shaped((2, 192, FEAT), BF16), shaped((GROUP, FEAT), BF16)],
        [pltpu.SemaphoreType.DMA],
        span=20,
        after=(packed,),
        hbm=(2,),
    )
    from_left = lax.ppermute(grad_out, "cp", cp_pairs(1, 0))
    from_right = lax.ppermute(grad_out, "cp", cp_pairs(3, 0))
    weight = lax.all_gather(
        turned, "dp", axis=0, axis_index_groups=[list(range(8)), list(range(8, 16))]
    ).reshape(NX, 2, 2, 192, FEAT)
    low = lax.ppermute(from_left[:half], "cp", cp_pairs(1, 0))
    high = lax.ppermute(from_right[half:], "cp", cp_pairs(3, 0))
    grads_out = (grad_out, from_left, from_right, low, high)

    attended, q_all, kv_all, stats = call(
        forward_kernel,
        "forward",
        meta,
        (blocks,),
        [
            shaped((GROUP, FEAT), BF16),
            shaped((HEADS, GROUP, HD), BF16),
            shaped((2, GROUP, HD), BF16),
            shaped((8, GROUP), F32),
        ],
        [pltpu.VMEM((HD, GROUP), BF16)],
        span=100,
    )
    att = (attended, lax.ppermute(attended, "cp", cp_pairs(0, 1)))

    send_high, send_low, grad_own = call(
        grad_kernel,
        "grad_attended",
        meta,
        (*grads_out, weight),
        [shaped((half, FEAT), BF16)] * 2 + [shaped((GROUP, FEAT), F32)],
        [pltpu.VMEM((GROUP, NX * FEAT), BF16), pltpu.VMEM((2 * FEAT, NX * FEAT), BF16)],
        after=(attended,),
    )
    part_high = lax.ppermute(send_high, "cp", cp_pairs(0, 1))
    part_low = lax.ppermute(send_low, "cp", cp_pairs(0, 1))

    (out_all,) = call(
        out_kernel,
        "out",
        meta,
        (*att, weight),
        [shaped((NX, GROUP, FEAT), BF16)],
        [pltpu.VMEM((2 * FEAT, NX * FEAT), BF16)],
        after=(grad_own,),
        span=20,
    )
    output = lax.psum_scatter(
        out_all,
        "cp",
        scatter_dimension=0,
        axis_index_groups=[[x * 2 + h for x in range(NX)] for h in range(2)],
    )

    keep, *sends = call(
        grad_weight_kernel,
        "grad_weight",
        meta,
        (*att, *grads_out),
        [shaped((2, NX, 192, FEAT), F32)] + [shaped((NX, 96, FEAT), BF16)] * 4,
        [pltpu.VMEM((GROUP, NX * FEAT), BF16), pltpu.VMEM((FEAT, NX * FEAT), F32)],
        after=(out_all, part_high),
        span=80,
    )
    core_parts = [lax.ppermute(p, "dp", core_pairs()) for p in sends]

    z_own, *z_sends = call(
        z_kernel,
        "z_sum",
        meta,
        (keep, *core_parts),
        [shaped((2, 192, FEAT), F32)] + [shaped((2, 192, FEAT), BF16)] * 3,
        after=(part_low,),
    )
    z_parts = [lax.ppermute(p, "dp", z_pairs(dz)) for dz, p in zip((1, 2, 3), z_sends)]

    (grads,) = call(
        backward_kernel,
        "backward",
        meta,
        (q_all, kv_all, stats, grad_own, part_high, part_low),
        [shaped((8, 5 * ROWS, ROWS), BF16)],
        [
            pltpu.VMEM((HD, GROUP), BF16),
            pltpu.VMEM((HEADS, GROUP, HD), BF16),
            pltpu.VMEM((HEADS, GROUP, HD), BF16),
            pltpu.VMEM((GROUP, HD), F32),
            pltpu.VMEM((GROUP, HD), F32),
        ],
        after=(z_own,),
    )
    returned = lax.all_to_all(grads, "cp", 0, 0)

    y_own, y_send = call(
        y_kernel,
        "y_sum",
        meta,
        (z_own, *z_parts),
        [shaped((192, FEAT), BF16), shaped((192, FEAT), BF16)],
        after=(grads,),
        span=15,
    )
    totals = [lax.ppermute(p, both, x_to_z_pairs(dy)) for dy, p in ((0, y_own), (1, y_send))]
    (grad_weight,) = call(sum_kernel, "grad_weight_total", meta, totals, [shaped((192, FEAT), F32)])

    grad_queries, grad_keys, grad_values = call(
        unpack_kernel,
        "unpack",
        meta,
        (returned,),
        [shaped((ROWS, 8 * FEAT), BF16), shaped((ROWS, 4 * HD), BF16), shaped((ROWS, 4 * HD), BF16)],
    )
    return output, grad_queries, grad_keys, grad_values, grad_weight


def solution(mesh):
    in_specs = (
        P(("dp", "cp"), None),
        P(("dp", "cp"), None),
        P(("dp", "cp"), None),
        P("dp", "cp"),
        P("dp", "cp"),
        P("dp", "cp"),
    )
    out_specs = (
        P("dp", "cp"),
        P(("dp", "cp"), None),
        P(("dp", "cp"), None),
        P(("dp", "cp"), None),
        P("dp", "cp"),
    )
    return jax.shard_map(
        per_device, mesh=mesh, in_specs=in_specs, out_specs=out_specs, check_vma=False
    )
```

time: 188 us -> 170 us (0.904)
  the two profiles are of different devices: /device:TPU:9 before, /device:TPU:22 now
where the time goes in v2:
time: 170 us; the launch traced here: 169 us
  waiting for transfers between devices  55.6 us (33%)
  starting transfers between devices  47.5 us (28%)
  Pallas kernels  46.9 us (28%)
  between operations  14.2 us (8%)
  local copies, waits for them, and re-layouts  4.95 us (3%)
    pallas_call x11, Pallas kernels, call(): pl.pallas_call(body, name=name, out_shape=tuple(outs), in_specs=[pl.Block...  46.9 us
    ppermute x2, waiting for transfers between devices, per_device(): lax.ppermute(p, both, x_to_z_pairs(dy))  26.9 us
    all_to_all x1, waiting for transfers between devices, per_device(): blocks = lax.all_to_all(packed, 'cp', 0, 0)  10.1 us
    ppermute x2, starting transfers between devices, per_device(): turned = [lax.ppermute(out_weight, both, x_to_z_pairs(dy)) for dy in (0, 1)]  8.04 us
    ppermute x1, waiting for transfers between devices, per_device(): high = lax.ppermute(from_right[half:], 'cp', cp_pairs(3, 0))  8.03 us
    all_to_all x1, starting transfers between devices, per_device(): returned = lax.all_to_all(grads, 'cp', 0, 0)  7.93 us
    all_to_all x1, starting transfers between devices, per_device(): blocks = lax.all_to_all(packed, 'cp', 0, 0)  7.91 us
    ppermute x2, starting transfers between devices, per_device(): lax.ppermute(p, both, x_to_z_pairs(dy))  7.33 us
  transfers between devices with their start and end apart: 22, of which 11 were waited for; matrix products, arithmetic and copies ran while one was open for 0% of the time, Pallas kernels for 28%

profile of v2, /device:TPU:22, one launch (start us, length us, event | category | flops | bytes accessed | tf_op | source)
XLA Modules:
  0.0 169.0 jit_solution(11148617758398318454)
XLA Ops:
  7.2 4.8 %collective-permute-start.2 = (bf16[192,384]{1,0:T(8,128)(2,1)}, bf16[192,384]{1,0:T(8,128)(2,1)S(1)}, u32[]{:S(2)}, u32[]{:S(2)}) collective-permute-start(bf16[192,384]{1,0:T(8,128)(2,1)} %param.10), channel_id=1, source_target_pairs={{0,64},{1,65},{2,80},{3,81},{4,96},{5,97},{6,112},{7,113},{8,72},{... | collective-permute-start | bytes 442376 | tf_op jit(solution)/shard_map/ppermute | solution.py:313
  11.9 3.3 %collective-permute-start.1 = (bf16[192,384]{1,0:T(8,128)(2,1)}, bf16[192,384]{1,0:T(8,128)(2,1)S(1)}, u32[]{:S(2)}, u32[]{:S(2)}) collective-permute-start(bf16[192,384]{1,0:T(8,128)(2,1)} %param.10), channel_id=1, source_target_pairs={{0,0},{1,1},{2,16},{3,17},{4,32},{5,33},{6,48},{7,49},{8,8},{9,9},... | collective-permute-start | bytes 442376 | tf_op jit(solution)/shard_map/ppermute | solution.py:313
  15.9 3.4 %pack.1.refs_3_ = bf16[8,656,128]{2,1,0:T(8,128)(2,1)} custom-call(s32[5]{0:T(128)} %stack.23.meta_ref, bf16[128,3072]{1,0:T(8,128)(2,1)} %refs_0_.1, bf16[128,512]{1,0:T(8,128)(2,1)} %refs_1_.1, bf16[128,512]{1,0:T(8,128)(2,1)} %refs_2_.2, s32[1,128]{1,0:T(1,128)} %refs_3_.1), custom_call_target="tpu_custom_call" | custom-call | tf_op jit(solution)/shard_map/pack/pallas_call | solution.py:72
  19.3 7.9 %all-to-all-start = ((bf16[8,656,128]{2,1,0:T(8,128)(2,1)}), bf16[8,656,128]{2,1,0:T(8,128)(2,1)S(1)}, u32[]{:S(2)}, u32[]{:S(2)}) async-start(bf16[8,656,128]{2,1,0:T(8,128)(2,1)} %pack.1.refs_3_), calls=%async_computation | async-start | bytes 2686976 | tf_op jit(solution)/shard_map/all_to_all | solution.py:324
  27.2 1.4 collective-permute-done.1.refs_0_
  29.7 1.7 turned.1
  31.5 3.2 %collective-permute-start.3 = (bf16[1024,384]{1,0:T(8,128)(2,1)}, bf16[1024,384]{1,0:T(8,128)(2,1)S(1)}, u32[]{:S(2)}, u32[]{:S(2)}) collective-permute-start(bf16[1024,384]{1,0:T(8,128)(2,1)} %get-tuple-element.30.refs_0_.refs_2_), channel_id=1, source_target_pairs={{0,2},{1,3},{2,4},{3,5},{4,6},{5,7},{6,0},{7,1},{8,10},{9,11},{10,... | collective-permute-start | bytes 2359304 | tf_op jit(solution)/shard_map/ppermute | solution.py:336
  34.8 10.1 %all-to-all-done.refs_0_ = bf16[8,656,128]{2,1,0:T(8,128)(2,1)S(1)} async-done(((bf16[8,656,128]{2,1,0:T(8,128)(2,1)}), bf16[8,656,128]{2,1,0:T(8,128)(2,1)S(1)}, u32[]{:S(2)}, u32[]{:S(2)}) %all-to-all-start) | async-done | bytes 1343520 | tf_op jit(solution)/shard_map/all_to_all | solution.py:324
  44.9 7.3 %forward.1 = (bf16[1024,384]{1,0:T(8,128)(2,1)}, bf16[3,1024,128]{2,1,0:T(8,128)(2,1)S(1)}, bf16[2,1024,128]{2,1,0:T(8,128)(2,1)S(1)}, f32[8,1024]{1,0:T(8,128)S(1)}) custom-call(s32[5]{0:T(128)S(1)} %copy-done.8, bf16[8,656,128]{2,1,0:T(8,128)(2,1)S(1)} %all-to-all-done.refs_0_), custom_call_target="tpu_custom_call" | custom-call | flops 99999997952 | tf_op jit(solution)/shard_map/forward/pallas_call | solution.py:72
  52.9 5.9 %collective-permute-done.4.refs_2_.refs_4_ = bf16[1024,384]{1,0:T(8,128)(2,1)S(1)} collective-permute-done((bf16[1024,384]{1,0:T(8,128)(2,1)}, bf16[1024,384]{1,0:T(8,128)(2,1)S(1)}, u32[]{:S(2)}, u32[]{:S(2)}) %collective-permute-start.4) | collective-permute-done | bytes 786464 | tf_op jit(solution)/shard_map/ppermute | solution.py:337
  58.8 1.6 collective-permute-start.6
  60.5 1.8 %collective-permute-start.5 = (bf16[512,384]{1,0:T(8,128)(2,1)S(1)}, bf16[512,384]{1,0:T(8,128)(2,1)S(1)}, u32[]{:S(2)}, u32[]{:S(2)}) collective-permute-start(bf16[512,384]{1,0:T(8,128)(2,1)S(1)} %slice.8), channel_id=1, source_target_pairs={{0,2},{1,3},{2,4},{3,5},{4,6},{5,7},{6,0},{7,1},{8,10},{9,11},{10,... | collective-permute-start | bytes 1179656 | tf_op jit(solution)/shard_map/ppermute | solution.py:341
  62.2 8.0 %collective-permute-done.6.refs_4_.refs_6_ = bf16[512,384]{1,0:T(8,128)(2,1)S(1)} collective-permute-done((bf16[512,384]{1,0:T(8,128)(2,1)S(1)}, bf16[512,384]{1,0:T(8,128)(2,1)S(1)}, u32[]{:S(2)}, u32[]{:S(2)}) %collective-permute-start.6) | collective-permute-done | bytes 393248 | tf_op jit(solution)/shard_map/ppermute | solution.py:342
  70.3 7.1 %grad_attended.1 = (bf16[512,384]{1,0:T(8,128)(2,1)S(1)}, bf16[512,384]{1,0:T(8,128)(2,1)}, f32[1024,384]{1,0:T(8,128)}) custom-call(s32[5]{0:T(128)S(1)} %copy-done.8, bf16[1024,384]{1,0:T(8,128)(2,1)} %get-tuple-element.30.refs_0_.refs_2_, bf16[1024,384]{1,0:T(8,128)(2,1)S(1)} %collective-permute-done.3.refs_1_.refs_3_, ...), custom_call_target="tpu_custom_call" | custom-call | tf_op jit(solution)/shard_map/grad_attended/pallas_call | solution.py:72
  77.4 1.4 collective-permute-start.7
  78.8 2.1 %collective-permute-start.8 = (bf16[512,384]{1,0:T(8,128)(2,1)}, bf16[512,384]{1,0:T(8,128)(2,1)S(1)}, u32[]{:S(2)}, u32[]{:S(2)}) collective-permute-start(bf16[512,384]{1,0:T(8,128)(2,1)} %get-tuple-element.36), channel_id=1, source_target_pairs={{0,1},{1,0},{2,3},{3,2},{4,5},{5,4},{6,7},{7,6},{8,9},{9,8},{10,11... | collective-permute-start | bytes 1179656 | tf_op jit(solution)/shard_map/ppermute | solution.py:371
  80.9 1.4 copy-done.4
  82.3 7.1 %out.1.refs_7_ = bf16[4,1024,384]{2,1,0:T(8,128)(2,1)} custom-call(s32[5]{0:T(128)S(1)} %copy-done.8, bf16[1024,384]{1,0:T(8,128)(2,1)} %get-tuple-element.28.refs_6_.refs_0_, bf16[1024,384]{1,0:T(8,128)(2,1)} %collective-permute-done.refs_1_, bf16[4,2,2,192,384]{4,3,2,1,0:T(8,128)(2,1)S(1)} %bitcast.8, f32[1024,384]{1,0:T(8,128)S(1)} %copy-done.4), custom_call_target="tpu_custom_call" | custom-call | flops 20000000000 | tf_op jit(solution)/shard_map/out/pallas_call | solution.py:72
  89.5 1.4 collective-permute-done.7.refs_8_.refs_4_
  90.9 6.2 %grad_weight.1 = (f32[2,4,192,384]{3,2,1,0:T(8,128)}, bf16[4,96,384]{2,1,0:T(8,128)(2,1)S(1)}, bf16[4,96,384]{2,1,0:T(8,128)(2,1)S(1)}, bf16[4,96,384]{2,1,0:T(8,128)(2,1)S(1)}, bf16[4,96,384]{2,1,0:T(8,128)(2,1)S(1)}) custom-call(s32[5]{0:T(128)S(1)} %copy-done.8, bf16[1024,384]{1,0:T(8,128)(2,1)} %get-tuple-element.28.refs_6_.refs_0_, ...), custom_call_target="tpu_custom_call" | custom-call | flops 80000000000 | tf_op jit(solution)/shard_map/grad_weight/pallas_call | solution.py:72
  100.0 1.7 copy-done.2
  101.7 1.6 z_sum.1
  103.3 1.5 collective-permute-start.13
  104.8 2.5 %collective-permute-start.14 = (bf16[2,192,384]{2,1,0:T(8,128)(2,1)}, bf16[2,192,384]{2,1,0:T(8,128)(2,1)S(1)}, u32[]{:S(2)}, u32[]{:S(2)}) collective-permute-start(bf16[2,192,384]{2,1,0:T(8,128)(2,1)} %get-tuple-element.47), channel_id=1, source_target_pairs={{0,32},{8,40},{16,48},{24,56},{32,0},{40,8},{48,16},{56,24},{64,96... | collective-permute-start | bytes 884744 | tf_op jit(solution)/shard_map/ppermute | solution.py:410
  107.5 8.8 %backward.1.refs_4_ = bf16[8,640,128]{2,1,0:T(8,128)(2,1)} custom-call(s32[5]{0:T(128)S(1)} %copy-done.8, bf16[3,1024,128]{2,1,0:T(8,128)(2,1)S(1)} %copy-done.7, bf16[2,1024,128]{2,1,0:T(8,128)(2,1)S(1)} %get-tuple-element.33.refs_1_, f32[8,1024]{1,0:T(8,128)S(1)} %get-tuple-element.34.refs_2_, f32[1024,384]{1,0:T(8,128)S(1)} %copy-done.5, ...), custom_call_target="tpu_custom_call" | custom-call | tf_op jit(solution)/shard_map/backward/pallas_call | solution.py:72
  116.3 7.9 %all-to-all-start.1 = ((bf16[8,640,128]{2,1,0:T(8,128)(2,1)}), bf16[8,640,128]{2,1,0:T(8,128)(2,1)S(1)}, u32[]{:S(2)}, u32[]{:S(2)}) async-start(bf16[8,640,128]{2,1,0:T(8,128)(2,1)} %backward.1.refs_4_), calls=%async_computation.2 | async-start | bytes 2621440 | tf_op jit(solution)/shard_map/all_to_all | solution.py:427
  125.0 3.5 %collective-permute-start.16 = (bf16[192,384]{1,0:T(8,128)(2,1)S(1)}, bf16[192,384]{1,0:T(8,128)(2,1)S(1)}, u32[]{:S(2)}, u32[]{:S(2)}) collective-permute-start(bf16[192,384]{1,0:T(8,128)(2,1)S(1)} %get-tuple-element.49), channel_id=1, source_target_pairs={{0,0},{1,1},{2,16},{3,17},{4,32},{5,33},{6,48},{7,49},{8,8},{9,9},... | collective-permute-start | bytes 442376 | tf_op jit(solution)/shard_map/ppermute | solution.py:438
  128.5 3.8 %collective-permute-start.17 = (bf16[192,384]{1,0:T(8,128)(2,1)S(1)}, bf16[192,384]{1,0:T(8,128)(2,1)S(1)}, u32[]{:S(2)}, u32[]{:S(2)}) collective-permute-start(bf16[192,384]{1,0:T(8,128)(2,1)S(1)} %get-tuple-element.50), channel_id=1, source_target_pairs={{0,64},{1,65},{2,80},{3,81},{4,96},{5,97},{6,112},{7,113},{8,72},{... | collective-permute-start | bytes 442376 | tf_op jit(solution)/shard_map/ppermute | solution.py:438
  132.3 20.4 %collective-permute-done.16.refs_0_ = bf16[192,384]{1,0:T(8,128)(2,1)S(1)} collective-permute-done((bf16[192,384]{1,0:T(8,128)(2,1)S(1)}, bf16[192,384]{1,0:T(8,128)(2,1)S(1)}, u32[]{:S(2)}, u32[]{:S(2)}) %collective-permute-start.16) | collective-permute-done | bytes 147488 | tf_op jit(solution)/shard_map/ppermute | solution.py:438
  152.7 6.4 %collective-permute-done.17.refs_1_ = bf16[192,384]{1,0:T(8,128)(2,1)S(1)} collective-permute-done((bf16[192,384]{1,0:T(8,128)(2,1)S(1)}, bf16[192,384]{1,0:T(8,128)(2,1)S(1)}, u32[]{:S(2)}, u32[]{:S(2)}) %collective-permute-start.17) | collective-permute-done | bytes 147488 | tf_op jit(solution)/shard_map/ppermute | solution.py:438
  159.2 1.3 grad_weight_total.1
  160.5 1.7 %unpack.1 = (bf16[128,3072]{1,0:T(8,128)(2,1)}, bf16[128,512]{1,0:T(8,128)(2,1)}, bf16[128,512]{1,0:T(8,128)(2,1)}) custom-call(s32[5]{0:T(128)S(1)} %copy-done.8, bf16[8,640,128]{2,1,0:T(8,128)(2,1)S(1)} %all-to-all-done.1.refs_0_), custom_call_target="tpu_custom_call" | custom-call | tf_op jit(solution)/shard_map/unpack/pallas_call | solution.py:72
  (48 shorter events, 6.5 us)
Async XLA Ops:
  7.2 20.0 %collective-permute-start.2 = (bf16[192,384]{1,0:T(8,128)(2,1)}, bf16[192,384]{1,0:T(8,128)(2,1)S(1)}, u32[]{:S(2)}, u32[]{:S(2)}) collective-permute-start(bf16[192,384]{1,0:T(8,128)(2,1)} %param.10), channel_id=1, source_target_pairs={{0,64},{1,65},{2,80},{3,81},{4,96},{5,97},{6,112},{7,113},{8,72},{... | collective-permute-start | bytes 442376 | tf_op jit(solution)/shard_map/ppermute | solution.py:313
  11.9 16.7 %collective-permute-start.1 = (bf16[192,384]{1,0:T(8,128)(2,1)}, bf16[192,384]{1,0:T(8,128)(2,1)S(1)}, u32[]{:S(2)}, u32[]{:S(2)}) collective-permute-start(bf16[192,384]{1,0:T(8,128)(2,1)} %param.10), channel_id=1, source_target_pairs={{0,0},{1,1},{2,16},{3,17},{4,32},{5,33},{6,48},{7,49},{8,8},{9,9},... | collective-permute-start | bytes 442376 | tf_op jit(solution)/shard_map/ppermute | solution.py:313
  19.3 9.3 %copy-start = (bf16[8,656,128]{2,1,0:T(8,128)(2,1)S(1)}, bf16[8,656,128]{2,1,0:T(8,128)(2,1)}, u32[]{:S(2)}) copy-start(bf16[8,656,128]{2,1,0:T(8,128)(2,1)} %pack.1.refs_3_) | copy-start | bytes 4030468
  19.3 9.3 %copy-start.8 = (s32[5]{0:T(128)S(1)}, s32[5]{0:T(128)}, u32[]{:S(2)}) copy-start(s32[5]{0:T(128)} %stack.23.meta_ref) | copy-start | bytes 64
  19.3 25.6 %all-to-all-start = ((bf16[8,656,128]{2,1,0:T(8,128)(2,1)}), bf16[8,656,128]{2,1,0:T(8,128)(2,1)S(1)}, u32[]{:S(2)}, u32[]{:S(2)}) async-start(bf16[8,656,128]{2,1,0:T(8,128)(2,1)} %pack.1.refs_3_), calls=%async_computation | async-start | bytes 2686976 | tf_op jit(solution)/shard_map/all_to_all | solution.py:324
  27.2 43.1 %all-gather.3.cloned.1.call-start = ((), (), s32[]{:S(2)}) async-start(), calls=%async_computation.4 | async-start | bytes 2654208 | tf_op jit(solution)/shard_map/all_gather | solution.py:338
  28.6 1.1 copy-start.9
  31.4 27.4 %collective-permute-start.4 = (bf16[1024,384]{1,0:T(8,128)(2,1)}, bf16[1024,384]{1,0:T(8,128)(2,1)S(1)}, u32[]{:S(2)}, u32[]{:S(2)}) collective-permute-start(bf16[1024,384]{1,0:T(8,128)(2,1)} %get-tuple-element.30.refs_0_.refs_2_), channel_id=1, source_target_pairs={{0,6},{1,7},{2,0},{3,1},{4,2},{5,3},{6,4},{7,5},{8,14},{9,15},{10,... | collective-permute-start | bytes 2359304 | tf_op jit(solution)/shard_map/ppermute | solution.py:337
  31.5 28.9 %collective-permute-start.3 = (bf16[1024,384]{1,0:T(8,128)(2,1)}, bf16[1024,384]{1,0:T(8,128)(2,1)S(1)}, u32[]{:S(2)}, u32[]{:S(2)}) collective-permute-start(bf16[1024,384]{1,0:T(8,128)(2,1)} %get-tuple-element.30.refs_0_.refs_2_), channel_id=1, source_target_pairs={{0,2},{1,3},{2,4},{3,5},{4,6},{5,7},{6,0},{7,1},{8,10},{9,11},{10,... | collective-permute-start | bytes 2359304 | tf_op jit(solution)/shard_map/ppermute | solution.py:336
  34.7 127.4 %reduce-scatter.2.cloned.1.call-start = ((), (), s32[]{:S(2)}) async-start(), calls=%async_computation.3 | async-start | bytes 3932160 | tf_op jit(solution)/shard_map/reduce_scatter | solution.py:383
  52.1 8.3 %copy-start.6 = (bf16[3,1024,128]{2,1,0:T(8,128)(2,1)}, bf16[3,1024,128]{2,1,0:T(8,128)(2,1)S(1)}, u32[]{:S(2)}) copy-start(bf16[3,1024,128]{2,1,0:T(8,128)(2,1)S(1)} %get-tuple-element.32.refs_0_) | copy-start | bytes 2359300
  52.1 28.8 %collective-permute-start = (bf16[1024,384]{1,0:T(8,128)(2,1)}, bf16[1024,384]{1,0:T(8,128)(2,1)}, u32[]{:S(2)}, u32[]{:S(2)}) collective-permute-start(bf16[1024,384]{1,0:T(8,128)(2,1)} %get-tuple-element.28.refs_6_.refs_0_), channel_id=1, source_target_pairs={{0,1},{1,0},{2,3},{3,2},{4,5},{5,4},{6,7},{7,6},{8,9},{9,8},{10,11... | collective-permute-start | bytes 2359304 | tf_op jit(solution)/shard_map/ppermute | solution.py:359
  58.8 18.6 %copy-start.3 = (bf16[1024,384]{1,0:T(8,128)(2,1)}, bf16[1024,384]{1,0:T(8,128)(2,1)S(1)}, u32[]{:S(2)}) copy-start(bf16[1024,384]{1,0:T(8,128)(2,1)S(1)} %collective-permute-done.4.refs_2_.refs_4_) | copy-start | bytes 2359300
  58.8 11.5 %collective-permute-start.6 = (bf16[512,384]{1,0:T(8,128)(2,1)S(1)}, bf16[512,384]{1,0:T(8,128)(2,1)S(1)}, u32[]{:S(2)}, u32[]{:S(2)}) collective-permute-start(bf16[512,384]{1,0:T(8,128)(2,1)S(1)} %slice.9), channel_id=1, source_target_pairs={{0,6},{1,7},{2,0},{3,1},{4,2},{5,3},{6,4},{7,5},{8,14},{9,15},{10,... | collective-permute-start | bytes 1179656 | tf_op jit(solution)/shard_map/ppermute | solution.py:342
  60.5 9.8 %collective-permute-start.5 = (bf16[512,384]{1,0:T(8,128)(2,1)S(1)}, bf16[512,384]{1,0:T(8,128)(2,1)S(1)}, u32[]{:S(2)}, u32[]{:S(2)}) collective-permute-start(bf16[512,384]{1,0:T(8,128)(2,1)S(1)} %slice.8), channel_id=1, source_target_pairs={{0,2},{1,3},{2,4},{3,5},{4,6},{5,7},{6,0},{7,1},{8,10},{9,11},{10,... | collective-permute-start | bytes 1179656 | tf_op jit(solution)/shard_map/ppermute | solution.py:341
  70.3 10.6 %copy-start.1 = (bf16[16,192,384]{2,1,0:T(8,128)(2,1)S(1)}, bf16[16,192,384]{2,1,0:T(8,128)(2,1)}, u32[]{:S(2)}) copy-start(bf16[16,192,384]{2,1,0:T(8,128)(2,1)} %all-gather.3.cloned.1.call-done) | copy-start | bytes 7077892
  77.4 13.6 %collective-permute-start.7 = (bf16[512,384]{1,0:T(8,128)(2,1)S(1)}, bf16[512,384]{1,0:T(8,128)(2,1)S(1)}, u32[]{:S(2)}, u32[]{:S(2)}) collective-permute-start(bf16[512,384]{1,0:T(8,128)(2,1)S(1)} %get-tuple-element.35), channel_id=1, source_target_pairs={{0,1},{1,0},{2,3},{3,2},{4,5},{5,4},{6,7},{7,6},{8,9},{9,8},{10,11... | collective-permute-start | bytes 1179656 | tf_op jit(solution)/shard_map/ppermute | solution.py:370
  78.8 19.3 %collective-permute-start.8 = (bf16[512,384]{1,0:T(8,128)(2,1)}, bf16[512,384]{1,0:T(8,128)(2,1)S(1)}, u32[]{:S(2)}, u32[]{:S(2)}) collective-permute-start(bf16[512,384]{1,0:T(8,128)(2,1)} %get-tuple-element.36), channel_id=1, source_target_pairs={{0,1},{1,0},{2,3},{3,2},{4,5},{5,4},{6,7},{7,6},{8,9},{9,8},{10,11... | collective-permute-start | bytes 1179656 | tf_op jit(solution)/shard_map/ppermute | solution.py:371
  80.9 1.4 copy-start.4
  97.1 1.6 collective-permute-start.9
  97.1 2.0 %collective-permute-start.10 = (bf16[4,96,384]{2,1,0:T(8,128)(2,1)S(1)}, bf16[4,96,384]{2,1,0:T(8,128)(2,1)S(1)}, u32[]{:S(2)}, u32[]{:S(2)}) collective-permute-start(bf16[4,96,384]{2,1,0:T(8,128)(2,1)S(1)} %get-tuple-element.39), channel_id=1, source_target_pairs={{0,8},{8,0},{16,24},{24,16},{32,40},{40,32},{48,56},{56,48},{64,72... | collective-permute-start | bytes 884744 | tf_op jit(solution)/shard_map/ppermute | solution.py:400
  97.6 1.9 %collective-permute-start.11 = (bf16[4,96,384]{2,1,0:T(8,128)(2,1)S(1)}, bf16[4,96,384]{2,1,0:T(8,128)(2,1)S(1)}, u32[]{:S(2)}, u32[]{:S(2)}) collective-permute-start(bf16[4,96,384]{2,1,0:T(8,128)(2,1)S(1)} %get-tuple-element.40), channel_id=1, source_target_pairs={{0,8},{8,0},{16,24},{24,16},{32,40},{40,32},{48,56},{56,48},{64,72... | collective-permute-start | bytes 884744 | tf_op jit(solution)/shard_map/ppermute | solution.py:400
  97.6 2.3 %collective-permute-start.12 = (bf16[4,96,384]{2,1,0:T(8,128)(2,1)S(1)}, bf16[4,96,384]{2,1,0:T(8,128)(2,1)S(1)}, u32[]{:S(2)}, u32[]{:S(2)}) collective-permute-start(bf16[4,96,384]{2,1,0:T(8,128)(2,1)S(1)} %get-tuple-element.41), channel_id=1, source_target_pairs={{0,8},{8,0},{16,24},{24,16},{32,40},{40,32},{48,56},{56,48},{64,72... | collective-permute-start | bytes 884744 | tf_op jit(solution)/shard_map/ppermute | solution.py:400
  100.0 1.7 copy-start.2
  101.7 5.8 %copy-start.5 = (f32[1024,384]{1,0:T(8,128)S(1)}, f32[1024,384]{1,0:T(8,128)}, u32[]{:S(2)}) copy-start(f32[1024,384]{1,0:T(8,128)} %get-tuple-element.31.refs_3_) | copy-start | bytes 4718596
  101.7 5.8 %copy-start.7 = (bf16[3,1024,128]{2,1,0:T(8,128)(2,1)S(1)}, bf16[3,1024,128]{2,1,0:T(8,128)(2,1)}, u32[]{:S(2)}) copy-start(bf16[3,1024,128]{2,1,0:T(8,128)(2,1)} %copy-done.6) | copy-start | bytes 2359300
  103.3 21.0 %collective-permute-start.13 = (bf16[2,192,384]{2,1,0:T(8,128)(2,1)}, bf16[2,192,384]{2,1,0:T(8,128)(2,1)S(1)}, u32[]{:S(2)}, u32[]{:S(2)}) collective-permute-start(bf16[2,192,384]{2,1,0:T(8,128)(2,1)} %get-tuple-element.46), channel_id=1, source_target_pairs={{0,16},{8,24},{16,32},{24,40},{32,48},{40,56},{48,0},{56,8},{64,80... | collective-permute-start | bytes 884744 | tf_op jit(solution)/shard_map/ppermute | solution.py:410
  104.8 19.4 %collective-permute-start.14 = (bf16[2,192,384]{2,1,0:T(8,128)(2,1)}, bf16[2,192,384]{2,1,0:T(8,128)(2,1)S(1)}, u32[]{:S(2)}, u32[]{:S(2)}) collective-permute-start(bf16[2,192,384]{2,1,0:T(8,128)(2,1)} %get-tuple-element.47), channel_id=1, source_target_pairs={{0,32},{8,40},{16,48},{24,56},{32,0},{40,8},{48,16},{56,24},{64,96... | collective-permute-start | bytes 884744 | tf_op jit(solution)/shard_map/ppermute | solution.py:410
  107.4 16.9 %collective-permute-start.15 = (bf16[2,192,384]{2,1,0:T(8,128)(2,1)}, bf16[2,192,384]{2,1,0:T(8,128)(2,1)S(1)}, u32[]{:S(2)}, u32[]{:S(2)}) collective-permute-start(bf16[2,192,384]{2,1,0:T(8,128)(2,1)} %get-tuple-element.48), channel_id=1, source_target_pairs={{0,48},{8,56},{16,0},{24,8},{32,16},{40,24},{48,32},{56,40},{64,11... | collective-permute-start | bytes 884744 | tf_op jit(solution)/shard_map/ppermute | solution.py:410
  116.3 44.1 %all-to-all-start.1 = ((bf16[8,640,128]{2,1,0:T(8,128)(2,1)}), bf16[8,640,128]{2,1,0:T(8,128)(2,1)S(1)}, u32[]{:S(2)}, u32[]{:S(2)}) async-start(bf16[8,640,128]{2,1,0:T(8,128)(2,1)} %backward.1.refs_4_), calls=%async_computation.2 | async-start | bytes 2621440 | tf_op jit(solution)/shard_map/all_to_all | solution.py:427
  125.0 27.8 %collective-permute-start.16 = (bf16[192,384]{1,0:T(8,128)(2,1)S(1)}, bf16[192,384]{1,0:T(8,128)(2,1)S(1)}, u32[]{:S(2)}, u32[]{:S(2)}) collective-permute-start(bf16[192,384]{1,0:T(8,128)(2,1)S(1)} %get-tuple-element.49), channel_id=1, source_target_pairs={{0,0},{1,1},{2,16},{3,17},{4,32},{5,33},{6,48},{7,49},{8,8},{9,9},... | collective-permute-start | bytes 442376 | tf_op jit(solution)/shard_map/ppermute | solution.py:438
  128.5 30.7 %collective-permute-start.17 = (bf16[192,384]{1,0:T(8,128)(2,1)S(1)}, bf16[192,384]{1,0:T(8,128)(2,1)S(1)}, u32[]{:S(2)}, u32[]{:S(2)}) collective-permute-start(bf16[192,384]{1,0:T(8,128)(2,1)S(1)} %get-tuple-element.50), channel_id=1, source_target_pairs={{0,64},{1,65},{2,80},{3,81},{4,96},{5,97},{6,112},{7,113},{8,72},{... | collective-permute-start | bytes 442376 | tf_op jit(solution)/shard_map/ppermute | solution.py:438
Sparse Core Ops, SparseCore 0:
  34.9 25.0 all-gather.2
  89.6 37.8 reduce-scatter.1

commit v3 on v2

--- a/solution.py
+++ b/solution.py
@@ -18,6 +18,7 @@
 SEG_ROWS = 16
 PACK = 5 * ROWS + SEG_ROWS
 SCALE = 1.0 / math.sqrt(HD)
+FAR = -(2.0**17)
 EXP2_SCALE = SCALE * math.log2(math.e)
 F32 = jnp.float32
 BF16 = jnp.bfloat16
@@ -63,24 +64,38 @@
     return lax.dot_general(a, b, (((0,), (0,)), ((), ())), preferred_element_type=F32)
 
 
-def call(kernel, name, meta, operands, outs, scratch=(), span=0, after=(), hbm=(), vmem=48):
+def call(
+    kernel, name, meta, operands, outs, scratch=(), span=0, after=(), hbm=(), vmem=32, grid=(), blocks=None, out_blocks=None
+):
     count = len(operands)
 
     def body(meta_ref, *refs):
         kernel(meta_ref, *refs[:count], *refs[count + len(after) :])
+
+    def whole(i):
+        return pl.BlockSpec(memory_space=pl.ANY if i in hbm else pltpu.VMEM)
 
     return pl.pallas_call(
         body,
         name=name,
         out_shape=tuple(outs),
+        grid=grid,
         in_specs=[pl.BlockSpec(memory_space=pltpu.SMEM)]
-        + [pl.BlockSpec(memory_space=pl.ANY if i in hbm else pltpu.VMEM) for i in range(count)]
+        + (blocks or [whole(i) for i in range(count)])
         + [pl.BlockSpec(memory_space=pl.ANY)] * len(after),
-        out_specs=tuple(pl.BlockSpec(memory_space=pltpu.VMEM) for _ in outs),
+        out_specs=tuple(out_blocks or [pl.BlockSpec(memory_space=pltpu.VMEM) for _ in outs]),
         scratch_shapes=list(scratch),
         compiler_params=pltpu.CompilerParams(vmem_limit_bytes=vmem * 1024 * 1024),
         cost_estimate=pl.CostEstimate(flops=span * 10**9, bytes_accessed=0, transcendentals=0),
     )(meta, *operands, *after)
+
+
+def row_block(height, width, index):
+    return pl.BlockSpec((height, width), lambda i: (index(i), 0))
+
+
+def whole_block(shape):
+    return pl.BlockSpec(shape, lambda i: (0,) * len(shape))
 
 
 def shaped(shape, dtype):
@@ -107,15 +122,57 @@
         copy.wait()
 
 
-def transposed_scores(k, q, first, qb):
-    scores = dot_nt(k, q)
-    key_pos = lax.broadcasted_iota(jnp.int32, scores.shape, 0)
-    query_pos = lax.broadcasted_iota(jnp.int32, scores.shape, 1) + qb * QB
-    return jnp.where((key_pos <= query_pos) & (key_pos >= first), scores * EXP2_SCALE, -1e30)
-
-
-def forward_kernel(meta, *refs):
-    blocks, (att_ref, q_ref, kv_ref, stat_ref, vt_ref) = refs[0], refs[1:]
+def key_parts(qb):
+    start = QB if qb == 3 else 0
+    return [r for r in ((start, qb * QB, False), (qb * QB, (qb + 1) * QB, True)) if r[0] < r[1]]
+
+
+def widen(boundary, q_ref, k_ref, q_wide, k_wide):
+    shape = (GROUP, HD)
+    column = lax.broadcasted_iota(jnp.int32, shape, 1) == 0
+    second = lax.broadcasted_iota(jnp.int32, shape, 0) >= boundary
+    q_more = jnp.where(column & second, FAR, 0.0).astype(BF16)
+    k_more = jnp.where(column & jnp.logical_not(second), 1.0, 0.0).astype(BF16)
+    for head in range(HEADS):
+        q_wide[head, :, pl.ds(0, HD)] = q_ref[head]
+        q_wide[head, :, pl.ds(HD, HD)] = q_more
+    k_wide[:, pl.ds(0, HD)] = k_ref[0]
+    k_wide[:, pl.ds(HD, HD)] = k_more
+
+
+def transposed_scores(k, q, diagonal):
+    scores = dot_nt(k, q) * EXP2_SCALE
+    if diagonal:
+        key_pos = lax.broadcasted_iota(jnp.int32, scores.shape, 0)
+        query_pos = lax.broadcasted_iota(jnp.int32, scores.shape, 1)
+        scores = jnp.where(key_pos <= query_pos, scores, -1e30)
+    return scores
+
+
+def forward_rows(qbs, q_wide, k_wide, vt_ref, att_ref, stat_ref):
+    base = qbs[0] * QB
+    for qb in qbs:
+        out_rows = pl.ds(qb * QB - base, QB)
+        for head in range(HEADS):
+            q = q_wide[head, pl.ds(qb * QB, QB), :]
+            parts = [
+                (pl.ds(lo, hi - lo), transposed_scores(k_wide[pl.ds(lo, hi - lo), :], q, diagonal))
+                for lo, hi, diagonal in key_parts(qb)
+            ]
+            peaks = [jnp.max(scores, axis=0, keepdims=True) for _, scores in parts]
+            peak = peaks[0] if len(peaks) == 1 else jnp.maximum(*peaks)
+            total, mixed = 0.0, 0.0
+            for span, scores in parts:
+                weights = jnp.exp2(scores - peak)
+                total = total + jnp.sum(weights, axis=0, keepdims=True)
+                mixed = mixed + dot_nn(vt_ref[:, span], weights.astype(BF16))
+            stat_ref[head : head + 1, out_rows] = peak + jnp.log2(total)
+            att_ref[out_rows, pl.ds(head * HD, HD)] = (mixed / total).T.astype(BF16)
+
+
+def forward_low_kernel(
+    meta, blocks, att_ref, q_ref, kv_ref, vt_ref, boundary_ref, stat_ref, q_wide, k_wide
+):
     seg_sum = jnp.zeros((1, ROWS), F32)
     for source in range(8):
         rows = pl.ds(source * ROWS, ROWS)
@@ -126,53 +183,49 @@
         seg_sum = seg_sum + blocks[source, pl.ds(5 * ROWS, SEG_ROWS), :].astype(F32)[0:1]
     second = jnp.sum(seg_sum, axis=1, keepdims=True)
     boundary = (GROUP - second).astype(jnp.int32)
-    position = lax.broadcasted_iota(jnp.int32, (1, GROUP), 1)
-    first = jnp.where(position >= boundary, boundary, 0)
+    boundary_ref[...] = jnp.broadcast_to(boundary, boundary_ref.shape)
+    vt_ref[...] = kv_ref[1].astype(F32).T.astype(BF16)
     stat_ref[...] = jnp.zeros_like(stat_ref)
-    stat_ref[3:4, :] = first.astype(F32)
-    vt_ref[...] = kv_ref[1].astype(F32).T.astype(BF16)
-    for qb in range(GROUP // QB):
-        keys = (qb + 1) * QB
-        rows = pl.ds(qb * QB, QB)
-        for head in range(HEADS):
-            scores = transposed_scores(
-                kv_ref[0, pl.ds(0, keys), :], q_ref[head, rows, :], first[:, qb * QB : keys], qb
-            )
-            peak = jnp.max(scores, axis=0, keepdims=True)
-            weights = jnp.exp2(scores - peak)
-            total = jnp.sum(weights, axis=0, keepdims=True)
-            stat_ref[head : head + 1, rows] = peak + jnp.log2(total)
-            mixed = dot_nn(vt_ref[:, pl.ds(0, keys)], weights.astype(BF16)) / total
-            att_ref[rows, pl.ds(head * HD, HD)] = mixed.T.astype(BF16)
-
-
-def backward_kernel(meta, q_ref, kv_ref, stat_ref, own_ref, *refs):
-    high_ref, low_ref, out, kt_ref, g_ref, gq_ref, gk_ref, gv_ref = refs
-    half = GROUP // 2
-    for received, first in ((low_ref, 0), (high_ref, half)):
-        total = own_ref[pl.ds(first, half), :] + received[...].astype(F32)
-        for head in range(HEADS):
-            g_ref[head, pl.ds(first, half), :] = total[:, head * HD : (head + 1) * HD].astype(BF16)
+    widen(boundary, q_ref, kv_ref, q_wide, k_wide)
+    forward_rows((0, 1), q_wide, k_wide, vt_ref, att_ref, stat_ref)
+
+
+def forward_high_kernel(meta, q_ref, kv_ref, vt_ref, boundary_ref, att_ref, stat_ref, q_wide, k_wide):
+    stat_ref[...] = jnp.zeros_like(stat_ref)
+    widen(boundary_ref[0:1, 0:1], q_ref, kv_ref, q_wide, k_wide)
+    forward_rows((2, 3), q_wide, k_wide, vt_ref, att_ref, stat_ref)
+
+
+def backward_kernel(meta, q_ref, kv_ref, boundary_ref, stat_low, stat_high, own_ref, *refs):
+    part_ref, out, kt_ref, g_ref, gq_ref, gk_ref, gv_ref, q_wide, k_wide = refs
+    total = own_ref[...] + part_ref[...].astype(F32)
+    for head in range(HEADS):
+        g_ref[head] = total[:, head * HD : (head + 1) * HD].astype(BF16)
     kt_ref[...] = kv_ref[0].astype(F32).T.astype(BF16)
     gk_ref[...] = jnp.zeros_like(gk_ref)
     gv_ref[...] = jnp.zeros_like(gv_ref)
-    first = stat_ref[3:4, :].astype(jnp.int32)
+    widen(boundary_ref[0:1, 0:1], q_ref, kv_ref, q_wide, k_wide)
     for qb in range(GROUP // QB):
-        keys = (qb + 1) * QB
         rows = pl.ds(qb * QB, QB)
-        span = pl.ds(0, keys)
+        stat_ref, stat_rows = (stat_low, rows) if qb < 2 else (stat_high, pl.ds(qb * QB - GROUP // 2, QB))
         for head in range(HEADS):
             q = q_ref[head, rows, :]
             g = g_ref[head, rows, :]
-            scores = transposed_scores(kv_ref[0, span, :], q, first[:, qb * QB : keys], qb)
-            prob = jnp.exp2(scores - stat_ref[head : head + 1, rows])
-            grad_prob = dot_nt(kv_ref[1, span, :], g)
-            delta = jnp.sum(prob * grad_prob, axis=0, keepdims=True)
-            grad_logit = (prob * (grad_prob - delta)).astype(BF16)
-            gv_ref[span, :] += dot_nn(prob.astype(BF16), g)
-            gk_ref[span, :] += dot_nn(grad_logit, q)
-            gq = dot_nn(kt_ref[:, span], grad_logit) * SCALE
-            gq_ref[head, rows, :] = gq.T.astype(BF16)
+            parts, delta = [], 0.0
+            for lo, hi, diagonal in key_parts(qb):
+                span = pl.ds(lo, hi - lo)
+                scores = transposed_scores(k_wide[span, :], q_wide[head, rows, :], diagonal)
+                prob = jnp.exp2(scores - stat_ref[head : head + 1, stat_rows])
+                grad_prob = dot_nt(kv_ref[1, span, :], g)
+                delta = delta + jnp.sum(prob * grad_prob, axis=0, keepdims=True)
+                gv_ref[span, :] += dot_nn(prob.astype(BF16), g)
+                parts.append((span, prob, grad_prob))
+            gq = 0.0
+            for span, prob, grad_prob in parts:
+                grad_logit = (prob * (grad_prob - delta)).astype(BF16)
+                gk_ref[span, :] += dot_nn(grad_logit, q)
+                gq = gq + dot_nn(kt_ref[:, span], grad_logit)
+            gq_ref[head, rows, :] = (gq * SCALE).T.astype(BF16)
     for to in range(8):
         rows = pl.ds(to * ROWS, ROWS)
         for head in range(HEADS):
@@ -212,49 +265,62 @@
 
 
 def grad_kernel(meta, *refs):
-    grads, w_ref, high_ref, low_ref, own_ref, held, wide = refs[:5], *refs[5:]
+    grads, w_ref, send_ref, own_ref, held, wide = refs[:5], *refs[5:]
     x, h = meta[0], meta[1]
-    gather_columns(x, grads, held)
-    for shift in range(NX):
-        slot = lax.rem(x - shift + NX, NX)
-        place_weight(meta, w_ref, 1 - h, slot, wide, 0, shift * FEAT)
-        place_weight(meta, w_ref, h, slot, wide, FEAT, shift * FEAT)
-
-    for send, first in ((high_ref, GROUP // 2), (low_ref, 0)):
-
-        @pl.loop(0, GROUP // QB // 2)
-        def _(i):
-            row = pl.multiple_of(i * QB, QB)
-            rows = pl.ds(row + first, QB)
-            total = dot_nt(held[rows, :], wide[...])
-            send[pl.ds(row, QB), :] = total[:, :FEAT].astype(BF16)
-            own_ref[rows, :] = total[:, FEAT:]
-
-
-def out_kernel(meta, here_ref, there_ref, w_ref, out, wide):
+    step = pl.program_id(0)
+
+    @pl.when(step == 0)
+    def _():
+        for shift in range(NX):
+            slot = lax.rem(x - shift + NX, NX)
+            place_weight(meta, w_ref, 1 - h, slot, wide, 0, shift * FEAT)
+            place_weight(meta, w_ref, h, slot, wide, FEAT, shift * FEAT)
+
+    own, right, left, low, high = grads
+    for shift, part in ((0, own), (1, right), (3, left)):
+        held[:, pl.ds(shift * FEAT, FEAT)] = part[...]
+    far = pl.ds(2 * FEAT, FEAT)
+    is_high = step >= 2
+
+    @pl.when(is_high)
+    def _():
+        held[:, far] = high[...]
+
+    @pl.when(jnp.logical_not(is_high))
+    def _():
+        held[:, far] = low[...]
+
+    total = dot_nt(held[...], wide[...])
+    send_ref[...] = total[:, :FEAT].astype(BF16)
+    own_ref[...] = total[:, FEAT:]
+
+
+def out_kernel(meta, here_low, here_high, there_low, there_high, w_ref, out, wide):
     h = meta[1]
+    is_low = pl.program_id(0) < 2
+
+    @pl.when(pl.program_id(0) == 0)
+    def _():
+        for column in range(NX):
+            place_weight(meta, w_ref, h, column, wide, 0, column * FEAT)
+            place_weight(meta, w_ref, 1 - h, column, wide, FEAT, column * FEAT)
+
+    here = jnp.where(is_low, here_low[...], here_high[...])
+    there = jnp.where(is_low, there_low[...], there_high[...])
+    total = dot_nn(here, wide[pl.ds(0, FEAT), :]) + dot_nn(there, wide[pl.ds(FEAT, FEAT), :])
     for column in range(NX):
-        place_weight(meta, w_ref, h, column, wide, 0, column * FEAT)
-        place_weight(meta, w_ref, 1 - h, column, wide, FEAT, column * FEAT)
-
-    @pl.loop(0, GROUP // QB)
-    def _(i):
-        rows = pl.ds(pl.multiple_of(i * QB, QB), QB)
-        total = dot_nn(here_ref[rows, :], wide[pl.ds(0, FEAT), :]) + dot_nn(
-            there_ref[rows, :], wide[pl.ds(FEAT, FEAT), :]
-        )
-        for column in range(NX):
-            out[column, rows, :] = total[:, column * FEAT : (column + 1) * FEAT].astype(BF16)
+        out[column] = total[:, column * FEAT : (column + 1) * FEAT].astype(BF16)
 
 
 def grad_weight_kernel(meta, *refs):
-    att, grads, (keep_ref, *sends, held, total) = refs[:2], refs[2:7], refs[7:]
+    att, grads, (keep_ref, *sends, held, total) = refs[:4], refs[4:9], refs[9:]
+    half = GROUP // 2
     x, h, core = meta[0], meta[1], meta[3]
     gather_columns(x, grads, held)
     for which in range(2):
         part = h if which == 0 else 1 - h
-        turned = att[which][...].T
-        total[...] = dot_nn(turned, held[...])
+        low, high = att[2 * which][...].T, att[2 * which + 1][...].T
+        total[...] = dot_nn(low, held[pl.ds(0, half), :]) + dot_nn(high, held[pl.ds(half, half), :])
         for shift in range(NX):
             slot = lax.rem(x - shift + NX, NX)
             cols = pl.ds(shift * FEAT, FEAT)
@@ -301,6 +367,18 @@
     copy.wait()
 
 
+def halves_kernel(meta, left_ref, right_ref, low_ref, high_ref, sems):
+    half = low_ref.shape[0]
+    copies = [
+        pltpu.make_async_copy(left_ref.at[pl.ds(0, half), :], low_ref, sems.at[0]),
+        pltpu.make_async_copy(right_ref.at[pl.ds(half, half), :], high_ref, sems.at[1]),
+    ]
+    for copy in copies:
+        copy.start()
+    for copy in copies:
+        copy.wait()
+
+
 def per_device(queries, key_heads, value_heads, segment_ids, out_weight, grad_out):
     dp = lax.axis_index("dp")
     cp = lax.axis_index("cp")
@@ -338,47 +416,63 @@
     weight = lax.all_gather(
         turned, "dp", axis=0, axis_index_groups=[list(range(8)), list(range(8, 16))]
     ).reshape(NX, 2, 2, 192, FEAT)
-    low = lax.ppermute(from_left[:half], "cp", cp_pairs(1, 0))
-    high = lax.ppermute(from_right[half:], "cp", cp_pairs(3, 0))
-    grads_out = (grad_out, from_left, from_right, low, high)
-
-    attended, q_all, kv_all, stats = call(
-        forward_kernel,
-        "forward",
+
+    wide_scratch = [pltpu.VMEM((HEADS, GROUP, 2 * HD), BF16), pltpu.VMEM((GROUP, 2 * HD), BF16)]
+    att_low, q_all, kv_all, v_turned, boundary, stat_low = call(
+        forward_low_kernel,
+        "forward_low",
         meta,
         (blocks,),
         [
-            shaped((GROUP, FEAT), BF16),
+            shaped((half, FEAT), BF16),
             shaped((HEADS, GROUP, HD), BF16),
             shaped((2, GROUP, HD), BF16),
-            shaped((8, GROUP), F32),
+            shaped((HD, GROUP), BF16),
+            shaped((8, 128), jnp.int32),
+            shaped((8, half), F32),
         ],
-        [pltpu.VMEM((HD, GROUP), BF16)],
+        wide_scratch,
+        span=0,
+    )
+    there_low = lax.ppermute(att_low, "cp", cp_pairs(0, 1))
+    att_high, stat_high = call(
+        forward_high_kernel,
+        "forward_high",
+        meta,
+        (q_all, kv_all, v_turned, boundary),
+        [shaped((half, FEAT), BF16), shaped((8, half), F32)],
+        wide_scratch,
         span=100,
     )
-    att = (attended, lax.ppermute(attended, "cp", cp_pairs(0, 1)))
-
-    send_high, send_low, grad_own = call(
-        grad_kernel,
-        "grad_attended",
-        meta,
-        (*grads_out, weight),
-        [shaped((half, FEAT), BF16)] * 2 + [shaped((GROUP, FEAT), F32)],
-        [pltpu.VMEM((GROUP, NX * FEAT), BF16), pltpu.VMEM((2 * FEAT, NX * FEAT), BF16)],
-        after=(attended,),
-    )
-    part_high = lax.ppermute(send_high, "cp", cp_pairs(0, 1))
-    part_low = lax.ppermute(send_low, "cp", cp_pairs(0, 1))
-
+    there_high = lax.ppermute(att_high, "cp", cp_pairs(0, 1))
+
+    left_low, right_high = call(
+        halves_kernel,
+        "halves",
+        meta,
+        (from_left, from_right),
+        [shaped((half, FEAT), BF16)] * 2,
+        [pltpu.SemaphoreType.DMA((2,))],
+        after=(att_high,),
+        hbm=(0, 1),
+    )
+    low = lax.ppermute(left_low, "cp", cp_pairs(1, 0))
+    high = lax.ppermute(right_high, "cp", cp_pairs(3, 0))
+    grads_out = (grad_out, from_left, from_right, low, high)
+
+    weight_block = whole_block((NX, 2, 2, 192, FEAT))
     (out_all,) = call(
         out_kernel,
         "out",
         meta,
-        (*att, weight),
+        (att_low, att_high, there_low, there_high, weight),
         [shaped((NX, GROUP, FEAT), BF16)],
         [pltpu.VMEM((2 * FEAT, NX * FEAT), BF16)],
-        after=(grad_own,),
         span=20,
+        vmem=61,
+        grid=(4,),
+        blocks=[row_block(QB, FEAT, lambda i: i % 2)] * 4 + [weight_block],
+        out_blocks=[pl.BlockSpec((NX, QB, FEAT), lambda i: (0, i, 0))],
     )
     output = lax.psum_scatter(
         out_all,
@@ -387,14 +481,30 @@
         axis_index_groups=[[x * 2 + h for x in range(NX)] for h in range(2)],
     )
 
+    grad_send, grad_own = call(
+        grad_kernel,
+        "grad_attended",
+        meta,
+        (*grads_out, weight),
+        [shaped((GROUP, FEAT), BF16), shaped((GROUP, FEAT), F32)],
+        [pltpu.VMEM((QB, NX * FEAT), BF16), pltpu.VMEM((2 * FEAT, NX * FEAT), BF16)],
+        after=(out_all,),
+        vmem=61,
+        grid=(4,),
+        blocks=[row_block(QB, FEAT, lambda i: i)] * 3
+        + [row_block(QB, FEAT, lambda i: lax.min(i, 1)), row_block(QB, FEAT, lambda i: lax.max(i - 2, 0)), weight_block],
+        out_blocks=[row_block(QB, FEAT, lambda i: i)] * 2,
+    )
+    grad_part = lax.ppermute(grad_send, "cp", cp_pairs(0, 1))
+
     keep, *sends = call(
         grad_weight_kernel,
         "grad_weight",
         meta,
-        (*att, *grads_out),
+        (att_low, att_high, there_low, there_high, *grads_out),
         [shaped((2, NX, 192, FEAT), F32)] + [shaped((NX, 96, FEAT), BF16)] * 4,
         [pltpu.VMEM((GROUP, NX * FEAT), BF16), pltpu.VMEM((FEAT, NX * FEAT), F32)],
-        after=(out_all, part_high),
+        after=(grad_own,),
         span=80,
     )
     core_parts = [lax.ppermute(p, "dp", core_pairs()) for p in sends]
@@ -405,7 +515,6 @@
         meta,
         (keep, *core_parts),
         [shaped((2, 192, FEAT), F32)] + [shaped((2, 192, FEAT), BF16)] * 3,
-        after=(part_low,),
     )
     z_parts = [lax.ppermute(p, "dp", z_pairs(dz)) for dz, p in zip((1, 2, 3), z_sends)]
 
@@ -413,7 +522,7 @@
         backward_kernel,
         "backward",
         meta,
-        (q_all, kv_all, stats, grad_own, part_high, part_low),
+        (q_all, kv_all, boundary, stat_low, stat_high, grad_own, grad_part),
         [shaped((8, 5 * ROWS, ROWS), BF16)],
         [
             pltpu.VMEM((HD, GROUP), BF16),
@@ -421,7 +530,8 @@
             pltpu.VMEM((HEADS, GROUP, HD), BF16),
             pltpu.VMEM((GROUP, HD), F32),
             pltpu.VMEM((GROUP, HD), F32),
-        ],
+        ]
+        + wide_scratch,
         after=(z_own,),
     )
     returned = lax.all_to_all(grads, "cp", 0, 0)

time: 170 us -> 158 us (0.929)
  waiting for transfers between devices: 55.6 us -> 46.3 us
  starting transfers between devices: 47.5 us -> 44.9 us
    ppermute x2, waiting for transfers between devices: 26.9 us -> 20.4 us  [per_device(): lax.ppermute(p, both, x_to_z_pairs(dy))]
    ppermute x1, waiting for transfers between devices: 5.88 us -> 0.01 us  [per_device(): from_right = lax.ppermute(grad_out, 'cp', cp_pairs(3, 0))]
    ppermute x2, waiting for transfers between devices: 1.4 us -> 7 us  [per_device(): turned = [lax.ppermute(out_weight, both, x_to_z_pairs(dy)) for dy in (0, 1)]]
    ppermute x1, waiting for transfers between devices: 0.01 us -> 4.51 us  [per_device(): from_left = lax.ppermute(grad_out, 'cp', cp_pairs(1, 0))]
    all_to_all x1, waiting for transfers between devices: 10.1 us -> 5.74 us  [per_device(): blocks = lax.all_to_all(packed, 'cp', 0, 0)]
    ppermute x1, starting transfers between devices: 3.22 us -> 0.07 us  [per_device(): from_left = lax.ppermute(grad_out, 'cp', cp_pairs(1, 0))]
    ppermute x5, waiting for transfers between devices: 9.48 us -> 6.83 us  [the longest x1 2.68 us: per_device(): grad_part = lax.ppermute(grad_send, 'cp', cp_pairs(0, 1))]
    ppermute x1, starting transfers between devices: 0.07 us -> 2.01 us  [per_device(): from_right = lax.ppermute(grad_out, 'cp', cp_pairs(3, 0))]
  transfers between devices with their start and end apart: 22 -> 22, of which waited for: 11 -> 13; matrix products, arithmetic and copies ran while one was open for 0% -> 0% of each run, Pallas kernels for 28% -> 30%
where the time goes in v3:
time: 158 us; the launch traced here: 157 us
  Pallas kernels  46.8 us (30%)
  waiting for transfers between devices  46.3 us (29%)
  starting transfers between devices  44.9 us (28%)
  between operations  14.3 us (9%)
  local copies, waits for them, and re-layouts  4.65 us (3%)
    pallas_call x13, Pallas kernels, call(): pl.pallas_call(body, name=name, out_shape=tuple(outs), grid=grid, in_spec...  46.8 us
    ppermute x2, waiting for transfers between devices, per_device(): lax.ppermute(p, both, x_to_z_pairs(dy))  20.4 us
    ppermute x2, starting transfers between devices, per_device(): turned = [lax.ppermute(out_weight, both, x_to_z_pairs(dy)) for dy in (0, 1)]  8.05 us
    all_to_all x1, starting transfers between devices, per_device(): blocks = lax.all_to_all(packed, 'cp', 0, 0)  7.91 us
    ppermute x2, starting transfers between devices, per_device(): lax.ppermute(p, both, x_to_z_pairs(dy))  7.51 us
    ppermute x2, waiting for transfers between devices, per_device(): turned = [lax.ppermute(out_weight, both, x_to_z_pairs(dy)) for dy in (0, 1)]  7 us
    all_to_all x1, starting transfers between devices, per_device(): returned = lax.all_to_all(grads, 'cp', 0, 0)  6.91 us
    all_to_all x1, waiting for transfers between devices, per_device(): blocks = lax.all_to_all(packed, 'cp', 0, 0)  5.74 us
  transfers between devices with their start and end apart: 22, of which 13 were waited for; matrix products, arithmetic and copies ran while one was open for 0% of the time, Pallas kernels for 30%

profile of v3, /device:TPU:22, one launch (start us, length us, event | category | flops | bytes accessed | tf_op | source)
XLA Modules:
  0.0 157.0 jit_solution(6550511108012398649)
XLA Ops:
  7.2 5.9 %collective-permute-start.2 = (bf16[192,384]{1,0:T(8,128)(2,1)}, bf16[192,384]{1,0:T(8,128)(2,1)S(1)}, u32[]{:S(2)}, u32[]{:S(2)}) collective-permute-start(bf16[192,384]{1,0:T(8,128)(2,1)} %param.10), channel_id=1, source_target_pairs={{0,0},{1,1},{2,16},{3,17},{4,32},{5,33},{6,48},{7,49},{8,8},{9,9},... | collective-permute-start | bytes 442376 | tf_op jit(solution)/shard_map/ppermute | solution.py:391
  13.0 2.2 %collective-permute-start.3 = (bf16[192,384]{1,0:T(8,128)(2,1)}, bf16[192,384]{1,0:T(8,128)(2,1)S(1)}, u32[]{:S(2)}, u32[]{:S(2)}) collective-permute-start(bf16[192,384]{1,0:T(8,128)(2,1)} %param.10), channel_id=1, source_target_pairs={{0,64},{1,65},{2,80},{3,81},{4,96},{5,97},{6,112},{7,113},{8,72},{... | collective-permute-start | bytes 442376 | tf_op jit(solution)/shard_map/ppermute | solution.py:391
  15.9 3.4 %pack.1.refs_3_ = bf16[8,656,128]{2,1,0:T(8,128)(2,1)} custom-call(s32[5]{0:T(128)} %stack.23.meta_ref, bf16[128,3072]{1,0:T(8,128)(2,1)} %refs_0_.1, bf16[128,512]{1,0:T(8,128)(2,1)} %refs_1_.1, bf16[128,512]{1,0:T(8,128)(2,1)} %refs_2_.2, s32[1,128]{1,0:T(1,128)} %refs_3_.1), custom_call_target="tpu_custom_call" | custom-call | tf_op jit(solution)/shard_map/pack/pallas_call | solution.py:78
  19.3 7.9 %all-to-all-start = ((bf16[8,656,128]{2,1,0:T(8,128)(2,1)}), bf16[8,656,128]{2,1,0:T(8,128)(2,1)S(1)}, u32[]{:S(2)}, u32[]{:S(2)}) async-start(bf16[8,656,128]{2,1,0:T(8,128)(2,1)} %pack.1.refs_3_), calls=%async_computation | async-start | bytes 2686976 | tf_op jit(solution)/shard_map/all_to_all | solution.py:402
  28.5 5.8 %collective-permute-done.3.refs_1_ = bf16[192,384]{1,0:T(8,128)(2,1)S(1)} collective-permute-done((bf16[192,384]{1,0:T(8,128)(2,1)}, bf16[192,384]{1,0:T(8,128)(2,1)S(1)}, u32[]{:S(2)}, u32[]{:S(2)}) %collective-permute-start.3) | collective-permute-done | bytes 147488 | tf_op jit(solution)/shard_map/ppermute | solution.py:391
  35.4 1.6 %turned.1 = (bf16[2,192,384]{2,1,0:T(8,128)(2,1)}, bf16[1024,384]{1,0:T(8,128)(2,1)}) custom-call(s32[5]{0:T(128)S(1)} %copy-done.11, bf16[192,384]{1,0:T(8,128)(2,1)S(1)} %collective-permute-done.2.refs_0_, bf16[192,384]{1,0:T(8,128)(2,1)S(1)} %collective-permute-done.3.refs_1_, bf16[1024,384]{1,0:T(8,128)(2,1)S(1)} %copy-done.13, ...), custom_call_target="tpu_custom_call" | custom-call | flops 20000000000 | tf_op jit(solution)/shard_map/turned/pallas_call | solution.py:78
  37.1 2.0 %collective-permute-start.5 = (bf16[1024,384]{1,0:T(8,128)(2,1)}, bf16[1024,384]{1,0:T(8,128)(2,1)S(1)}, u32[]{:S(2)}, u32[]{:S(2)}) collective-permute-start(bf16[1024,384]{1,0:T(8,128)(2,1)} %get-tuple-element.42.refs_0_.refs_4_), channel_id=1, source_target_pairs={{0,6},{1,7},{2,0},{3,1},{4,2},{5,3},{6,4},{7,5},{8,14},{9,15},{10,... | collective-permute-start | bytes 2359304 | tf_op jit(solution)/shard_map/ppermute | solution.py:415
  39.2 5.7 %all-to-all-done.refs_0_ = bf16[8,656,128]{2,1,0:T(8,128)(2,1)S(1)} async-done(((bf16[8,656,128]{2,1,0:T(8,128)(2,1)}), bf16[8,656,128]{2,1,0:T(8,128)(2,1)S(1)}, u32[]{:S(2)}, u32[]{:S(2)}) %all-to-all-start) | async-done | bytes 1343520 | tf_op jit(solution)/shard_map/all_to_all | solution.py:402
  44.9 2.4 %forward_low.1 = (bf16[512,384]{1,0:T(8,128)(2,1)S(1)}, bf16[3,1024,128]{2,1,0:T(8,128)(2,1)S(1)}, bf16[2,1024,128]{2,1,0:T(8,128)(2,1)S(1)}, bf16[128,1024]{1,0...) custom-call(s32[5]{0:T(128)S(1)} %copy-done.11, bf16[8,656,128]{2,1,0:T(8,128)(2,1)S(1)} %all-to-all-done.refs_0_), custom_call_target="tpu_custom_call" | custom-call | tf_op jit(solution)/shard_map/forward_low/pallas_call | solution.py:78
  48.5 3.6 %forward_high.1 = (bf16[512,384]{1,0:T(8,128)(2,1)S(1)}, f32[8,512]{1,0:T(8,128)S(1)}) custom-call(s32[5]{0:T(128)S(1)} %copy-done.11, bf16[3,1024,128]{2,1,0:T(8,128)(2,1)S(1)} %get-tuple-element.34.refs_0_, bf16[2,1024,128]{2,1,0:T(8,128)(2,1)S(1)} %get-tuple-element.35.refs_1_, bf16[128,1024]{1,0:T(8,128)(2,1)S(1)} %get-tuple-element.36.refs_2_, ...), custom_call_target="tpu_custom_call" | custom-call | flops 99999997952 | tf_op jit(solution)/shard_map/forward_high/pallas_call | solution.py:78
  52.1 2.5 %collective-permute-start.1 = (bf16[512,384]{1,0:T(8,128)(2,1)S(1)}, bf16[512,384]{1,0:T(8,128)(2,1)}, u32[]{:S(2)}, u32[]{:S(2)}) collective-permute-start(bf16[512,384]{1,0:T(8,128)(2,1)S(1)} %get-tuple-element.38.refs_1_.refs_2_), channel_id=1, source_target_pairs={{0,1},{1,0},{2,3},{3,2},{4,5},{5,4},{6,7},{7,6},{8,9},{9,8},{10,11... | collective-permute-start | bytes 1179656 | tf_op jit(solution)/shard_map/ppermute | solution.py:447
  54.7 4.5 %collective-permute-done.4.refs_0_.refs_1_.refs_5_ = bf16[1024,384]{1,0:T(8,128)(2,1)S(1)} collective-permute-done((bf16[1024,384]{1,0:T(8,128)(2,1)}, bf16[1024,384]{1,0:T(8,128)(2,1)S(1)}, u32[]{:S(2)}, u32[]{:S(2)}) %collective-permute-start.4) | collective-permute-done | bytes 786464 | tf_op jit(solution)/shard_map/ppermute | solution.py:414
  59.2 1.9 %halves.1 = (bf16[512,384]{1,0:T(8,128)(2,1)}, bf16[512,384]{1,0:T(8,128)(2,1)}) custom-call(s32[5]{0:T(128)S(1)} %copy-done.11, bf16[1024,384]{1,0:T(8,128)(2,1)S(1)} %collective-permute-done.4.refs_0_.refs_1_.refs_5_, bf16[1024,384]{1,0:T(8,128)(2,1)S(1)} %collective-permute-done.5.refs_1_.refs_2_.refs_6_, ...), custom_call_target="tpu_custom_call" | custom-call | tf_op jit(solution)/shard_map/halves/pallas_call | solution.py:78
  61.1 2.4 %collective-permute-start.6 = (bf16[512,384]{1,0:T(8,128)(2,1)}, bf16[512,384]{1,0:T(8,128)(2,1)}, u32[]{:S(2)}, u32[]{:S(2)}) collective-permute-start(bf16[512,384]{1,0:T(8,128)(2,1)} %get-tuple-element.43), channel_id=1, source_target_pairs={{0,2},{1,3},{2,4},{3,5},{4,6},{5,7},{6,0},{7,1},{8,10},{9,11},{10,... | collective-permute-start | bytes 1179656 | tf_op jit(solution)/shard_map/ppermute | solution.py:459
  63.5 1.7 %collective-permute-done.1.refs_3_ = bf16[512,384]{1,0:T(8,128)(2,1)} collective-permute-done((bf16[512,384]{1,0:T(8,128)(2,1)S(1)}, bf16[512,384]{1,0:T(8,128)(2,1)}, u32[]{:S(2)}, u32[]{:S(2)}) %collective-permute-start.1) | collective-permute-done | bytes 393248 | tf_op jit(solution)/shard_map/ppermute | solution.py:447
  65.3 7.8 %out.1.refs_6_ = bf16[4,1024,384]{2,1,0:T(8,128)(2,1)} custom-call(s32[5]{0:T(128)} %stack.23.meta_ref, bf16[512,384]{1,0:T(8,128)(2,1)} %copy-done.14, bf16[512,384]{1,0:T(8,128)(2,1)} %copy-done.9, bf16[512,384]{1,0:T(8,128)(2,1)} %copy-done.16, bf16[512,384]{1,0:T(8,128)(2,1)} %collective-permute-done.1.refs_3_, bf16[4,2,2,192,384]{4,3,2,1,0:T(8,128)(2,1)} %bitcast.7), custom_call_target="tpu_custom_call" | custom-call | flops 20000000000 | tf_op jit(solution)/shard_map/out/pallas_call | solution.py:78
  73.1 2.4 %collective-permute-done.7.refs_4_.refs_8_ = bf16[512,384]{1,0:T(8,128)(2,1)} collective-permute-done((bf16[512,384]{1,0:T(8,128)(2,1)}, bf16[512,384]{1,0:T(8,128)(2,1)}, u32[]{:S(2)}, u32[]{:S(2)}) %collective-permute-start.7) | collective-permute-done | bytes 393248 | tf_op jit(solution)/shard_map/ppermute | solution.py:460
  75.5 7.4 %grad_attended.1 = (bf16[1024,384]{1,0:T(8,128)(2,1)}, f32[1024,384]{1,0:T(8,128)}) custom-call(s32[5]{0:T(128)} %stack.23.meta_ref, bf16[1024,384]{1,0:T(8,128)(2,1)} %get-tuple-element.42.refs_0_.refs_4_, bf16[1024,384]{1,0:T(8,128)(2,1)} %copy-done.1, bf16[1024,384]{1,0:T(8,128)(2,1)} %copy-done.3, ...), custom_call_target="tpu_custom_call" | custom-call | tf_op jit(solution)/shard_map/grad_attended/pallas_call | solution.py:78
  83.0 1.8 %copy-done.5 = f32[1024,384]{1,0:T(8,128)S(1)} copy-done((f32[1024,384]{1,0:T(8,128)S(1)}, f32[1024,384]{1,0:T(8,128)}, u32[]{:S(2)}) %copy-start.5) | copy-done | bytes 1572888
  85.8 4.5 %grad_weight.1 = (f32[2,4,192,384]{3,2,1,0:T(8,128)S(1)}, bf16[4,96,384]{2,1,0:T(8,128)(2,1)S(1)}, bf16[4,96,384]{2,1,0:T(8,128)(2,1)S(1)}, bf16[4,96,384]{2,1,0:T(8,128)(2,1)S(1)}, bf16[4,96,384]{2,1,0:T(8,128)(2,1)S(1)}) custom-call(s32[5]{0:T(128)S(1)} %copy-done.12, bf16[512,384]{1,0:T(8,128)(2,1)S(1)} %copy-done.15, bf16[512,384]{1,0:T(8,128)(2,1)S(1)} %copy-done.10, ...), custom_call_target="tpu_custom_call" | custom-call | flops 80000000000 | tf_op jit(solution)/shard_map/grad_weight/pallas_call | solution.py:78
  93.3 1.6 z_sum.1
  94.8 1.6 collective-permute-start.13
  96.4 3.6 %collective-permute-start.14 = (bf16[2,192,384]{2,1,0:T(8,128)(2,1)}, bf16[2,192,384]{2,1,0:T(8,128)(2,1)}, u32[]{:S(2)}, u32[]{:S(2)}) collective-permute-start(bf16[2,192,384]{2,1,0:T(8,128)(2,1)} %get-tuple-element.57), channel_id=1, source_target_pairs={{0,32},{8,40},{16,48},{24,56},{32,0},{40,8},{48,16},{56,24},{64,96... | collective-permute-start | bytes 884744 | tf_op jit(solution)/shard_map/ppermute | solution.py:519
  100.0 2.7 %collective-permute-done.8.refs_6_ = bf16[1024,384]{1,0:T(8,128)(2,1)S(1)} collective-permute-done((bf16[1024,384]{1,0:T(8,128)(2,1)}, bf16[1024,384]{1,0:T(8,128)(2,1)S(1)}, u32[]{:S(2)}, u32[]{:S(2)}) %collective-permute-start.8) | collective-permute-done | bytes 786464 | tf_op jit(solution)/shard_map/ppermute | solution.py:498
  102.7 8.4 %backward.1.refs_4_ = bf16[8,640,128]{2,1,0:T(8,128)(2,1)} custom-call(s32[5]{0:T(128)S(1)} %copy-done.12, bf16[3,1024,128]{2,1,0:T(8,128)(2,1)S(1)} %copy-done.8, bf16[2,1024,128]{2,1,0:T(8,128)(2,1)S(1)} %get-tuple-element.35.refs_1_, s32[8,128]{1,0:T(8,128)S(1)} %get-tuple-element.37.refs_3_.refs_2_, f32[8,512]{1,0:T(8,128)S(1)} %get-tuple-element.40.refs_3_, ...), custom_call_target="tpu_custom_call" | custom-call | tf_op jit(solution)/shard_map/backward/pallas_call | solution.py:78
  111.1 6.9 %all-to-all-start.1 = ((bf16[8,640,128]{2,1,0:T(8,128)(2,1)}), bf16[8,640,128]{2,1,0:T(8,128)(2,1)S(1)}, u32[]{:S(2)}, u32[]{:S(2)}) async-start(bf16[8,640,128]{2,1,0:T(8,128)(2,1)} %backward.1.refs_4_), calls=%async_computation.2 | async-start | bytes 2621440 | tf_op jit(solution)/shard_map/all_to_all | solution.py:537
  119.2 4.3 %collective-permute-start.16 = (bf16[192,384]{1,0:T(8,128)(2,1)S(1)}, bf16[192,384]{1,0:T(8,128)(2,1)S(1)}, u32[]{:S(2)}, u32[]{:S(2)}) collective-permute-start(bf16[192,384]{1,0:T(8,128)(2,1)S(1)} %get-tuple-element.59), channel_id=1, source_target_pairs={{0,0},{1,1},{2,16},{3,17},{4,32},{5,33},{6,48},{7,49},{8,8},{9,9},... | collective-permute-start | bytes 442376 | tf_op jit(solution)/shard_map/ppermute | solution.py:548
  123.5 3.2 %collective-permute-start.17 = (bf16[192,384]{1,0:T(8,128)(2,1)S(1)}, bf16[192,384]{1,0:T(8,128)(2,1)S(1)}, u32[]{:S(2)}, u32[]{:S(2)}) collective-permute-start(bf16[192,384]{1,0:T(8,128)(2,1)S(1)} %get-tuple-element.60), channel_id=1, source_target_pairs={{0,64},{1,65},{2,80},{3,81},{4,96},{5,97},{6,112},{7,113},{8,72},{... | collective-permute-start | bytes 442376 | tf_op jit(solution)/shard_map/ppermute | solution.py:548
  126.8 18.8 %collective-permute-done.16.refs_0_ = bf16[192,384]{1,0:T(8,128)(2,1)S(1)} collective-permute-done((bf16[192,384]{1,0:T(8,128)(2,1)S(1)}, bf16[192,384]{1,0:T(8,128)(2,1)S(1)}, u32[]{:S(2)}, u32[]{:S(2)}) %collective-permute-start.16) | collective-permute-done | bytes 147488 | tf_op jit(solution)/shard_map/ppermute | solution.py:548
  145.6 1.6 %collective-permute-done.17.refs_1_ = bf16[192,384]{1,0:T(8,128)(2,1)S(1)} collective-permute-done((bf16[192,384]{1,0:T(8,128)(2,1)S(1)}, bf16[192,384]{1,0:T(8,128)(2,1)S(1)}, u32[]{:S(2)}, u32[]{:S(2)}) %collective-permute-start.17) | collective-permute-done | bytes 147488 | tf_op jit(solution)/shard_map/ppermute | solution.py:548
  147.1 1.3 grad_weight_total.1
  148.4 1.7 %unpack.1 = (bf16[128,3072]{1,0:T(8,128)(2,1)}, bf16[128,512]{1,0:T(8,128)(2,1)}, bf16[128,512]{1,0:T(8,128)(2,1)}) custom-call(s32[5]{0:T(128)S(1)} %copy-done.12, bf16[8,640,128]{2,1,0:T(8,128)(2,1)S(1)} %all-to-all-done.1.refs_0_), custom_call_target="tpu_custom_call" | custom-call | tf_op jit(solution)/shard_map/unpack/pallas_call | solution.py:78
  (64 shorter events, 9.5 us)
Async XLA Ops:
  7.2 21.3 %collective-permute-start.2 = (bf16[192,384]{1,0:T(8,128)(2,1)}, bf16[192,384]{1,0:T(8,128)(2,1)S(1)}, u32[]{:S(2)}, u32[]{:S(2)}) collective-permute-start(bf16[192,384]{1,0:T(8,128)(2,1)} %param.10), channel_id=1, source_target_pairs={{0,0},{1,1},{2,16},{3,17},{4,32},{5,33},{6,48},{7,49},{8,8},{9,9},... | collective-permute-start | bytes 442376 | tf_op jit(solution)/shard_map/ppermute | solution.py:391
  13.0 21.2 %collective-permute-start.3 = (bf16[192,384]{1,0:T(8,128)(2,1)}, bf16[192,384]{1,0:T(8,128)(2,1)S(1)}, u32[]{:S(2)}, u32[]{:S(2)}) collective-permute-start(bf16[192,384]{1,0:T(8,128)(2,1)} %param.10), channel_id=1, source_target_pairs={{0,64},{1,65},{2,80},{3,81},{4,96},{5,97},{6,112},{7,113},{8,72},{... | collective-permute-start | bytes 442376 | tf_op jit(solution)/shard_map/ppermute | solution.py:391
  19.3 14.9 %copy-start = (bf16[8,656,128]{2,1,0:T(8,128)(2,1)S(1)}, bf16[8,656,128]{2,1,0:T(8,128)(2,1)}, u32[]{:S(2)}) copy-start(bf16[8,656,128]{2,1,0:T(8,128)(2,1)} %pack.1.refs_3_) | copy-start | bytes 4030468
  19.3 14.9 %copy-start.11 = (s32[5]{0:T(128)S(1)}, s32[5]{0:T(128)}, u32[]{:S(2)}) copy-start(s32[5]{0:T(128)} %stack.23.meta_ref) | copy-start | bytes 64
  19.3 25.6 %all-to-all-start = ((bf16[8,656,128]{2,1,0:T(8,128)(2,1)}), bf16[8,656,128]{2,1,0:T(8,128)(2,1)S(1)}, u32[]{:S(2)}, u32[]{:S(2)}) async-start(bf16[8,656,128]{2,1,0:T(8,128)(2,1)} %pack.1.refs_3_), calls=%async_computation | async-start | bytes 2686976 | tf_op jit(solution)/shard_map/all_to_all | solution.py:402
  27.3 38.0 %all-gather.3.cloned.1.call-start = ((), (), s32[]{:S(2)}) async-start(), calls=%async_computation.4 | async-start | bytes 2654208 | tf_op jit(solution)/shard_map/all_gather | solution.py:416
  37.0 22.2 %collective-permute-start.4 = (bf16[1024,384]{1,0:T(8,128)(2,1)}, bf16[1024,384]{1,0:T(8,128)(2,1)S(1)}, u32[]{:S(2)}, u32[]{:S(2)}) collective-permute-start(bf16[1024,384]{1,0:T(8,128)(2,1)} %get-tuple-element.42.refs_0_.refs_4_), channel_id=1, source_target_pairs={{0,2},{1,3},{2,4},{3,5},{4,6},{5,7},{6,0},{7,1},{8,10},{9,11},{10,... | collective-permute-start | bytes 2359304 | tf_op jit(solution)/shard_map/ppermute | solution.py:414
  37.1 22.1 %collective-permute-start.5 = (bf16[1024,384]{1,0:T(8,128)(2,1)}, bf16[1024,384]{1,0:T(8,128)(2,1)S(1)}, u32[]{:S(2)}, u32[]{:S(2)}) collective-permute-start(bf16[1024,384]{1,0:T(8,128)(2,1)} %get-tuple-element.42.refs_0_.refs_4_), channel_id=1, source_target_pairs={{0,6},{1,7},{2,0},{3,1},{4,2},{5,3},{6,4},{7,5},{8,14},{9,15},{10,... | collective-permute-start | bytes 2359304 | tf_op jit(solution)/shard_map/ppermute | solution.py:415
  39.1 111.0 %reduce-scatter.2.cloned.1.call-start = ((), (), s32[]{:S(2)}) async-start(), calls=%async_computation.3 | async-start | bytes 3932160 | tf_op jit(solution)/shard_map/reduce_scatter | solution.py:477
  47.4 16.1 %collective-permute-start = (bf16[512,384]{1,0:T(8,128)(2,1)S(1)}, bf16[512,384]{1,0:T(8,128)(2,1)S(1)}, u32[]{:S(2)}, u32[]{:S(2)}) collective-permute-start(bf16[512,384]{1,0:T(8,128)(2,1)S(1)} %get-tuple-element.33.refs_0_), channel_id=1, source_target_pairs={{0,1},{1,0},{2,3},{3,2},{4,5},{5,4},{6,7},{7,6},{8,9},{9,8},{10,11... | collective-permute-start | bytes 1179656 | tf_op jit(solution)/shard_map/ppermute | solution.py:437
  52.1 13.1 %copy-start.9 = (bf16[512,384]{1,0:T(8,128)(2,1)}, bf16[512,384]{1,0:T(8,128)(2,1)S(1)}, u32[]{:S(2)}) copy-start(bf16[512,384]{1,0:T(8,128)(2,1)S(1)} %get-tuple-element.38.refs_1_.refs_2_) | copy-start | bytes 1179652
  52.1 13.1 %collective-permute-start.1 = (bf16[512,384]{1,0:T(8,128)(2,1)S(1)}, bf16[512,384]{1,0:T(8,128)(2,1)}, u32[]{:S(2)}, u32[]{:S(2)}) collective-permute-start(bf16[512,384]{1,0:T(8,128)(2,1)S(1)} %get-tuple-element.38.refs_1_.refs_2_), channel_id=1, source_target_pairs={{0,1},{1,0},{2,3},{3,2},{4,5},{5,4},{6,7},{7,6},{8,9},{9,8},{10,11... | collective-permute-start | bytes 1179656 | tf_op jit(solution)/shard_map/ppermute | solution.py:447
  59.2 13.9 %copy-start.1 = (bf16[1024,384]{1,0:T(8,128)(2,1)}, bf16[1024,384]{1,0:T(8,128)(2,1)S(1)}, u32[]{:S(2)}) copy-start(bf16[1024,384]{1,0:T(8,128)(2,1)S(1)} %collective-permute-done.4.refs_0_.refs_1_.refs_5_) | copy-start | bytes 2359300
  59.2 13.9 %copy-start.3 = (bf16[1024,384]{1,0:T(8,128)(2,1)}, bf16[1024,384]{1,0:T(8,128)(2,1)S(1)}, u32[]{:S(2)}) copy-start(bf16[1024,384]{1,0:T(8,128)(2,1)S(1)} %collective-permute-done.5.refs_1_.refs_2_.refs_6_) | copy-start | bytes 2359300
  61.1 12.0 %collective-permute-start.6 = (bf16[512,384]{1,0:T(8,128)(2,1)}, bf16[512,384]{1,0:T(8,128)(2,1)}, u32[]{:S(2)}, u32[]{:S(2)}) collective-permute-start(bf16[512,384]{1,0:T(8,128)(2,1)} %get-tuple-element.43), channel_id=1, source_target_pairs={{0,2},{1,3},{2,4},{3,5},{4,6},{5,7},{6,0},{7,1},{8,10},{9,11},{10,... | collective-permute-start | bytes 1179656 | tf_op jit(solution)/shard_map/ppermute | solution.py:459
  63.5 12.0 %collective-permute-start.7 = (bf16[512,384]{1,0:T(8,128)(2,1)}, bf16[512,384]{1,0:T(8,128)(2,1)}, u32[]{:S(2)}, u32[]{:S(2)}) collective-permute-start(bf16[512,384]{1,0:T(8,128)(2,1)} %get-tuple-element.44), channel_id=1, source_target_pairs={{0,6},{1,7},{2,0},{3,1},{4,2},{5,3},{6,4},{7,5},{8,14},{9,15},{10,... | collective-permute-start | bytes 1179656 | tf_op jit(solution)/shard_map/ppermute | solution.py:460
  73.1 9.9 %copy-start.2 = (bf16[1024,384]{1,0:T(8,128)(2,1)S(1)}, bf16[1024,384]{1,0:T(8,128)(2,1)}, u32[]{:S(2)}) copy-start(bf16[1024,384]{1,0:T(8,128)(2,1)} %copy-done.1) | copy-start | bytes 2359300
  73.1 9.9 %copy-start.4 = (bf16[1024,384]{1,0:T(8,128)(2,1)S(1)}, bf16[1024,384]{1,0:T(8,128)(2,1)}, u32[]{:S(2)}) copy-start(bf16[1024,384]{1,0:T(8,128)(2,1)} %copy-done.3) | copy-start | bytes 2359300
  73.1 9.9 %copy-start.10 = (bf16[512,384]{1,0:T(8,128)(2,1)S(1)}, bf16[512,384]{1,0:T(8,128)(2,1)}, u32[]{:S(2)}) copy-start(bf16[512,384]{1,0:T(8,128)(2,1)} %copy-done.9) | copy-start | bytes 1179652
  73.1 9.9 %copy-start.12 = (s32[5]{0:T(128)S(1)}, s32[5]{0:T(128)}, u32[]{:S(2)}) copy-start(s32[5]{0:T(128)} %stack.23.meta_ref) | copy-start | bytes 64
  73.1 9.9 %copy-start.15 = (bf16[512,384]{1,0:T(8,128)(2,1)S(1)}, bf16[512,384]{1,0:T(8,128)(2,1)}, u32[]{:S(2)}) copy-start(bf16[512,384]{1,0:T(8,128)(2,1)} %copy-done.14) | copy-start | bytes 1179652
  83.0 19.7 %collective-permute-start.8 = (bf16[1024,384]{1,0:T(8,128)(2,1)}, bf16[1024,384]{1,0:T(8,128)(2,1)S(1)}, u32[]{:S(2)}, u32[]{:S(2)}) collective-permute-start(bf16[1024,384]{1,0:T(8,128)(2,1)} %get-tuple-element.46), channel_id=1, source_target_pairs={{0,1},{1,0},{2,3},{3,2},{4,5},{5,4},{6,7},{7,6},{8,9},{9,8},{10,11... | collective-permute-start | bytes 2359304 | tf_op jit(solution)/shard_map/ppermute | solution.py:498
  90.3 1.7 %collective-permute-start.9 = (bf16[4,96,384]{2,1,0:T(8,128)(2,1)S(1)}, bf16[4,96,384]{2,1,0:T(8,128)(2,1)S(1)}, u32[]{:S(2)}, u32[]{:S(2)}) collective-permute-start(bf16[4,96,384]{2,1,0:T(8,128)(2,1)S(1)} %get-tuple-element.48), channel_id=1, source_target_pairs={{0,8},{8,0},{16,24},{24,16},{32,40},{40,32},{48,56},{56,48},{64,72... | collective-permute-start | bytes 884744 | tf_op jit(solution)/shard_map/ppermute | solution.py:510
  90.4 2.0 %collective-permute-start.10 = (bf16[4,96,384]{2,1,0:T(8,128)(2,1)S(1)}, bf16[4,96,384]{2,1,0:T(8,128)(2,1)S(1)}, u32[]{:S(2)}, u32[]{:S(2)}) collective-permute-start(bf16[4,96,384]{2,1,0:T(8,128)(2,1)S(1)} %get-tuple-element.49), channel_id=1, source_target_pairs={{0,8},{8,0},{16,24},{24,16},{32,40},{40,32},{48,56},{56,48},{64,72... | collective-permute-start | bytes 884744 | tf_op jit(solution)/shard_map/ppermute | solution.py:510
  90.9 1.9 %collective-permute-start.11 = (bf16[4,96,384]{2,1,0:T(8,128)(2,1)S(1)}, bf16[4,96,384]{2,1,0:T(8,128)(2,1)S(1)}, u32[]{:S(2)}, u32[]{:S(2)}) collective-permute-start(bf16[4,96,384]{2,1,0:T(8,128)(2,1)S(1)} %get-tuple-element.50), channel_id=1, source_target_pairs={{0,8},{8,0},{16,24},{24,16},{32,40},{40,32},{48,56},{56,48},{64,72... | collective-permute-start | bytes 884744 | tf_op jit(solution)/shard_map/ppermute | solution.py:510
  91.2 2.1 %collective-permute-start.12 = (bf16[4,96,384]{2,1,0:T(8,128)(2,1)S(1)}, bf16[4,96,384]{2,1,0:T(8,128)(2,1)S(1)}, u32[]{:S(2)}, u32[]{:S(2)}) collective-permute-start(bf16[4,96,384]{2,1,0:T(8,128)(2,1)S(1)} %get-tuple-element.51), channel_id=1, source_target_pairs={{0,8},{8,0},{16,24},{24,16},{32,40},{40,32},{48,56},{56,48},{64,72... | collective-permute-start | bytes 884744 | tf_op jit(solution)/shard_map/ppermute | solution.py:510
  94.8 23.2 %collective-permute-start.13 = (bf16[2,192,384]{2,1,0:T(8,128)(2,1)}, bf16[2,192,384]{2,1,0:T(8,128)(2,1)S(1)}, u32[]{:S(2)}, u32[]{:S(2)}) collective-permute-start(bf16[2,192,384]{2,1,0:T(8,128)(2,1)} %get-tuple-element.56), channel_id=1, source_target_pairs={{0,16},{8,24},{16,32},{24,40},{32,48},{40,56},{48,0},{56,8},{64,80... | collective-permute-start | bytes 884744 | tf_op jit(solution)/shard_map/ppermute | solution.py:519
  96.4 21.6 %collective-permute-start.14 = (bf16[2,192,384]{2,1,0:T(8,128)(2,1)}, bf16[2,192,384]{2,1,0:T(8,128)(2,1)}, u32[]{:S(2)}, u32[]{:S(2)}) collective-permute-start(bf16[2,192,384]{2,1,0:T(8,128)(2,1)} %get-tuple-element.57), channel_id=1, source_target_pairs={{0,32},{8,40},{16,48},{24,56},{32,0},{40,8},{48,16},{56,24},{64,96... | collective-permute-start | bytes 884744 | tf_op jit(solution)/shard_map/ppermute | solution.py:519
  100.0 18.0 %collective-permute-start.15 = (bf16[2,192,384]{2,1,0:T(8,128)(2,1)S(1)}, bf16[2,192,384]{2,1,0:T(8,128)(2,1)}, u32[]{:S(2)}, u32[]{:S(2)}) collective-permute-start(bf16[2,192,384]{2,1,0:T(8,128)(2,1)S(1)} %get-tuple-element.58), channel_id=1, source_target_pairs={{0,48},{8,56},{16,0},{24,8},{32,16},{40,24},{48,32},{56,40},{64,11... | collective-permute-start | bytes 884744 | tf_op jit(solution)/shard_map/ppermute | solution.py:519
  111.1 37.3 %all-to-all-start.1 = ((bf16[8,640,128]{2,1,0:T(8,128)(2,1)}), bf16[8,640,128]{2,1,0:T(8,128)(2,1)S(1)}, u32[]{:S(2)}, u32[]{:S(2)}) async-start(bf16[8,640,128]{2,1,0:T(8,128)(2,1)} %backward.1.refs_4_), calls=%async_computation.2 | async-start | bytes 2621440 | tf_op jit(solution)/shard_map/all_to_all | solution.py:537
  119.2 26.3 %collective-permute-start.16 = (bf16[192,384]{1,0:T(8,128)(2,1)S(1)}, bf16[192,384]{1,0:T(8,128)(2,1)S(1)}, u32[]{:S(2)}, u32[]{:S(2)}) collective-permute-start(bf16[192,384]{1,0:T(8,128)(2,1)S(1)} %get-tuple-element.59), channel_id=1, source_target_pairs={{0,0},{1,1},{2,16},{3,17},{4,32},{5,33},{6,48},{7,49},{8,8},{9,9},... | collective-permute-start | bytes 442376 | tf_op jit(solution)/shard_map/ppermute | solution.py:548
  123.5 23.6 %collective-permute-start.17 = (bf16[192,384]{1,0:T(8,128)(2,1)S(1)}, bf16[192,384]{1,0:T(8,128)(2,1)S(1)}, u32[]{:S(2)}, u32[]{:S(2)}) collective-permute-start(bf16[192,384]{1,0:T(8,128)(2,1)S(1)} %get-tuple-element.60), channel_id=1, source_target_pairs={{0,64},{1,65},{2,80},{3,81},{4,96},{5,97},{6,112},{7,113},{8,72},{... | collective-permute-start | bytes 442376 | tf_op jit(solution)/shard_map/ppermute | solution.py:548
  (8 other events, 34.0 us)
Sparse Core Ops, SparseCore 0:
  39.2 24.2 all-gather.2
  73.2 37.9 reduce-scatter.1

commit v4 on v3

--- a/solution.py
+++ b/solution.py
@@ -69,8 +69,11 @@
 ):
     count = len(operands)
 
-    def body(meta_ref, *refs):
-        kernel(meta_ref, *refs[:count], *refs[count + len(after) :])
+    lead = 0 if meta is None else 1
+
+    def body(*refs):
+        head, refs = refs[:lead], refs[lead:]
+        kernel(*head, *refs[:count], *refs[count + len(after) :])
 
     def whole(i):
         return pl.BlockSpec(memory_space=pl.ANY if i in hbm else pltpu.VMEM)
@@ -80,14 +83,14 @@
         name=name,
         out_shape=tuple(outs),
         grid=grid,
-        in_specs=[pl.BlockSpec(memory_space=pltpu.SMEM)]
+        in_specs=[pl.BlockSpec(memory_space=pltpu.SMEM)] * lead
         + (blocks or [whole(i) for i in range(count)])
         + [pl.BlockSpec(memory_space=pl.ANY)] * len(after),
         out_specs=tuple(out_blocks or [pl.BlockSpec(memory_space=pltpu.VMEM) for _ in outs]),
         scratch_shapes=list(scratch),
         compiler_params=pltpu.CompilerParams(vmem_limit_bytes=vmem * 1024 * 1024),
         cost_estimate=pl.CostEstimate(flops=span * 10**9, bytes_accessed=0, transcendentals=0),
-    )(meta, *operands, *after)
+    )(*([meta] * lead), *operands, *after)
 
 
 def row_block(height, width, index):
@@ -102,7 +105,7 @@
     return jax.ShapeDtypeStruct(shape, dtype)
 
 
-def pack_kernel(meta, q_ref, k_ref, v_ref, seg_ref, out, sems):
+def pack_kernel(q_ref, k_ref, v_ref, seg_ref, out, sems):
     copies = []
     for to in range(8):
         to_x, to_h = to // 2, to % 2
@@ -280,7 +283,7 @@
     for shift, part in ((0, own), (1, right), (3, left)):
         held[:, pl.ds(shift * FEAT, FEAT)] = part[...]
     far = pl.ds(2 * FEAT, FEAT)
-    is_high = step >= 2
+    is_high = step == 1
 
     @pl.when(is_high)
     def _():
@@ -297,7 +300,7 @@
 
 def out_kernel(meta, here_low, here_high, there_low, there_high, w_ref, out, wide):
     h = meta[1]
-    is_low = pl.program_id(0) < 2
+    is_low = pl.program_id(0) == 0
 
     @pl.when(pl.program_id(0) == 0)
     def _():
@@ -392,7 +395,7 @@
     (packed,) = call(
         pack_kernel,
         "pack",
-        meta,
+        None,
         (queries, key_heads, value_heads, segment_ids),
         [shaped((8, PACK, ROWS), BF16)],
         [pltpu.SemaphoreType.DMA((8, 5))],
@@ -470,9 +473,9 @@
         [pltpu.VMEM((2 * FEAT, NX * FEAT), BF16)],
         span=20,
         vmem=61,
-        grid=(4,),
-        blocks=[row_block(QB, FEAT, lambda i: i % 2)] * 4 + [weight_block],
-        out_blocks=[pl.BlockSpec((NX, QB, FEAT), lambda i: (0, i, 0))],
+        grid=(2,),
+        blocks=[row_block(half, FEAT, lambda i: 0)] * 4 + [weight_block],
+        out_blocks=[pl.BlockSpec((NX, half, FEAT), lambda i: (0, i, 0))],
     )
     output = lax.psum_scatter(
         out_all,
@@ -487,13 +490,14 @@
         meta,
         (*grads_out, weight),
         [shaped((GROUP, FEAT), BF16), shaped((GROUP, FEAT), F32)],
-        [pltpu.VMEM((QB, NX * FEAT), BF16), pltpu.VMEM((2 * FEAT, NX * FEAT), BF16)],
+        [pltpu.VMEM((half, NX * FEAT), BF16), pltpu.VMEM((2 * FEAT, NX * FEAT), BF16)],
         after=(out_all,),
         vmem=61,
-        grid=(4,),
-        blocks=[row_block(QB, FEAT, lambda i: i)] * 3
-        + [row_block(QB, FEAT, lambda i: lax.min(i, 1)), row_block(QB, FEAT, lambda i: lax.max(i - 2, 0)), weight_block],
-        out_blocks=[row_block(QB, FEAT, lambda i: i)] * 2,
+        grid=(2,),
+        blocks=[row_block(half, FEAT, lambda i: i)] * 3
+        + [row_block(half, FEAT, lambda i: 0)] * 2
+        + [weight_block],
+        out_blocks=[row_block(half, FEAT, lambda i: i)] * 2,
     )
     grad_part = lax.ppermute(grad_send, "cp", cp_pairs(0, 1))
 

time: 158 us -> 156 us (0.987)
  starting transfers between devices: 44.9 us -> 48 us
  waiting for transfers between devices: 46.3 us -> 44 us
    ppermute x2, starting transfers between devices: 7.51 us -> 9.54 us  [per_device(): lax.ppermute(p, both, x_to_z_pairs(dy))]
    all_to_all x1, waiting for transfers between devices: 5.74 us -> 3.75 us  [per_device(): blocks = lax.all_to_all(packed, 'cp', 0, 0)]
    ppermute x2, waiting for transfers between devices: 7 us -> 8.9 us  [per_device(): turned = [lax.ppermute(out_weight, both, x_to_z_pairs(dy)) for dy in (0, 1)]]
  transfers between devices with their start and end apart: 22 -> 22, of which waited for: 13 -> 14; matrix products, arithmetic and copies ran while one was open for 0% -> 0% of each run, Pallas kernels for 30% -> 29%
where the time goes in v4:
time: 156 us
  starting transfers between devices  48 us (31%)
  Pallas kernels  45.5 us (29%)
  waiting for transfers between devices  44 us (28%)
  between operations  14.3 us (9%)
  local copies, waits for them, and re-layouts  3.92 us (3%)
    pallas_call x13, Pallas kernels, call(): pl.pallas_call(body, name=name, out_shape=tuple(outs), grid=grid, in_spec...  45.5 us
    ppermute x2, waiting for transfers between devices, per_device(): lax.ppermute(p, both, x_to_z_pairs(dy))  19 us
    ppermute x2, starting transfers between devices, per_device(): lax.ppermute(p, both, x_to_z_pairs(dy))  9.54 us
    ppermute x2, waiting for transfers between devices, per_device(): turned = [lax.ppermute(out_weight, both, x_to_z_pairs(dy)) for dy in (0, 1)]  8.9 us
    ppermute x2, starting transfers between devices, per_device(): turned = [lax.ppermute(out_weight, both, x_to_z_pairs(dy)) for dy in (0, 1)]  8.05 us
    all_to_all x1, starting transfers between devices, per_device(): blocks = lax.all_to_all(packed, 'cp', 0, 0)  7.91 us
    all_to_all x1, starting transfers between devices, per_device(): returned = lax.all_to_all(grads, 'cp', 0, 0)  7.16 us
    ppermute x3, starting transfers between devices, per_device(): lax.ppermute(p, 'dp', z_pairs(dz))  5.23 us
  transfers between devices with their start and end apart: 22, of which 14 were waited for; matrix products, arithmetic and copies ran while one was open for 0% of the time, Pallas kernels for 29%

profile of v4, /device:TPU:22, one launch (start us, length us, event | category | flops | bytes accessed | tf_op | source)
XLA Modules:
  0.0 155.7 jit_solution(137560674010869390)
XLA Ops:
  7.2 5.9 %collective-permute-start.2 = (bf16[192,384]{1,0:T(8,128)(2,1)}, bf16[192,384]{1,0:T(8,128)(2,1)S(1)}, u32[]{:S(2)}, u32[]{:S(2)}) collective-permute-start(bf16[192,384]{1,0:T(8,128)(2,1)} %param.10), channel_id=1, source_target_pairs={{0,0},{1,1},{2,16},{3,17},{4,32},{5,33},{6,48},{7,49},{8,8},{9,9},... | collective-permute-start | bytes 442376 | tf_op jit(solution)/shard_map/ppermute | solution.py:394
  13.0 2.2 %collective-permute-start.3 = (bf16[192,384]{1,0:T(8,128)(2,1)}, bf16[192,384]{1,0:T(8,128)(2,1)S(1)}, u32[]{:S(2)}, u32[]{:S(2)}) collective-permute-start(bf16[192,384]{1,0:T(8,128)(2,1)} %param.10), channel_id=1, source_target_pairs={{0,64},{1,65},{2,80},{3,81},{4,96},{5,97},{6,112},{7,113},{8,72},{... | collective-permute-start | bytes 442376 | tf_op jit(solution)/shard_map/ppermute | solution.py:394
  15.2 3.4 %pack.1.refs_4_ = bf16[8,656,128]{2,1,0:T(8,128)(2,1)} custom-call(bf16[128,3072]{1,0:T(8,128)(2,1)} %refs_0_.1, bf16[128,512]{1,0:T(8,128)(2,1)} %refs_1_.1, bf16[128,512]{1,0:T(8,128)(2,1)} %refs_2_.1, s32[1,128]{1,0:T(1,128)} %refs_3_.2), custom_call_target="tpu_custom_call" | custom-call | tf_op jit(solution)/shard_map/pack/pallas_call | solution.py:81
  18.7 7.9 %all-to-all-start = ((bf16[8,656,128]{2,1,0:T(8,128)(2,1)}), bf16[8,656,128]{2,1,0:T(8,128)(2,1)S(1)}, u32[]{:S(2)}, u32[]{:S(2)}) async-start(bf16[8,656,128]{2,1,0:T(8,128)(2,1)} %pack.1.refs_4_), calls=%async_computation | async-start | bytes 2686976 | tf_op jit(solution)/shard_map/all_to_all | solution.py:405
  26.7 1.8 %collective-permute-done.2.refs_1_ = bf16[192,384]{1,0:T(8,128)(2,1)S(1)} collective-permute-done((bf16[192,384]{1,0:T(8,128)(2,1)}, bf16[192,384]{1,0:T(8,128)(2,1)S(1)}, u32[]{:S(2)}, u32[]{:S(2)}) %collective-permute-start.2) | collective-permute-done | bytes 147488 | tf_op jit(solution)/shard_map/ppermute | solution.py:394
  28.5 7.1 %collective-permute-done.3.refs_2_ = bf16[192,384]{1,0:T(8,128)(2,1)S(1)} collective-permute-done((bf16[192,384]{1,0:T(8,128)(2,1)}, bf16[192,384]{1,0:T(8,128)(2,1)S(1)}, u32[]{:S(2)}, u32[]{:S(2)}) %collective-permute-start.3) | collective-permute-done | bytes 147488 | tf_op jit(solution)/shard_map/ppermute | solution.py:394
  36.7 1.6 %turned.1 = (bf16[2,192,384]{2,1,0:T(8,128)(2,1)}, bf16[1024,384]{1,0:T(8,128)(2,1)}) custom-call(s32[5]{0:T(128)S(1)} %stack.23.refs_0_, bf16[192,384]{1,0:T(8,128)(2,1)S(1)} %collective-permute-done.2.refs_1_, bf16[192,384]{1,0:T(8,128)(2,1)S(1)} %collective-permute-done.3.refs_2_, bf16[1024,384]{1,0:T(8,128)(2,1)S(1)} %copy-done.13, ...), custom_call_target="tpu_custom_call" | custom-call | flops 20000000000 | tf_op jit(solution)/shard_map/turned/pallas_call | solution.py:81
  38.4 2.0 %collective-permute-start.5 = (bf16[1024,384]{1,0:T(8,128)(2,1)}, bf16[1024,384]{1,0:T(8,128)(2,1)S(1)}, u32[]{:S(2)}, u32[]{:S(2)}) collective-permute-start(bf16[1024,384]{1,0:T(8,128)(2,1)} %get-tuple-element.42.refs_1_.refs_5_), channel_id=1, source_target_pairs={{0,6},{1,7},{2,0},{3,1},{4,2},{5,3},{6,4},{7,5},{8,14},{9,15},{10,... | collective-permute-start | bytes 2359304 | tf_op jit(solution)/shard_map/ppermute | solution.py:418
  40.5 3.8 %all-to-all-done.refs_1_ = bf16[8,656,128]{2,1,0:T(8,128)(2,1)S(1)} async-done(((bf16[8,656,128]{2,1,0:T(8,128)(2,1)}), bf16[8,656,128]{2,1,0:T(8,128)(2,1)S(1)}, u32[]{:S(2)}, u32[]{:S(2)}) %all-to-all-start) | async-done | bytes 1343520 | tf_op jit(solution)/shard_map/all_to_all | solution.py:405
  44.2 2.4 %forward_low.1 = (bf16[512,384]{1,0:T(8,128)(2,1)S(1)}, bf16[3,1024,128]{2,1,0:T(8,128)(2,1)S(1)}, bf16[2,1024,128]{2,1,0:T(8,128)(2,1)S(1)}, bf16[128,1024]{1,0...) custom-call(s32[5]{0:T(128)S(1)} %stack.23.refs_0_, bf16[8,656,128]{2,1,0:T(8,128)(2,1)S(1)} %all-to-all-done.refs_1_), custom_call_target="tpu_custom_call" | custom-call | tf_op jit(solution)/shard_map/forward_low/pallas_call | solution.py:81
  46.7 2.1 %collective-permute-start = (bf16[512,384]{1,0:T(8,128)(2,1)S(1)}, bf16[512,384]{1,0:T(8,128)(2,1)S(1)}, u32[]{:S(2)}, u32[]{:S(2)}) collective-permute-start(bf16[512,384]{1,0:T(8,128)(2,1)S(1)} %get-tuple-element.33.refs_1_), channel_id=1, source_target_pairs={{0,1},{1,0},{2,3},{3,2},{4,5},{5,4},{6,7},{7,6},{8,9},{9,8},{10,11... | collective-permute-start | bytes 1179656 | tf_op jit(solution)/shard_map/ppermute | solution.py:440
  48.8 3.6 %forward_high.1 = (bf16[512,384]{1,0:T(8,128)(2,1)S(1)}, f32[8,512]{1,0:T(8,128)S(1)}) custom-call(s32[5]{0:T(128)S(1)} %stack.23.refs_0_, bf16[3,1024,128]{2,1,0:T(8,128)(2,1)S(1)} %get-tuple-element.34.refs_1_, bf16[2,1024,128]{2,1,0:T(8,128)(2,1)S(1)} %get-tuple-element.35.refs_2_, bf16[128,1024]{1,0:T(8,128)(2,1)S(1)} %get-tuple-element.36.refs_3_, ...), custom_call_target="tpu_custom_call" | custom-call | flops 99999997952 | tf_op jit(solution)/shard_map/forward_high/pallas_call | solution.py:81
  52.4 1.6 %collective-permute-start.1 = (bf16[512,384]{1,0:T(8,128)(2,1)S(1)}, bf16[512,384]{1,0:T(8,128)(2,1)}, u32[]{:S(2)}, u32[]{:S(2)}) collective-permute-start(bf16[512,384]{1,0:T(8,128)(2,1)S(1)} %get-tuple-element.38.refs_2_.refs_3_), channel_id=1, source_target_pairs={{0,1},{1,0},{2,3},{3,2},{4,5},{5,4},{6,7},{7,6},{8,9},{9,8},{10,11... | collective-permute-start | bytes 1179656 | tf_op jit(solution)/shard_map/ppermute | solution.py:450
  54.0 4.5 %collective-permute-done.4.refs_1_.refs_2_.refs_6_ = bf16[1024,384]{1,0:T(8,128)(2,1)S(1)} collective-permute-done((bf16[1024,384]{1,0:T(8,128)(2,1)}, bf16[1024,384]{1,0:T(8,128)(2,1)S(1)}, u32[]{:S(2)}, u32[]{:S(2)}) %collective-permute-start.4) | collective-permute-done | bytes 786464 | tf_op jit(solution)/shard_map/ppermute | solution.py:417
  58.5 1.8 %halves.1 = (bf16[512,384]{1,0:T(8,128)(2,1)}, bf16[512,384]{1,0:T(8,128)(2,1)}) custom-call(s32[5]{0:T(128)S(1)} %stack.23.refs_0_, bf16[1024,384]{1,0:T(8,128)(2,1)S(1)} %collective-permute-done.4.refs_1_.refs_2_.refs_6_, bf16[1024,384]{1,0:T(8,128)(2,1)S(1)} %collective-permute-done.5.refs_2_.refs_3_.refs_7_, ...), custom_call_target="tpu_custom_call" | custom-call | tf_op jit(solution)/shard_map/halves/pallas_call | solution.py:81
  60.3 2.4 %collective-permute-start.6 = (bf16[512,384]{1,0:T(8,128)(2,1)}, bf16[512,384]{1,0:T(8,128)(2,1)}, u32[]{:S(2)}, u32[]{:S(2)}) collective-permute-start(bf16[512,384]{1,0:T(8,128)(2,1)} %get-tuple-element.43), channel_id=1, source_target_pairs={{0,2},{1,3},{2,4},{3,5},{4,6},{5,7},{6,0},{7,1},{8,10},{9,11},{10,... | collective-permute-start | bytes 1179656 | tf_op jit(solution)/shard_map/ppermute | solution.py:462
  62.8 1.8 %collective-permute-done.1.refs_4_ = bf16[512,384]{1,0:T(8,128)(2,1)} collective-permute-done((bf16[512,384]{1,0:T(8,128)(2,1)S(1)}, bf16[512,384]{1,0:T(8,128)(2,1)}, u32[]{:S(2)}, u32[]{:S(2)}) %collective-permute-start.1) | collective-permute-done | bytes 393248 | tf_op jit(solution)/shard_map/ppermute | solution.py:450
  64.8 7.2 %out.1.refs_7_ = bf16[4,1024,384]{2,1,0:T(8,128)(2,1)} custom-call(s32[5]{0:T(128)} %copy-done.11, bf16[512,384]{1,0:T(8,128)(2,1)} %copy-done.14, bf16[512,384]{1,0:T(8,128)(2,1)} %copy-done.9, bf16[512,384]{1,0:T(8,128)(2,1)} %copy-done.16, bf16[512,384]{1,0:T(8,128)(2,1)} %collective-permute-done.1.refs_4_, bf16[4,2,2,192,384]{4,3,2,1,0:T(8,128)(2,1)} %bitcast.7), custom_call_target="tpu_custom_call" | custom-call | flops 20000000000 | tf_op jit(solution)/shard_map/out/pallas_call | solution.py:81
  72.1 2.2 %collective-permute-done.7.refs_5_.refs_9_ = bf16[512,384]{1,0:T(8,128)(2,1)} collective-permute-done((bf16[512,384]{1,0:T(8,128)(2,1)}, bf16[512,384]{1,0:T(8,128)(2,1)}, u32[]{:S(2)}, u32[]{:S(2)}) %collective-permute-start.7) | collective-permute-done | bytes 393248 | tf_op jit(solution)/shard_map/ppermute | solution.py:463
  74.3 6.8 %grad_attended.1 = (bf16[1024,384]{1,0:T(8,128)(2,1)}, f32[1024,384]{1,0:T(8,128)}) custom-call(s32[5]{0:T(128)} %copy-done.11, bf16[1024,384]{1,0:T(8,128)(2,1)} %get-tuple-element.42.refs_1_.refs_5_, bf16[1024,384]{1,0:T(8,128)(2,1)} %copy-done.1, bf16[1024,384]{1,0:T(8,128)(2,1)} %copy-done.3, bf16[512,384]{1,0:T(8,128)(2,1)} %collective-permute-done.6.refs_4_.refs_8_, ...), custom_call_target="tpu_custom_call" | custom-call | tf_op jit(solution)/shard_map/grad_attended/pallas_call | solution.py:81
  81.9 1.6 %copy-done.5 = f32[1024,384]{1,0:T(8,128)S(1)} copy-done((f32[1024,384]{1,0:T(8,128)S(1)}, f32[1024,384]{1,0:T(8,128)}, u32[]{:S(2)}) %copy-start.5) | copy-done | bytes 1572888
  84.6 4.5 %grad_weight.1 = (f32[2,4,192,384]{3,2,1,0:T(8,128)S(1)}, bf16[4,96,384]{2,1,0:T(8,128)(2,1)S(1)}, bf16[4,96,384]{2,1,0:T(8,128)(2,1)S(1)}, bf16[4,96,384]{2,1,0:T(8,128)(2,1)S(1)}, bf16[4,96,384]{2,1,0:T(8,128)(2,1)S(1)}) custom-call(s32[5]{0:T(128)S(1)} %copy-done.12, bf16[512,384]{1,0:T(8,128)(2,1)S(1)} %copy-done.15, bf16[512,384]{1,0:T(8,128)(2,1)S(1)} %copy-done.10, ...), custom_call_target="tpu_custom_call" | custom-call | flops 80000000000 | tf_op jit(solution)/shard_map/grad_weight/pallas_call | solution.py:81
  92.0 1.6 z_sum.1
  94.8 4.0 %collective-permute-start.14 = (bf16[2,192,384]{2,1,0:T(8,128)(2,1)}, bf16[2,192,384]{2,1,0:T(8,128)(2,1)}, u32[]{:S(2)}, u32[]{:S(2)}) collective-permute-start(bf16[2,192,384]{2,1,0:T(8,128)(2,1)} %get-tuple-element.57), channel_id=1, source_target_pairs={{0,32},{8,40},{16,48},{24,56},{32,0},{40,8},{48,16},{56,24},{64,96... | collective-permute-start | bytes 884744 | tf_op jit(solution)/shard_map/ppermute | solution.py:523
  98.8 1.7 %collective-permute-done.8.refs_7_ = bf16[1024,384]{1,0:T(8,128)(2,1)S(1)} collective-permute-done((bf16[1024,384]{1,0:T(8,128)(2,1)}, bf16[1024,384]{1,0:T(8,128)(2,1)S(1)}, u32[]{:S(2)}, u32[]{:S(2)}) %collective-permute-start.8) | collective-permute-done | bytes 786464 | tf_op jit(solution)/shard_map/ppermute | solution.py:502
  100.5 8.4 %backward.1.refs_5_ = bf16[8,640,128]{2,1,0:T(8,128)(2,1)} custom-call(s32[5]{0:T(128)S(1)} %copy-done.12, bf16[3,1024,128]{2,1,0:T(8,128)(2,1)S(1)} %copy-done.8, bf16[2,1024,128]{2,1,0:T(8,128)(2,1)S(1)} %get-tuple-element.35.refs_2_, s32[8,128]{1,0:T(8,128)S(1)} %get-tuple-element.37.refs_4_.refs_3_, f32[8,512]{1,0:T(8,128)S(1)} %get-tuple-element.40.refs_4_, ...), custom_call_target="tpu_custom_call" | custom-call | tf_op jit(solution)/shard_map/backward/pallas_call | solution.py:81
  108.9 7.2 %all-to-all-start.1 = ((bf16[8,640,128]{2,1,0:T(8,128)(2,1)}), bf16[8,640,128]{2,1,0:T(8,128)(2,1)S(1)}, u32[]{:S(2)}, u32[]{:S(2)}) async-start(bf16[8,640,128]{2,1,0:T(8,128)(2,1)} %backward.1.refs_5_), calls=%async_computation.2 | async-start | bytes 2621440 | tf_op jit(solution)/shard_map/all_to_all | solution.py:541
  117.3 5.0 %collective-permute-start.16 = (bf16[192,384]{1,0:T(8,128)(2,1)S(1)}, bf16[192,384]{1,0:T(8,128)(2,1)S(1)}, u32[]{:S(2)}, u32[]{:S(2)}) collective-permute-start(bf16[192,384]{1,0:T(8,128)(2,1)S(1)} %get-tuple-element.59), channel_id=1, source_target_pairs={{0,0},{1,1},{2,16},{3,17},{4,32},{5,33},{6,48},{7,49},{8,8},{9,9},... | collective-permute-start | bytes 442376 | tf_op jit(solution)/shard_map/ppermute | solution.py:552
  122.3 4.6 %collective-permute-start.17 = (bf16[192,384]{1,0:T(8,128)(2,1)S(1)}, bf16[192,384]{1,0:T(8,128)(2,1)S(1)}, u32[]{:S(2)}, u32[]{:S(2)}) collective-permute-start(bf16[192,384]{1,0:T(8,128)(2,1)S(1)} %get-tuple-element.60), channel_id=1, source_target_pairs={{0,64},{1,65},{2,80},{3,81},{4,96},{5,97},{6,112},{7,113},{8,72},{... | collective-permute-start | bytes 442376 | tf_op jit(solution)/shard_map/ppermute | solution.py:552
  126.9 17.5 %collective-permute-done.16.refs_1_ = bf16[192,384]{1,0:T(8,128)(2,1)S(1)} collective-permute-done((bf16[192,384]{1,0:T(8,128)(2,1)S(1)}, bf16[192,384]{1,0:T(8,128)(2,1)S(1)}, u32[]{:S(2)}, u32[]{:S(2)}) %collective-permute-start.16) | collective-permute-done | bytes 147488 | tf_op jit(solution)/shard_map/ppermute | solution.py:552
  144.4 1.5 collective-permute-done.17.refs_2_
  147.1 1.7 %unpack.1 = (bf16[128,3072]{1,0:T(8,128)(2,1)}, bf16[128,512]{1,0:T(8,128)(2,1)}, bf16[128,512]{1,0:T(8,128)(2,1)}) custom-call(s32[5]{0:T(128)S(1)} %copy-done.12, bf16[8,640,128]{2,1,0:T(8,128)(2,1)S(1)} %all-to-all-done.1.refs_1_), custom_call_target="tpu_custom_call" | custom-call | tf_op jit(solution)/shard_map/unpack/pallas_call | solution.py:81
  (64 shorter events, 10.1 us)
Async XLA Ops:
  7.2 21.3 %collective-permute-start.2 = (bf16[192,384]{1,0:T(8,128)(2,1)}, bf16[192,384]{1,0:T(8,128)(2,1)S(1)}, u32[]{:S(2)}, u32[]{:S(2)}) collective-permute-start(bf16[192,384]{1,0:T(8,128)(2,1)} %param.10), channel_id=1, source_target_pairs={{0,0},{1,1},{2,16},{3,17},{4,32},{5,33},{6,48},{7,49},{8,8},{9,9},... | collective-permute-start | bytes 442376 | tf_op jit(solution)/shard_map/ppermute | solution.py:394
  13.0 22.5 %collective-permute-start.3 = (bf16[192,384]{1,0:T(8,128)(2,1)}, bf16[192,384]{1,0:T(8,128)(2,1)S(1)}, u32[]{:S(2)}, u32[]{:S(2)}) collective-permute-start(bf16[192,384]{1,0:T(8,128)(2,1)} %param.10), channel_id=1, source_target_pairs={{0,64},{1,65},{2,80},{3,81},{4,96},{5,97},{6,112},{7,113},{8,72},{... | collective-permute-start | bytes 442376 | tf_op jit(solution)/shard_map/ppermute | solution.py:394
  18.6 16.9 %copy-start = (bf16[8,656,128]{2,1,0:T(8,128)(2,1)S(1)}, bf16[8,656,128]{2,1,0:T(8,128)(2,1)}, u32[]{:S(2)}) copy-start(bf16[8,656,128]{2,1,0:T(8,128)(2,1)} %pack.1.refs_4_) | copy-start | bytes 4030468
  18.7 25.6 %all-to-all-start = ((bf16[8,656,128]{2,1,0:T(8,128)(2,1)}), bf16[8,656,128]{2,1,0:T(8,128)(2,1)S(1)}, u32[]{:S(2)}, u32[]{:S(2)}) async-start(bf16[8,656,128]{2,1,0:T(8,128)(2,1)} %pack.1.refs_4_), calls=%async_computation | async-start | bytes 2686976 | tf_op jit(solution)/shard_map/all_to_all | solution.py:405
  26.6 38.2 %all-gather.3.cloned.1.call-start = ((), (), s32[]{:S(2)}) async-start(), calls=%async_computation.4 | async-start | bytes 2654208 | tf_op jit(solution)/shard_map/all_gather | solution.py:419
  26.7 31.8 %copy-start.11 = (s32[5]{0:T(128)}, s32[5]{0:T(128)S(1)}, u32[]{:S(2)}) copy-start(s32[5]{0:T(128)S(1)} %stack.23.refs_0_) | copy-start | bytes 64
  38.3 20.2 %collective-permute-start.4 = (bf16[1024,384]{1,0:T(8,128)(2,1)}, bf16[1024,384]{1,0:T(8,128)(2,1)S(1)}, u32[]{:S(2)}, u32[]{:S(2)}) collective-permute-start(bf16[1024,384]{1,0:T(8,128)(2,1)} %get-tuple-element.42.refs_1_.refs_5_), channel_id=1, source_target_pairs={{0,2},{1,3},{2,4},{3,5},{4,6},{5,7},{6,0},{7,1},{8,10},{9,11},{10,... | collective-permute-start | bytes 2359304 | tf_op jit(solution)/shard_map/ppermute | solution.py:417
  38.4 20.1 %collective-permute-start.5 = (bf16[1024,384]{1,0:T(8,128)(2,1)}, bf16[1024,384]{1,0:T(8,128)(2,1)S(1)}, u32[]{:S(2)}, u32[]{:S(2)}) collective-permute-start(bf16[1024,384]{1,0:T(8,128)(2,1)} %get-tuple-element.42.refs_1_.refs_5_), channel_id=1, source_target_pairs={{0,6},{1,7},{2,0},{3,1},{4,2},{5,3},{6,4},{7,5},{8,14},{9,15},{10,... | collective-permute-start | bytes 2359304 | tf_op jit(solution)/shard_map/ppermute | solution.py:418
  40.4 108.4 %reduce-scatter.2.cloned.1.call-start = ((), (), s32[]{:S(2)}) async-start(), calls=%async_computation.3 | async-start | bytes 3932160 | tf_op jit(solution)/shard_map/reduce_scatter | solution.py:480
  46.7 16.1 %collective-permute-start = (bf16[512,384]{1,0:T(8,128)(2,1)S(1)}, bf16[512,384]{1,0:T(8,128)(2,1)S(1)}, u32[]{:S(2)}, u32[]{:S(2)}) collective-permute-start(bf16[512,384]{1,0:T(8,128)(2,1)S(1)} %get-tuple-element.33.refs_1_), channel_id=1, source_target_pairs={{0,1},{1,0},{2,3},{3,2},{4,5},{5,4},{6,7},{7,6},{8,9},{9,8},{10,11... | collective-permute-start | bytes 1179656 | tf_op jit(solution)/shard_map/ppermute | solution.py:440
  52.4 12.4 %copy-start.9 = (bf16[512,384]{1,0:T(8,128)(2,1)}, bf16[512,384]{1,0:T(8,128)(2,1)S(1)}, u32[]{:S(2)}) copy-start(bf16[512,384]{1,0:T(8,128)(2,1)S(1)} %get-tuple-element.38.refs_2_.refs_3_) | copy-start | bytes 1179652
  52.4 12.2 %collective-permute-start.1 = (bf16[512,384]{1,0:T(8,128)(2,1)S(1)}, bf16[512,384]{1,0:T(8,128)(2,1)}, u32[]{:S(2)}, u32[]{:S(2)}) collective-permute-start(bf16[512,384]{1,0:T(8,128)(2,1)S(1)} %get-tuple-element.38.refs_2_.refs_3_), channel_id=1, source_target_pairs={{0,1},{1,0},{2,3},{3,2},{4,5},{5,4},{6,7},{7,6},{8,9},{9,8},{10,11... | collective-permute-start | bytes 1179656 | tf_op jit(solution)/shard_map/ppermute | solution.py:450
  58.5 13.5 %copy-start.1 = (bf16[1024,384]{1,0:T(8,128)(2,1)}, bf16[1024,384]{1,0:T(8,128)(2,1)S(1)}, u32[]{:S(2)}) copy-start(bf16[1024,384]{1,0:T(8,128)(2,1)S(1)} %collective-permute-done.4.refs_1_.refs_2_.refs_6_) | copy-start | bytes 2359300
  58.5 13.5 %copy-start.3 = (bf16[1024,384]{1,0:T(8,128)(2,1)}, bf16[1024,384]{1,0:T(8,128)(2,1)S(1)}, u32[]{:S(2)}) copy-start(bf16[1024,384]{1,0:T(8,128)(2,1)S(1)} %collective-permute-done.5.refs_2_.refs_3_.refs_7_) | copy-start | bytes 2359300
  60.3 11.7 %collective-permute-start.6 = (bf16[512,384]{1,0:T(8,128)(2,1)}, bf16[512,384]{1,0:T(8,128)(2,1)}, u32[]{:S(2)}, u32[]{:S(2)}) collective-permute-start(bf16[512,384]{1,0:T(8,128)(2,1)} %get-tuple-element.43), channel_id=1, source_target_pairs={{0,2},{1,3},{2,4},{3,5},{4,6},{5,7},{6,0},{7,1},{8,10},{9,11},{10,... | collective-permute-start | bytes 1179656 | tf_op jit(solution)/shard_map/ppermute | solution.py:462
  62.8 11.6 %collective-permute-start.7 = (bf16[512,384]{1,0:T(8,128)(2,1)}, bf16[512,384]{1,0:T(8,128)(2,1)}, u32[]{:S(2)}, u32[]{:S(2)}) collective-permute-start(bf16[512,384]{1,0:T(8,128)(2,1)} %get-tuple-element.44), channel_id=1, source_target_pairs={{0,6},{1,7},{2,0},{3,1},{4,2},{5,3},{6,4},{7,5},{8,14},{9,15},{10,... | collective-permute-start | bytes 1179656 | tf_op jit(solution)/shard_map/ppermute | solution.py:463
  72.0 9.9 %copy-start.2 = (bf16[1024,384]{1,0:T(8,128)(2,1)S(1)}, bf16[1024,384]{1,0:T(8,128)(2,1)}, u32[]{:S(2)}) copy-start(bf16[1024,384]{1,0:T(8,128)(2,1)} %copy-done.1) | copy-start | bytes 2359300
  72.0 9.9 %copy-start.4 = (bf16[1024,384]{1,0:T(8,128)(2,1)S(1)}, bf16[1024,384]{1,0:T(8,128)(2,1)}, u32[]{:S(2)}) copy-start(bf16[1024,384]{1,0:T(8,128)(2,1)} %copy-done.3) | copy-start | bytes 2359300
  72.0 9.9 %copy-start.10 = (bf16[512,384]{1,0:T(8,128)(2,1)S(1)}, bf16[512,384]{1,0:T(8,128)(2,1)}, u32[]{:S(2)}) copy-start(bf16[512,384]{1,0:T(8,128)(2,1)} %copy-done.9) | copy-start | bytes 1179652
  72.0 9.9 %copy-start.12 = (s32[5]{0:T(128)S(1)}, s32[5]{0:T(128)}, u32[]{:S(2)}) copy-start(s32[5]{0:T(128)} %copy-done.11) | copy-start | bytes 64
  72.1 9.9 %copy-start.15 = (bf16[512,384]{1,0:T(8,128)(2,1)S(1)}, bf16[512,384]{1,0:T(8,128)(2,1)}, u32[]{:S(2)}) copy-start(bf16[512,384]{1,0:T(8,128)(2,1)} %copy-done.14) | copy-start | bytes 1179652
  81.1 19.4 %collective-permute-start.8 = (bf16[1024,384]{1,0:T(8,128)(2,1)}, bf16[1024,384]{1,0:T(8,128)(2,1)S(1)}, u32[]{:S(2)}, u32[]{:S(2)}) collective-permute-start(bf16[1024,384]{1,0:T(8,128)(2,1)} %get-tuple-element.46), channel_id=1, source_target_pairs={{0,1},{1,0},{2,3},{3,2},{4,5},{5,4},{6,7},{7,6},{8,9},{9,8},{10,11... | collective-permute-start | bytes 2359304 | tf_op jit(solution)/shard_map/ppermute | solution.py:502
  89.1 1.7 %collective-permute-start.9 = (bf16[4,96,384]{2,1,0:T(8,128)(2,1)S(1)}, bf16[4,96,384]{2,1,0:T(8,128)(2,1)S(1)}, u32[]{:S(2)}, u32[]{:S(2)}) collective-permute-start(bf16[4,96,384]{2,1,0:T(8,128)(2,1)S(1)} %get-tuple-element.48), channel_id=1, source_target_pairs={{0,8},{8,0},{16,24},{24,16},{32,40},{40,32},{48,56},{56,48},{64,72... | collective-permute-start | bytes 884744 | tf_op jit(solution)/shard_map/ppermute | solution.py:514
  89.2 2.0 %collective-permute-start.10 = (bf16[4,96,384]{2,1,0:T(8,128)(2,1)S(1)}, bf16[4,96,384]{2,1,0:T(8,128)(2,1)S(1)}, u32[]{:S(2)}, u32[]{:S(2)}) collective-permute-start(bf16[4,96,384]{2,1,0:T(8,128)(2,1)S(1)} %get-tuple-element.49), channel_id=1, source_target_pairs={{0,8},{8,0},{16,24},{24,16},{32,40},{40,32},{48,56},{56,48},{64,72... | collective-permute-start | bytes 884744 | tf_op jit(solution)/shard_map/ppermute | solution.py:514
  89.7 1.9 %collective-permute-start.11 = (bf16[4,96,384]{2,1,0:T(8,128)(2,1)S(1)}, bf16[4,96,384]{2,1,0:T(8,128)(2,1)S(1)}, u32[]{:S(2)}, u32[]{:S(2)}) collective-permute-start(bf16[4,96,384]{2,1,0:T(8,128)(2,1)S(1)} %get-tuple-element.50), channel_id=1, source_target_pairs={{0,8},{8,0},{16,24},{24,16},{32,40},{40,32},{48,56},{56,48},{64,72... | collective-permute-start | bytes 884744 | tf_op jit(solution)/shard_map/ppermute | solution.py:514
  89.8 2.2 %collective-permute-start.12 = (bf16[4,96,384]{2,1,0:T(8,128)(2,1)S(1)}, bf16[4,96,384]{2,1,0:T(8,128)(2,1)S(1)}, u32[]{:S(2)}, u32[]{:S(2)}) collective-permute-start(bf16[4,96,384]{2,1,0:T(8,128)(2,1)S(1)} %get-tuple-element.51), channel_id=1, source_target_pairs={{0,8},{8,0},{16,24},{24,16},{32,40},{40,32},{48,56},{56,48},{64,72... | collective-permute-start | bytes 884744 | tf_op jit(solution)/shard_map/ppermute | solution.py:514
  93.6 22.5 %collective-permute-start.13 = (bf16[2,192,384]{2,1,0:T(8,128)(2,1)}, bf16[2,192,384]{2,1,0:T(8,128)(2,1)S(1)}, u32[]{:S(2)}, u32[]{:S(2)}) collective-permute-start(bf16[2,192,384]{2,1,0:T(8,128)(2,1)} %get-tuple-element.56), channel_id=1, source_target_pairs={{0,16},{8,24},{16,32},{24,40},{32,48},{40,56},{48,0},{56,8},{64,80... | collective-permute-start | bytes 884744 | tf_op jit(solution)/shard_map/ppermute | solution.py:523
  94.8 21.3 %collective-permute-start.14 = (bf16[2,192,384]{2,1,0:T(8,128)(2,1)}, bf16[2,192,384]{2,1,0:T(8,128)(2,1)}, u32[]{:S(2)}, u32[]{:S(2)}) collective-permute-start(bf16[2,192,384]{2,1,0:T(8,128)(2,1)} %get-tuple-element.57), channel_id=1, source_target_pairs={{0,32},{8,40},{16,48},{24,56},{32,0},{40,8},{48,16},{56,24},{64,96... | collective-permute-start | bytes 884744 | tf_op jit(solution)/shard_map/ppermute | solution.py:523
  98.8 17.3 %collective-permute-start.15 = (bf16[2,192,384]{2,1,0:T(8,128)(2,1)S(1)}, bf16[2,192,384]{2,1,0:T(8,128)(2,1)}, u32[]{:S(2)}, u32[]{:S(2)}) collective-permute-start(bf16[2,192,384]{2,1,0:T(8,128)(2,1)S(1)} %get-tuple-element.58), channel_id=1, source_target_pairs={{0,48},{8,56},{16,0},{24,8},{32,16},{40,24},{48,32},{56,40},{64,11... | collective-permute-start | bytes 884744 | tf_op jit(solution)/shard_map/ppermute | solution.py:523
  108.9 38.2 %all-to-all-start.1 = ((bf16[8,640,128]{2,1,0:T(8,128)(2,1)}), bf16[8,640,128]{2,1,0:T(8,128)(2,1)S(1)}, u32[]{:S(2)}, u32[]{:S(2)}) async-start(bf16[8,640,128]{2,1,0:T(8,128)(2,1)} %backward.1.refs_5_), calls=%async_computation.2 | async-start | bytes 2621440 | tf_op jit(solution)/shard_map/all_to_all | solution.py:541
  117.3 27.0 %collective-permute-start.16 = (bf16[192,384]{1,0:T(8,128)(2,1)S(1)}, bf16[192,384]{1,0:T(8,128)(2,1)S(1)}, u32[]{:S(2)}, u32[]{:S(2)}) collective-permute-start(bf16[192,384]{1,0:T(8,128)(2,1)S(1)} %get-tuple-element.59), channel_id=1, source_target_pairs={{0,0},{1,1},{2,16},{3,17},{4,32},{5,33},{6,48},{7,49},{8,8},{9,9},... | collective-permute-start | bytes 442376 | tf_op jit(solution)/shard_map/ppermute | solution.py:552
  122.3 23.5 %collective-permute-start.17 = (bf16[192,384]{1,0:T(8,128)(2,1)S(1)}, bf16[192,384]{1,0:T(8,128)(2,1)S(1)}, u32[]{:S(2)}, u32[]{:S(2)}) collective-permute-start(bf16[192,384]{1,0:T(8,128)(2,1)S(1)} %get-tuple-element.60), channel_id=1, source_target_pairs={{0,64},{1,65},{2,80},{3,81},{4,96},{5,97},{6,112},{7,113},{8,72},{... | collective-permute-start | bytes 442376 | tf_op jit(solution)/shard_map/ppermute | solution.py:552
  (8 other events, 34.3 us)
Sparse Core Ops, SparseCore 0:
  40.5 24.2 all-gather.2
  72.1 38.4 reduce-scatter.1

commit v5 on v4

--- a/solution.py
+++ b/solution.py
@@ -147,7 +147,7 @@
     scores = dot_nt(k, q) * EXP2_SCALE
     if diagonal:
         key_pos = lax.broadcasted_iota(jnp.int32, scores.shape, 0)
-        query_pos = lax.broadcasted_iota(jnp.int32, scores.shape, 1)
+        query_pos = lax.broadcasted_iota(jnp.int32, scores.shape, 1) % QB
         scores = jnp.where(key_pos <= query_pos, scores, -1e30)
     return scores
 
@@ -211,24 +211,24 @@
     for qb in range(GROUP // QB):
         rows = pl.ds(qb * QB, QB)
         stat_ref, stat_rows = (stat_low, rows) if qb < 2 else (stat_high, pl.ds(qb * QB - GROUP // 2, QB))
-        for head in range(HEADS):
-            q = q_ref[head, rows, :]
-            g = g_ref[head, rows, :]
-            parts, delta = [], 0.0
-            for lo, hi, diagonal in key_parts(qb):
-                span = pl.ds(lo, hi - lo)
-                scores = transposed_scores(k_wide[span, :], q_wide[head, rows, :], diagonal)
-                prob = jnp.exp2(scores - stat_ref[head : head + 1, stat_rows])
-                grad_prob = dot_nt(kv_ref[1, span, :], g)
-                delta = delta + jnp.sum(prob * grad_prob, axis=0, keepdims=True)
-                gv_ref[span, :] += dot_nn(prob.astype(BF16), g)
-                parts.append((span, prob, grad_prob))
-            gq = 0.0
-            for span, prob, grad_prob in parts:
-                grad_logit = (prob * (grad_prob - delta)).astype(BF16)
-                gk_ref[span, :] += dot_nn(grad_logit, q)
-                gq = gq + dot_nn(kt_ref[:, span], grad_logit)
-            gq_ref[head, rows, :] = (gq * SCALE).T.astype(BF16)
+        q = q_ref[:, rows, :].reshape(HEADS * QB, HD)
+        g = g_ref[:, rows, :].reshape(HEADS * QB, HD)
+        q_more = q_wide[:, rows, :].reshape(HEADS * QB, 2 * HD)
+        stat = jnp.concatenate([stat_ref[head : head + 1, stat_rows] for head in range(HEADS)], axis=1)
+        parts, delta = [], 0.0
+        for lo, hi, diagonal in key_parts(qb):
+            span = pl.ds(lo, hi - lo)
+            prob = jnp.exp2(transposed_scores(k_wide[span, :], q_more, diagonal) - stat)
+            grad_prob = dot_nt(kv_ref[1, span, :], g)
+            delta = delta + jnp.sum(prob * grad_prob, axis=0, keepdims=True)
+            gv_ref[span, :] += dot_nn(prob.astype(BF16), g)
+            parts.append((span, prob, grad_prob))
+        gq = 0.0
+        for span, prob, grad_prob in parts:
+            grad_logit = (prob * (grad_prob - delta)).astype(BF16)
+            gk_ref[span, :] += dot_nn(grad_logit, q)
+            gq = gq + dot_nn(kt_ref[:, span], grad_logit)
+        gq_ref[:, rows, :] = (gq * SCALE).T.astype(BF16).reshape(HEADS, QB, HD)
     for to in range(8):
         rows = pl.ds(to * ROWS, ROWS)
         for head in range(HEADS):

time: 156 us -> 156 us (level)
  no operation moved by 1% of the time
where the time goes in v5:
time: 156 us; the launch traced here: 155 us
  starting transfers between devices  48 us (31%)
  Pallas kernels  44.5 us (29%)
  waiting for transfers between devices  44 us (28%)
  between operations  14.3 us (9%)
  local copies, waits for them, and re-layouts  3.92 us (3%)
    pallas_call x13, Pallas kernels, call(): pl.pallas_call(body, name=name, out_shape=tuple(outs), grid=grid, in_spec...  44.5 us
    ppermute x2, waiting for transfers between devices, per_device(): lax.ppermute(p, both, x_to_z_pairs(dy))  19 us
    ppermute x2, starting transfers between devices, per_device(): lax.ppermute(p, both, x_to_z_pairs(dy))  9.54 us
    ppermute x2, waiting for transfers between devices, per_device(): turned = [lax.ppermute(out_weight, both, x_to_z_pairs(dy)) for dy in (0, 1)]  8.9 us
    ppermute x2, starting transfers between devices, per_device(): turned = [lax.ppermute(out_weight, both, x_to_z_pairs(dy)) for dy in (0, 1)]  8.05 us
    all_to_all x1, starting transfers between devices, per_device(): blocks = lax.all_to_all(packed, 'cp', 0, 0)  7.91 us
    all_to_all x1, starting transfers between devices, per_device(): returned = lax.all_to_all(grads, 'cp', 0, 0)  7.17 us
    ppermute x3, starting transfers between devices, per_device(): lax.ppermute(p, 'dp', z_pairs(dz))  5.24 us
  transfers between devices with their start and end apart: 22, of which 14 were waited for; matrix products, arithmetic and copies ran while one was open for 0% of the time, Pallas kernels for 29%

profile of v5, /device:TPU:22, one launch (start us, length us, event | category | flops | bytes accessed | tf_op | source)
XLA Modules:
  0.0 154.7 jit_solution(11795647765416492427)
XLA Ops:
  7.2 5.9 %collective-permute-start.2 = (bf16[192,384]{1,0:T(8,128)(2,1)}, bf16[192,384]{1,0:T(8,128)(2,1)S(1)}, u32[]{:S(2)}, u32[]{:S(2)}) collective-permute-start(bf16[192,384]{1,0:T(8,128)(2,1)} %param.10), channel_id=1, source_target_pairs={{0,0},{1,1},{2,16},{3,17},{4,32},{5,33},{6,48},{7,49},{8,8},{9,9},... | collective-permute-start | bytes 442376 | tf_op jit(solution)/shard_map/ppermute | solution.py:394
  13.0 2.2 %collective-permute-start.3 = (bf16[192,384]{1,0:T(8,128)(2,1)}, bf16[192,384]{1,0:T(8,128)(2,1)S(1)}, u32[]{:S(2)}, u32[]{:S(2)}) collective-permute-start(bf16[192,384]{1,0:T(8,128)(2,1)} %param.10), channel_id=1, source_target_pairs={{0,64},{1,65},{2,80},{3,81},{4,96},{5,97},{6,112},{7,113},{8,72},{... | collective-permute-start | bytes 442376 | tf_op jit(solution)/shard_map/ppermute | solution.py:394
  15.2 3.4 %pack.1.refs_4_ = bf16[8,656,128]{2,1,0:T(8,128)(2,1)} custom-call(bf16[128,3072]{1,0:T(8,128)(2,1)} %refs_0_.1, bf16[128,512]{1,0:T(8,128)(2,1)} %refs_1_.1, bf16[128,512]{1,0:T(8,128)(2,1)} %refs_2_.1, s32[1,128]{1,0:T(1,128)} %refs_3_.2), custom_call_target="tpu_custom_call" | custom-call | tf_op jit(solution)/shard_map/pack/pallas_call | solution.py:81
  18.7 7.9 %all-to-all-start = ((bf16[8,656,128]{2,1,0:T(8,128)(2,1)}), bf16[8,656,128]{2,1,0:T(8,128)(2,1)S(1)}, u32[]{:S(2)}, u32[]{:S(2)}) async-start(bf16[8,656,128]{2,1,0:T(8,128)(2,1)} %pack.1.refs_4_), calls=%async_computation | async-start | bytes 2686976 | tf_op jit(solution)/shard_map/all_to_all | solution.py:405
  26.7 1.8 %collective-permute-done.2.refs_1_ = bf16[192,384]{1,0:T(8,128)(2,1)S(1)} collective-permute-done((bf16[192,384]{1,0:T(8,128)(2,1)}, bf16[192,384]{1,0:T(8,128)(2,1)S(1)}, u32[]{:S(2)}, u32[]{:S(2)}) %collective-permute-start.2) | collective-permute-done | bytes 147488 | tf_op jit(solution)/shard_map/ppermute | solution.py:394
  28.5 7.1 %collective-permute-done.3.refs_2_ = bf16[192,384]{1,0:T(8,128)(2,1)S(1)} collective-permute-done((bf16[192,384]{1,0:T(8,128)(2,1)}, bf16[192,384]{1,0:T(8,128)(2,1)S(1)}, u32[]{:S(2)}, u32[]{:S(2)}) %collective-permute-start.3) | collective-permute-done | bytes 147488 | tf_op jit(solution)/shard_map/ppermute | solution.py:394
  36.7 1.6 %turned.1 = (bf16[2,192,384]{2,1,0:T(8,128)(2,1)}, bf16[1024,384]{1,0:T(8,128)(2,1)}) custom-call(s32[5]{0:T(128)S(1)} %stack.23.refs_0_, bf16[192,384]{1,0:T(8,128)(2,1)S(1)} %collective-permute-done.2.refs_1_, bf16[192,384]{1,0:T(8,128)(2,1)S(1)} %collective-permute-done.3.refs_2_, bf16[1024,384]{1,0:T(8,128)(2,1)S(1)} %copy-done.13, ...), custom_call_target="tpu_custom_call" | custom-call | flops 20000000000 | tf_op jit(solution)/shard_map/turned/pallas_call | solution.py:81
  38.4 2.0 %collective-permute-start.5 = (bf16[1024,384]{1,0:T(8,128)(2,1)}, bf16[1024,384]{1,0:T(8,128)(2,1)S(1)}, u32[]{:S(2)}, u32[]{:S(2)}) collective-permute-start(bf16[1024,384]{1,0:T(8,128)(2,1)} %get-tuple-element.42.refs_1_.refs_5_), channel_id=1, source_target_pairs={{0,6},{1,7},{2,0},{3,1},{4,2},{5,3},{6,4},{7,5},{8,14},{9,15},{10,... | collective-permute-start | bytes 2359304 | tf_op jit(solution)/shard_map/ppermute | solution.py:418
  40.5 3.8 %all-to-all-done.refs_1_ = bf16[8,656,128]{2,1,0:T(8,128)(2,1)S(1)} async-done(((bf16[8,656,128]{2,1,0:T(8,128)(2,1)}), bf16[8,656,128]{2,1,0:T(8,128)(2,1)S(1)}, u32[]{:S(2)}, u32[]{:S(2)}) %all-to-all-start) | async-done | bytes 1343520 | tf_op jit(solution)/shard_map/all_to_all | solution.py:405
  44.2 2.4 %forward_low.1 = (bf16[512,384]{1,0:T(8,128)(2,1)S(1)}, bf16[3,1024,128]{2,1,0:T(8,128)(2,1)S(1)}, bf16[2,1024,128]{2,1,0:T(8,128)(2,1)S(1)}, bf16[128,1024]{1,0...) custom-call(s32[5]{0:T(128)S(1)} %stack.23.refs_0_, bf16[8,656,128]{2,1,0:T(8,128)(2,1)S(1)} %all-to-all-done.refs_1_), custom_call_target="tpu_custom_call" | custom-call | tf_op jit(solution)/shard_map/forward_low/pallas_call | solution.py:81
  46.7 2.1 %collective-permute-start = (bf16[512,384]{1,0:T(8,128)(2,1)S(1)}, bf16[512,384]{1,0:T(8,128)(2,1)S(1)}, u32[]{:S(2)}, u32[]{:S(2)}) collective-permute-start(bf16[512,384]{1,0:T(8,128)(2,1)S(1)} %get-tuple-element.33.refs_1_), channel_id=1, source_target_pairs={{0,1},{1,0},{2,3},{3,2},{4,5},{5,4},{6,7},{7,6},{8,9},{9,8},{10,11... | collective-permute-start | bytes 1179656 | tf_op jit(solution)/shard_map/ppermute | solution.py:440
  48.8 3.6 %forward_high.1 = (bf16[512,384]{1,0:T(8,128)(2,1)S(1)}, f32[8,512]{1,0:T(8,128)S(1)}) custom-call(s32[5]{0:T(128)S(1)} %stack.23.refs_0_, bf16[3,1024,128]{2,1,0:T(8,128)(2,1)S(1)} %get-tuple-element.34.refs_1_, bf16[2,1024,128]{2,1,0:T(8,128)(2,1)S(1)} %get-tuple-element.35.refs_2_, bf16[128,1024]{1,0:T(8,128)(2,1)S(1)} %get-tuple-element.36.refs_3_, ...), custom_call_target="tpu_custom_call" | custom-call | flops 99999997952 | tf_op jit(solution)/shard_map/forward_high/pallas_call | solution.py:81
  52.4 1.6 %collective-permute-start.1 = (bf16[512,384]{1,0:T(8,128)(2,1)S(1)}, bf16[512,384]{1,0:T(8,128)(2,1)}, u32[]{:S(2)}, u32[]{:S(2)}) collective-permute-start(bf16[512,384]{1,0:T(8,128)(2,1)S(1)} %get-tuple-element.38.refs_2_.refs_3_), channel_id=1, source_target_pairs={{0,1},{1,0},{2,3},{3,2},{4,5},{5,4},{6,7},{7,6},{8,9},{9,8},{10,11... | collective-permute-start | bytes 1179656 | tf_op jit(solution)/shard_map/ppermute | solution.py:450
  54.0 4.5 %collective-permute-done.4.refs_1_.refs_2_.refs_6_ = bf16[1024,384]{1,0:T(8,128)(2,1)S(1)} collective-permute-done((bf16[1024,384]{1,0:T(8,128)(2,1)}, bf16[1024,384]{1,0:T(8,128)(2,1)S(1)}, u32[]{:S(2)}, u32[]{:S(2)}) %collective-permute-start.4) | collective-permute-done | bytes 786464 | tf_op jit(solution)/shard_map/ppermute | solution.py:417
  58.5 1.8 %halves.1 = (bf16[512,384]{1,0:T(8,128)(2,1)}, bf16[512,384]{1,0:T(8,128)(2,1)}) custom-call(s32[5]{0:T(128)S(1)} %stack.23.refs_0_, bf16[1024,384]{1,0:T(8,128)(2,1)S(1)} %collective-permute-done.4.refs_1_.refs_2_.refs_6_, bf16[1024,384]{1,0:T(8,128)(2,1)S(1)} %collective-permute-done.5.refs_2_.refs_3_.refs_7_, ...), custom_call_target="tpu_custom_call" | custom-call | tf_op jit(solution)/shard_map/halves/pallas_call | solution.py:81
  60.3 2.4 %collective-permute-start.6 = (bf16[512,384]{1,0:T(8,128)(2,1)}, bf16[512,384]{1,0:T(8,128)(2,1)}, u32[]{:S(2)}, u32[]{:S(2)}) collective-permute-start(bf16[512,384]{1,0:T(8,128)(2,1)} %get-tuple-element.43), channel_id=1, source_target_pairs={{0,2},{1,3},{2,4},{3,5},{4,6},{5,7},{6,0},{7,1},{8,10},{9,11},{10,... | collective-permute-start | bytes 1179656 | tf_op jit(solution)/shard_map/ppermute | solution.py:462
  62.8 1.8 %collective-permute-done.1.refs_4_ = bf16[512,384]{1,0:T(8,128)(2,1)} collective-permute-done((bf16[512,384]{1,0:T(8,128)(2,1)S(1)}, bf16[512,384]{1,0:T(8,128)(2,1)}, u32[]{:S(2)}, u32[]{:S(2)}) %collective-permute-start.1) | collective-permute-done | bytes 393248 | tf_op jit(solution)/shard_map/ppermute | solution.py:450
  64.8 7.2 %out.1.refs_7_ = bf16[4,1024,384]{2,1,0:T(8,128)(2,1)} custom-call(s32[5]{0:T(128)} %copy-done.11, bf16[512,384]{1,0:T(8,128)(2,1)} %copy-done.14, bf16[512,384]{1,0:T(8,128)(2,1)} %copy-done.9, bf16[512,384]{1,0:T(8,128)(2,1)} %copy-done.16, bf16[512,384]{1,0:T(8,128)(2,1)} %collective-permute-done.1.refs_4_, bf16[4,2,2,192,384]{4,3,2,1,0:T(8,128)(2,1)} %bitcast.7), custom_call_target="tpu_custom_call" | custom-call | flops 20000000000 | tf_op jit(solution)/shard_map/out/pallas_call | solution.py:81
  72.1 2.2 %collective-permute-done.7.refs_5_.refs_9_ = bf16[512,384]{1,0:T(8,128)(2,1)} collective-permute-done((bf16[512,384]{1,0:T(8,128)(2,1)}, bf16[512,384]{1,0:T(8,128)(2,1)}, u32[]{:S(2)}, u32[]{:S(2)}) %collective-permute-start.7) | collective-permute-done | bytes 393248 | tf_op jit(solution)/shard_map/ppermute | solution.py:463
  74.3 6.8 %grad_attended.1 = (bf16[1024,384]{1,0:T(8,128)(2,1)}, f32[1024,384]{1,0:T(8,128)}) custom-call(s32[5]{0:T(128)} %copy-done.11, bf16[1024,384]{1,0:T(8,128)(2,1)} %get-tuple-element.42.refs_1_.refs_5_, bf16[1024,384]{1,0:T(8,128)(2,1)} %copy-done.1, bf16[1024,384]{1,0:T(8,128)(2,1)} %copy-done.3, bf16[512,384]{1,0:T(8,128)(2,1)} %collective-permute-done.6.refs_4_.refs_8_, ...), custom_call_target="tpu_custom_call" | custom-call | tf_op jit(solution)/shard_map/grad_attended/pallas_call | solution.py:81
  81.9 1.6 %copy-done.5 = f32[1024,384]{1,0:T(8,128)S(1)} copy-done((f32[1024,384]{1,0:T(8,128)S(1)}, f32[1024,384]{1,0:T(8,128)}, u32[]{:S(2)}) %copy-start.5) | copy-done | bytes 1572888
  84.6 4.5 %grad_weight.1 = (f32[2,4,192,384]{3,2,1,0:T(8,128)S(1)}, bf16[4,96,384]{2,1,0:T(8,128)(2,1)S(1)}, bf16[4,96,384]{2,1,0:T(8,128)(2,1)S(1)}, bf16[4,96,384]{2,1,0:T(8,128)(2,1)S(1)}, bf16[4,96,384]{2,1,0:T(8,128)(2,1)S(1)}) custom-call(s32[5]{0:T(128)S(1)} %copy-done.12, bf16[512,384]{1,0:T(8,128)(2,1)S(1)} %copy-done.15, bf16[512,384]{1,0:T(8,128)(2,1)S(1)} %copy-done.10, ...), custom_call_target="tpu_custom_call" | custom-call | flops 80000000000 | tf_op jit(solution)/shard_map/grad_weight/pallas_call | solution.py:81
  92.0 1.6 %z_sum.1 = (f32[2,192,384]{2,1,0:T(8,128)S(1)}, bf16[2,192,384]{2,1,0:T(8,128)(2,1)}, bf16[2,192,384]{2,1,0:T(8,128)(2,1)}, bf16[2,192,384]{2,1,0:T(8,128)(2,1)S(1)}) custom-call(s32[5]{0:T(128)S(1)} %copy-done.12, f32[2,4,192,384]{3,2,1,0:T(8,128)S(1)} %get-tuple-element.47.refs_1_, bf16[4,96,384]{2,1,0:T(8,128)(2,1)S(1)} %collective-permute-done.9.refs_2_, ...), custom_call_target="tpu_custom_call" | custom-call | tf_op jit(solution)/shard_map/z_sum/pallas_call | solution.py:81
  94.8 4.0 %collective-permute-start.14 = (bf16[2,192,384]{2,1,0:T(8,128)(2,1)}, bf16[2,192,384]{2,1,0:T(8,128)(2,1)}, u32[]{:S(2)}, u32[]{:S(2)}) collective-permute-start(bf16[2,192,384]{2,1,0:T(8,128)(2,1)} %get-tuple-element.57), channel_id=1, source_target_pairs={{0,32},{8,40},{16,48},{24,56},{32,0},{40,8},{48,16},{56,24},{64,96... | collective-permute-start | bytes 884744 | tf_op jit(solution)/shard_map/ppermute | solution.py:523
  98.8 1.7 %collective-permute-done.8.refs_7_ = bf16[1024,384]{1,0:T(8,128)(2,1)S(1)} collective-permute-done((bf16[1024,384]{1,0:T(8,128)(2,1)}, bf16[1024,384]{1,0:T(8,128)(2,1)S(1)}, u32[]{:S(2)}, u32[]{:S(2)}) %collective-permute-start.8) | collective-permute-done | bytes 786464 | tf_op jit(solution)/shard_map/ppermute | solution.py:502
  100.5 7.4 %backward.1.refs_5_ = bf16[8,640,128]{2,1,0:T(8,128)(2,1)} custom-call(s32[5]{0:T(128)S(1)} %copy-done.12, bf16[3,1024,128]{2,1,0:T(8,128)(2,1)S(1)} %copy-done.8, bf16[2,1024,128]{2,1,0:T(8,128)(2,1)S(1)} %get-tuple-element.35.refs_2_, s32[8,128]{1,0:T(8,128)S(1)} %get-tuple-element.37.refs_4_.refs_3_, f32[8,512]{1,0:T(8,128)S(1)} %get-tuple-element.40.refs_4_, ...), custom_call_target="tpu_custom_call" | custom-call | tf_op jit(solution)/shard_map/backward/pallas_call | solution.py:81
  107.9 7.2 %all-to-all-start.1 = ((bf16[8,640,128]{2,1,0:T(8,128)(2,1)}), bf16[8,640,128]{2,1,0:T(8,128)(2,1)S(1)}, u32[]{:S(2)}, u32[]{:S(2)}) async-start(bf16[8,640,128]{2,1,0:T(8,128)(2,1)} %backward.1.refs_5_), calls=%async_computation.2 | async-start | bytes 2621440 | tf_op jit(solution)/shard_map/all_to_all | solution.py:541
  116.3 5.0 %collective-permute-start.16 = (bf16[192,384]{1,0:T(8,128)(2,1)S(1)}, bf16[192,384]{1,0:T(8,128)(2,1)S(1)}, u32[]{:S(2)}, u32[]{:S(2)}) collective-permute-start(bf16[192,384]{1,0:T(8,128)(2,1)S(1)} %get-tuple-element.59), channel_id=1, source_target_pairs={{0,0},{1,1},{2,16},{3,17},{4,32},{5,33},{6,48},{7,49},{8,8},{9,9},... | collective-permute-start | bytes 442376 | tf_op jit(solution)/shard_map/ppermute | solution.py:552
  121.3 4.5 %collective-permute-start.17 = (bf16[192,384]{1,0:T(8,128)(2,1)S(1)}, bf16[192,384]{1,0:T(8,128)(2,1)S(1)}, u32[]{:S(2)}, u32[]{:S(2)}) collective-permute-start(bf16[192,384]{1,0:T(8,128)(2,1)S(1)} %get-tuple-element.60), channel_id=1, source_target_pairs={{0,64},{1,65},{2,80},{3,81},{4,96},{5,97},{6,112},{7,113},{8,72},{... | collective-permute-start | bytes 442376 | tf_op jit(solution)/shard_map/ppermute | solution.py:552
  125.8 17.5 %collective-permute-done.16.refs_1_ = bf16[192,384]{1,0:T(8,128)(2,1)S(1)} collective-permute-done((bf16[192,384]{1,0:T(8,128)(2,1)S(1)}, bf16[192,384]{1,0:T(8,128)(2,1)S(1)}, u32[]{:S(2)}, u32[]{:S(2)}) %collective-permute-start.16) | collective-permute-done | bytes 147488 | tf_op jit(solution)/shard_map/ppermute | solution.py:552
  143.3 1.5 collective-permute-done.17.refs_2_
  146.1 1.7 %unpack.1 = (bf16[128,3072]{1,0:T(8,128)(2,1)}, bf16[128,512]{1,0:T(8,128)(2,1)}, bf16[128,512]{1,0:T(8,128)(2,1)}) custom-call(s32[5]{0:T(128)S(1)} %copy-done.12, bf16[8,640,128]{2,1,0:T(8,128)(2,1)S(1)} %all-to-all-done.1.refs_1_), custom_call_target="tpu_custom_call" | custom-call | tf_op jit(solution)/shard_map/unpack/pallas_call | solution.py:81
  (64 shorter events, 10.1 us)
Async XLA Ops:
  7.2 21.3 %collective-permute-start.2 = (bf16[192,384]{1,0:T(8,128)(2,1)}, bf16[192,384]{1,0:T(8,128)(2,1)S(1)}, u32[]{:S(2)}, u32[]{:S(2)}) collective-permute-start(bf16[192,384]{1,0:T(8,128)(2,1)} %param.10), channel_id=1, source_target_pairs={{0,0},{1,1},{2,16},{3,17},{4,32},{5,33},{6,48},{7,49},{8,8},{9,9},... | collective-permute-start | bytes 442376 | tf_op jit(solution)/shard_map/ppermute | solution.py:394
  13.0 22.5 %collective-permute-start.3 = (bf16[192,384]{1,0:T(8,128)(2,1)}, bf16[192,384]{1,0:T(8,128)(2,1)S(1)}, u32[]{:S(2)}, u32[]{:S(2)}) collective-permute-start(bf16[192,384]{1,0:T(8,128)(2,1)} %param.10), channel_id=1, source_target_pairs={{0,64},{1,65},{2,80},{3,81},{4,96},{5,97},{6,112},{7,113},{8,72},{... | collective-permute-start | bytes 442376 | tf_op jit(solution)/shard_map/ppermute | solution.py:394
  18.6 16.9 %copy-start = (bf16[8,656,128]{2,1,0:T(8,128)(2,1)S(1)}, bf16[8,656,128]{2,1,0:T(8,128)(2,1)}, u32[]{:S(2)}) copy-start(bf16[8,656,128]{2,1,0:T(8,128)(2,1)} %pack.1.refs_4_) | copy-start | bytes 4030468
  18.7 25.6 %all-to-all-start = ((bf16[8,656,128]{2,1,0:T(8,128)(2,1)}), bf16[8,656,128]{2,1,0:T(8,128)(2,1)S(1)}, u32[]{:S(2)}, u32[]{:S(2)}) async-start(bf16[8,656,128]{2,1,0:T(8,128)(2,1)} %pack.1.refs_4_), calls=%async_computation | async-start | bytes 2686976 | tf_op jit(solution)/shard_map/all_to_all | solution.py:405
  26.6 38.2 %all-gather.3.cloned.1.call-start = ((), (), s32[]{:S(2)}) async-start(), calls=%async_computation.4 | async-start | bytes 2654208 | tf_op jit(solution)/shard_map/all_gather | solution.py:419
  26.7 31.8 %copy-start.11 = (s32[5]{0:T(128)}, s32[5]{0:T(128)S(1)}, u32[]{:S(2)}) copy-start(s32[5]{0:T(128)S(1)} %stack.23.refs_0_) | copy-start | bytes 64
  38.3 20.2 %collective-permute-start.4 = (bf16[1024,384]{1,0:T(8,128)(2,1)}, bf16[1024,384]{1,0:T(8,128)(2,1)S(1)}, u32[]{:S(2)}, u32[]{:S(2)}) collective-permute-start(bf16[1024,384]{1,0:T(8,128)(2,1)} %get-tuple-element.42.refs_1_.refs_5_), channel_id=1, source_target_pairs={{0,2},{1,3},{2,4},{3,5},{4,6},{5,7},{6,0},{7,1},{8,10},{9,11},{10,... | collective-permute-start | bytes 2359304 | tf_op jit(solution)/shard_map/ppermute | solution.py:417
  38.4 20.1 %collective-permute-start.5 = (bf16[1024,384]{1,0:T(8,128)(2,1)}, bf16[1024,384]{1,0:T(8,128)(2,1)S(1)}, u32[]{:S(2)}, u32[]{:S(2)}) collective-permute-start(bf16[1024,384]{1,0:T(8,128)(2,1)} %get-tuple-element.42.refs_1_.refs_5_), channel_id=1, source_target_pairs={{0,6},{1,7},{2,0},{3,1},{4,2},{5,3},{6,4},{7,5},{8,14},{9,15},{10,... | collective-permute-start | bytes 2359304 | tf_op jit(solution)/shard_map/ppermute | solution.py:418
  40.4 107.4 %reduce-scatter.2.cloned.1.call-start = ((), (), s32[]{:S(2)}) async-start(), calls=%async_computation.3 | async-start | bytes 3932160 | tf_op jit(solution)/shard_map/reduce_scatter | solution.py:480
  46.7 16.1 %collective-permute-start = (bf16[512,384]{1,0:T(8,128)(2,1)S(1)}, bf16[512,384]{1,0:T(8,128)(2,1)S(1)}, u32[]{:S(2)}, u32[]{:S(2)}) collective-permute-start(bf16[512,384]{1,0:T(8,128)(2,1)S(1)} %get-tuple-element.33.refs_1_), channel_id=1, source_target_pairs={{0,1},{1,0},{2,3},{3,2},{4,5},{5,4},{6,7},{7,6},{8,9},{9,8},{10,11... | collective-permute-start | bytes 1179656 | tf_op jit(solution)/shard_map/ppermute | solution.py:440
  52.4 12.4 %copy-start.9 = (bf16[512,384]{1,0:T(8,128)(2,1)}, bf16[512,384]{1,0:T(8,128)(2,1)S(1)}, u32[]{:S(2)}) copy-start(bf16[512,384]{1,0:T(8,128)(2,1)S(1)} %get-tuple-element.38.refs_2_.refs_3_) | copy-start | bytes 1179652
  52.4 12.2 %collective-permute-start.1 = (bf16[512,384]{1,0:T(8,128)(2,1)S(1)}, bf16[512,384]{1,0:T(8,128)(2,1)}, u32[]{:S(2)}, u32[]{:S(2)}) collective-permute-start(bf16[512,384]{1,0:T(8,128)(2,1)S(1)} %get-tuple-element.38.refs_2_.refs_3_), channel_id=1, source_target_pairs={{0,1},{1,0},{2,3},{3,2},{4,5},{5,4},{6,7},{7,6},{8,9},{9,8},{10,11... | collective-permute-start | bytes 1179656 | tf_op jit(solution)/shard_map/ppermute | solution.py:450
  58.5 13.5 %copy-start.1 = (bf16[1024,384]{1,0:T(8,128)(2,1)}, bf16[1024,384]{1,0:T(8,128)(2,1)S(1)}, u32[]{:S(2)}) copy-start(bf16[1024,384]{1,0:T(8,128)(2,1)S(1)} %collective-permute-done.4.refs_1_.refs_2_.refs_6_) | copy-start | bytes 2359300
  58.5 13.5 %copy-start.3 = (bf16[1024,384]{1,0:T(8,128)(2,1)}, bf16[1024,384]{1,0:T(8,128)(2,1)S(1)}, u32[]{:S(2)}) copy-start(bf16[1024,384]{1,0:T(8,128)(2,1)S(1)} %collective-permute-done.5.refs_2_.refs_3_.refs_7_) | copy-start | bytes 2359300
  60.3 11.7 %collective-permute-start.6 = (bf16[512,384]{1,0:T(8,128)(2,1)}, bf16[512,384]{1,0:T(8,128)(2,1)}, u32[]{:S(2)}, u32[]{:S(2)}) collective-permute-start(bf16[512,384]{1,0:T(8,128)(2,1)} %get-tuple-element.43), channel_id=1, source_target_pairs={{0,2},{1,3},{2,4},{3,5},{4,6},{5,7},{6,0},{7,1},{8,10},{9,11},{10,... | collective-permute-start | bytes 1179656 | tf_op jit(solution)/shard_map/ppermute | solution.py:462
  62.8 11.6 %collective-permute-start.7 = (bf16[512,384]{1,0:T(8,128)(2,1)}, bf16[512,384]{1,0:T(8,128)(2,1)}, u32[]{:S(2)}, u32[]{:S(2)}) collective-permute-start(bf16[512,384]{1,0:T(8,128)(2,1)} %get-tuple-element.44), channel_id=1, source_target_pairs={{0,6},{1,7},{2,0},{3,1},{4,2},{5,3},{6,4},{7,5},{8,14},{9,15},{10,... | collective-permute-start | bytes 1179656 | tf_op jit(solution)/shard_map/ppermute | solution.py:463
  72.0 9.9 %copy-start.2 = (bf16[1024,384]{1,0:T(8,128)(2,1)S(1)}, bf16[1024,384]{1,0:T(8,128)(2,1)}, u32[]{:S(2)}) copy-start(bf16[1024,384]{1,0:T(8,128)(2,1)} %copy-done.1) | copy-start | bytes 2359300
  72.0 9.9 %copy-start.4 = (bf16[1024,384]{1,0:T(8,128)(2,1)S(1)}, bf16[1024,384]{1,0:T(8,128)(2,1)}, u32[]{:S(2)}) copy-start(bf16[1024,384]{1,0:T(8,128)(2,1)} %copy-done.3) | copy-start | bytes 2359300
  72.0 9.9 %copy-start.10 = (bf16[512,384]{1,0:T(8,128)(2,1)S(1)}, bf16[512,384]{1,0:T(8,128)(2,1)}, u32[]{:S(2)}) copy-start(bf16[512,384]{1,0:T(8,128)(2,1)} %copy-done.9) | copy-start | bytes 1179652
  72.0 9.9 %copy-start.12 = (s32[5]{0:T(128)S(1)}, s32[5]{0:T(128)}, u32[]{:S(2)}) copy-start(s32[5]{0:T(128)} %copy-done.11) | copy-start | bytes 64
  72.1 9.9 %copy-start.15 = (bf16[512,384]{1,0:T(8,128)(2,1)S(1)}, bf16[512,384]{1,0:T(8,128)(2,1)}, u32[]{:S(2)}) copy-start(bf16[512,384]{1,0:T(8,128)(2,1)} %copy-done.14) | copy-start | bytes 1179652
  81.1 19.4 %collective-permute-start.8 = (bf16[1024,384]{1,0:T(8,128)(2,1)}, bf16[1024,384]{1,0:T(8,128)(2,1)S(1)}, u32[]{:S(2)}, u32[]{:S(2)}) collective-permute-start(bf16[1024,384]{1,0:T(8,128)(2,1)} %get-tuple-element.46), channel_id=1, source_target_pairs={{0,1},{1,0},{2,3},{3,2},{4,5},{5,4},{6,7},{7,6},{8,9},{9,8},{10,11... | collective-permute-start | bytes 2359304 | tf_op jit(solution)/shard_map/ppermute | solution.py:502
  89.1 1.7 %collective-permute-start.9 = (bf16[4,96,384]{2,1,0:T(8,128)(2,1)S(1)}, bf16[4,96,384]{2,1,0:T(8,128)(2,1)S(1)}, u32[]{:S(2)}, u32[]{:S(2)}) collective-permute-start(bf16[4,96,384]{2,1,0:T(8,128)(2,1)S(1)} %get-tuple-element.48), channel_id=1, source_target_pairs={{0,8},{8,0},{16,24},{24,16},{32,40},{40,32},{48,56},{56,48},{64,72... | collective-permute-start | bytes 884744 | tf_op jit(solution)/shard_map/ppermute | solution.py:514
  89.2 2.0 %collective-permute-start.10 = (bf16[4,96,384]{2,1,0:T(8,128)(2,1)S(1)}, bf16[4,96,384]{2,1,0:T(8,128)(2,1)S(1)}, u32[]{:S(2)}, u32[]{:S(2)}) collective-permute-start(bf16[4,96,384]{2,1,0:T(8,128)(2,1)S(1)} %get-tuple-element.49), channel_id=1, source_target_pairs={{0,8},{8,0},{16,24},{24,16},{32,40},{40,32},{48,56},{56,48},{64,72... | collective-permute-start | bytes 884744 | tf_op jit(solution)/shard_map/ppermute | solution.py:514
  89.7 1.9 %collective-permute-start.11 = (bf16[4,96,384]{2,1,0:T(8,128)(2,1)S(1)}, bf16[4,96,384]{2,1,0:T(8,128)(2,1)S(1)}, u32[]{:S(2)}, u32[]{:S(2)}) collective-permute-start(bf16[4,96,384]{2,1,0:T(8,128)(2,1)S(1)} %get-tuple-element.50), channel_id=1, source_target_pairs={{0,8},{8,0},{16,24},{24,16},{32,40},{40,32},{48,56},{56,48},{64,72... | collective-permute-start | bytes 884744 | tf_op jit(solution)/shard_map/ppermute | solution.py:514
  89.7 2.2 %collective-permute-start.12 = (bf16[4,96,384]{2,1,0:T(8,128)(2,1)S(1)}, bf16[4,96,384]{2,1,0:T(8,128)(2,1)S(1)}, u32[]{:S(2)}, u32[]{:S(2)}) collective-permute-start(bf16[4,96,384]{2,1,0:T(8,128)(2,1)S(1)} %get-tuple-element.51), channel_id=1, source_target_pairs={{0,8},{8,0},{16,24},{24,16},{32,40},{40,32},{48,56},{56,48},{64,72... | collective-permute-start | bytes 884744 | tf_op jit(solution)/shard_map/ppermute | solution.py:514
  93.6 21.5 %collective-permute-start.13 = (bf16[2,192,384]{2,1,0:T(8,128)(2,1)}, bf16[2,192,384]{2,1,0:T(8,128)(2,1)S(1)}, u32[]{:S(2)}, u32[]{:S(2)}) collective-permute-start(bf16[2,192,384]{2,1,0:T(8,128)(2,1)} %get-tuple-element.56), channel_id=1, source_target_pairs={{0,16},{8,24},{16,32},{24,40},{32,48},{40,56},{48,0},{56,8},{64,80... | collective-permute-start | bytes 884744 | tf_op jit(solution)/shard_map/ppermute | solution.py:523
  94.8 20.3 %collective-permute-start.14 = (bf16[2,192,384]{2,1,0:T(8,128)(2,1)}, bf16[2,192,384]{2,1,0:T(8,128)(2,1)}, u32[]{:S(2)}, u32[]{:S(2)}) collective-permute-start(bf16[2,192,384]{2,1,0:T(8,128)(2,1)} %get-tuple-element.57), channel_id=1, source_target_pairs={{0,32},{8,40},{16,48},{24,56},{32,0},{40,8},{48,16},{56,24},{64,96... | collective-permute-start | bytes 884744 | tf_op jit(solution)/shard_map/ppermute | solution.py:523
  98.8 16.3 %collective-permute-start.15 = (bf16[2,192,384]{2,1,0:T(8,128)(2,1)S(1)}, bf16[2,192,384]{2,1,0:T(8,128)(2,1)}, u32[]{:S(2)}, u32[]{:S(2)}) collective-permute-start(bf16[2,192,384]{2,1,0:T(8,128)(2,1)S(1)} %get-tuple-element.58), channel_id=1, source_target_pairs={{0,48},{8,56},{16,0},{24,8},{32,16},{40,24},{48,32},{56,40},{64,11... | collective-permute-start | bytes 884744 | tf_op jit(solution)/shard_map/ppermute | solution.py:523
  107.9 38.2 %all-to-all-start.1 = ((bf16[8,640,128]{2,1,0:T(8,128)(2,1)}), bf16[8,640,128]{2,1,0:T(8,128)(2,1)S(1)}, u32[]{:S(2)}, u32[]{:S(2)}) async-start(bf16[8,640,128]{2,1,0:T(8,128)(2,1)} %backward.1.refs_5_), calls=%async_computation.2 | async-start | bytes 2621440 | tf_op jit(solution)/shard_map/all_to_all | solution.py:541
  116.3 27.1 %collective-permute-start.16 = (bf16[192,384]{1,0:T(8,128)(2,1)S(1)}, bf16[192,384]{1,0:T(8,128)(2,1)S(1)}, u32[]{:S(2)}, u32[]{:S(2)}) collective-permute-start(bf16[192,384]{1,0:T(8,128)(2,1)S(1)} %get-tuple-element.59), channel_id=1, source_target_pairs={{0,0},{1,1},{2,16},{3,17},{4,32},{5,33},{6,48},{7,49},{8,8},{9,9},... | collective-permute-start | bytes 442376 | tf_op jit(solution)/shard_map/ppermute | solution.py:552
  121.3 23.5 %collective-permute-start.17 = (bf16[192,384]{1,0:T(8,128)(2,1)S(1)}, bf16[192,384]{1,0:T(8,128)(2,1)S(1)}, u32[]{:S(2)}, u32[]{:S(2)}) collective-permute-start(bf16[192,384]{1,0:T(8,128)(2,1)S(1)} %get-tuple-element.60), channel_id=1, source_target_pairs={{0,64},{1,65},{2,80},{3,81},{4,96},{5,97},{6,112},{7,113},{8,72},{... | collective-permute-start | bytes 442376 | tf_op jit(solution)/shard_map/ppermute | solution.py:552
  (8 other events, 34.3 us)
Sparse Core Ops, SparseCore 0:
  40.5 24.2 all-gather.2
  72.1 38.4 reduce-scatter.1
